TPU v7x, 512 devices: a whole 4x8x8 slice. The times are simulated.
512 devices in a mesh: seq: 32 (over y, x), rep: 16 (over z, core).
Axes of the slice: x: 4, y: 8, z: 8, core: 2. Of those that a mesh axis runs over, the one named last changes fastest.
Arguments:
- histories: bfloat16 [16, 32, 6, 64, 512], P('rep', 'seq'), may hold values from -6 to 6
- cotangents: bfloat16 [16, 32, 6, 64, 512], P('rep', 'seq'), may hold values from -6 to 6
- lengths: int32 [16, 32, 6], P('rep', 'seq'), may hold values from 0 to 64, as said below
- w_in: bfloat16 [512, 2048], replicated, may hold values from -0.25 to 0.25
- w_out: bfloat16 [512, 512], replicated, may hold values from -0.25 to 0.25
Outputs:
- input_grads: bfloat16 [16, 32, 6, 64, 512], P('rep', 'seq')
- w_in_grad: float32 [512, 2048], P('rep', 'seq')
Inputs may be any that keep to these rules, and one draw needn't show every extreme that they name: `lengths`: in each replica group exactly 64 slots have a positive length, every live length is at least 8, and in each group some rank has all 6 of its slots live.
All inputs are finite; a program needn't handle non-finite values.
Results may differ from a plain program's by a relative error of at most 0.025.
Values may be sent and summed in bfloat16 or wider, within the bound.
No kernel may reach another device: no remote copies, remote signals or barrier semaphores. Data moves between devices by JAX's collectives and lax.ppermute only.
A program may use at most 64 MiB of HBM per device.

v0:
```python
import jax
import jax.numpy as jnp
from jax import lax
from jax.sharding import Mesh
from jax.sharding import PartitionSpec as P

HEADS = 8
CAP = 2
REP = ("rep_0", "rep_1")


def sent_to_all(shard, axis):
    copies = jnp.broadcast_to(shard, (lax.axis_size(axis), *shard.shape))
    return lax.all_to_all(copies, axis, split_axis=0, concat_axis=0, tiled=True)


def laid_out(tiles, dim):
    shape = list(tiles.shape[1:])
    shape[dim] *= tiles.shape[0]
    return jnp.moveaxis(tiles, 0, dim).reshape(shape)


def gather_directly(shard, axis, dim):
    tiles = sent_to_all(shard, axis)
    return laid_out(tiles, dim)


def cut_along(shard, dim, count):
    before, after = (shard.shape[:dim], shard.shape[dim + 1 :])
    return jnp.moveaxis(shard.reshape(*before, count, -1, *after), dim, 0)


def sum_by_chip(shard, chips, core, dim):
    sizes = (lax.axis_size(chips), lax.axis_size(core))
    tiles = cut_along(shard, dim, sizes[0] * sizes[1])
    inside = tiles.shape[1:]
    tiles = tiles.reshape(*sizes, *inside).swapaxes(0, 1).reshape(-1, *inside)
    tiles = lax.psum_scatter(tiles, core, scatter_dimension=0, tiled=True)
    return lax.psum_scatter(tiles, chips, scatter_dimension=0, tiled=True)[0]


def sum_at_owner(shard, axis, dim):
    count = lax.axis_size(axis)
    tiles = lax.all_to_all(cut_along(shard, dim, count), axis, 0, 0, tiled=True)
    return jnp.sum(tiles.astype(jnp.float32), axis=0)


def layer_norm(values):
    average = jnp.mean(values, axis=-1, keepdims=True)
    centered = values - average
    spread = jnp.mean(centered * centered, axis=-1, keepdims=True)
    return centered * lax.rsqrt(spread + 1e-06)


def forward(history, weight_in, weight_out, lengths):
    count_slots, positions, features = history.shape
    head_size = features // HEADS
    normed = layer_norm(history.astype(jnp.float32)).astype(jnp.bfloat16)
    projected = jax.nn.silu(
        jnp.dot(
            normed.reshape(count_slots * positions, features),
            weight_in,
            preferred_element_type=jnp.float32,
        )
    ).astype(jnp.bfloat16)
    projected = projected.reshape(count_slots, positions, 4, HEADS, head_size)
    gate_rows = projected[:, :, 0].reshape(count_slots, positions, features)
    value_rows = projected[:, :, 1]
    query_rows = projected[:, :, 2]
    key_rows = projected[:, :, 3]
    scores = jnp.einsum(
        "cthe,cshe->chts", query_rows, key_rows, preferred_element_type=jnp.float32
    ) * head_size ** (-0.5)
    row_ids = jnp.arange(positions, dtype=jnp.int32)
    allowed = (row_ids[None, :] <= row_ids[:, None])[None, None] & (
        row_ids[None, None, None, :] < lengths[:, None, None, None]
    )
    weights = (
        jnp.where(allowed, jax.nn.silu(scores), 0.0)
        / lengths.astype(jnp.float32)[:, None, None, None]
    ).astype(jnp.bfloat16)
    attended = jnp.einsum(
        "chts,cshe->cthe", weights, value_rows, preferred_element_type=jnp.float32
    ).reshape(count_slots, positions, features)
    gated_out = (layer_norm(attended) * gate_rows.astype(jnp.float32)).astype(jnp.bfloat16)
    mixed_out = jnp.dot(
        gated_out.reshape(count_slots * positions, features),
        weight_out,
        preferred_element_type=jnp.float32,
    )
    return history.astype(jnp.float32) + mixed_out.reshape(count_slots, positions, features)


def cotangent_seed(cotangent, lengths):
    row_ids = jnp.arange(cotangent.shape[1], dtype=jnp.int32)
    valid = row_ids[None, :] < lengths[:, None]
    return jnp.where(valid[:, :, None], cotangent.astype(jnp.float32), 0.0)


def assign(flat_lengths, devices, home_slots):
    slot_total = devices * home_slots
    slot_index = jnp.arange(slot_total, dtype=jnp.int32)
    is_live = flat_lengths > 0
    work_cost = flat_lengths * flat_lengths
    ranking = jnp.where(
        is_live, slot_index - work_cost * slot_total, slot_total * slot_total + slot_index
    )
    ordered = jnp.argsort(ranking)
    leading = ordered[:devices]
    trailing = ordered[devices : 2 * devices][::-1]
    device_ids = jnp.arange(devices, dtype=jnp.int32)
    partner_ids = trailing[(device_ids[None, :] + device_ids[:, None]) % devices]
    clashes = jnp.any(leading[None, :] // home_slots == partner_ids // home_slots, axis=1)
    chosen_shift = jnp.argmin(jnp.where(clashes, devices + device_ids, device_ids))
    usable = jnp.logical_not(jnp.all(clashes))
    partners = trailing[(device_ids + chosen_shift) % devices]
    paired_dest = (
        jnp.zeros(slot_total, jnp.int32).at[leading].set(device_ids).at[partners].set(device_ids)
    )
    paired_slot = jnp.zeros(slot_total, jnp.int32).at[partners].set(1)
    position = jnp.cumsum(is_live.astype(jnp.int32)) - 1
    destination = jnp.where(is_live, jnp.where(usable, paired_dest, position % devices), -1)
    arrival = jnp.where(is_live, jnp.where(usable, paired_slot, position // devices), -1)
    return (destination, arrival)


def shards(histories, cotangents, lengths, w_in, w_out):
    home_slots = histories.shape[2]
    positions = histories.shape[3]
    features = histories.shape[4]
    devices = lax.axis_size("seq")
    device_index = lax.axis_index("seq")
    every_length = gather_directly(lengths, "seq", 1)
    flat_lengths = every_length.reshape(devices * home_slots)
    destination, arrival = assign(flat_lengths, devices, home_slots)
    my_dest = lax.dynamic_slice_in_dim(destination, device_index * home_slots, home_slots)
    device_ids = jnp.arange(devices, dtype=jnp.int32)
    routing = (my_dest[None, :] == device_ids[:, None]).astype(jnp.bfloat16)
    slot_index = jnp.arange(devices * home_slots, dtype=jnp.int32)
    selected = (destination[None, :] == device_index) & (
        arrival[None, :] == jnp.arange(CAP, dtype=jnp.int32)[:, None]
    )
    arriving = jnp.sum(jnp.where(selected, slot_index[None, :], 0), axis=1)
    arriving_length = flat_lengths[arriving]
    chooser = ((arriving // home_slots)[:, None] == device_ids[None, :]).astype(jnp.bfloat16)

    def outgoing(source):
        spread_out = jnp.dot(
            routing,
            source.reshape(home_slots, positions * features),
            preferred_element_type=jnp.bfloat16,
        )
        return spread_out.reshape(devices, positions, features)

    def collect(source):
        gathered = jnp.dot(
            chooser,
            source.reshape(devices, positions * features),
            preferred_element_type=jnp.bfloat16,
        )
        return gathered.reshape(CAP, positions, features)

    received = lax.all_to_all(outgoing(histories), "seq", split_axis=0, concat_axis=0, tiled=True)
    local_hist = collect(received)
    _, pullback = jax.vjp(
        lambda history_in, weight_in: forward(history_in, weight_in, w_out, arriving_length),
        local_hist,
        w_in,
    )
    local_cot = collect(
        lax.all_to_all(outgoing(cotangents), "seq", split_axis=0, concat_axis=0, tiled=True)
    )
    grad_hist, grad_in = pullback(cotangent_seed(local_cot, arriving_length))
    going_back = jnp.dot(
        chooser.T, grad_hist.reshape(CAP, positions * features), preferred_element_type=jnp.bfloat16
    )
    going_back = going_back.reshape(devices, positions, features)
    returned = lax.all_to_all(going_back, "seq", split_axis=0, concat_axis=0, tiled=True)
    home_grad = jnp.dot(
        routing.T,
        returned.reshape(devices, positions * features),
        preferred_element_type=jnp.bfloat16,
    )
    home_grad = home_grad.reshape(histories.shape)
    gradient = grad_in.astype(jnp.float32)
    row_block = sum_by_chip(gradient.astype(jnp.bfloat16), "rep_0", "rep_1", 0).astype(jnp.float32)
    w_in_grad = sum_at_owner(row_block.astype(jnp.bfloat16), "seq", 1)
    return (home_grad, w_in_grad)


def solution(mesh):
    torus = Mesh(mesh.devices.reshape(mesh.shape["seq"], 8, 2), ("seq", "rep_0", "rep_1"))
    placed = (
        P(REP, "seq", None, None, None),
        P(REP, "seq", None, None, None),
        P(REP, "seq", None),
        P(),
        P(),
    )
    return jax.shard_map(
        shards,
        mesh=torus,
        in_specs=placed,
        out_specs=(P(REP, "seq", None, None, None), P(REP, "seq")),
        check_vma=False,
    )
```

profile of v0, /device:TPU:8, one launch (start us, length us, event | category | flops | bytes accessed | tf_op | source)
XLA Modules:
  0.0 294.3 jit_solution(14026624557392354151)
XLA Ops:
  8.6 10.2 %all-to-all-start = ((s32[32,1,1,6]{3,2,1,0:T(1,128)}), s32[32,1,1,6]{3,2,1,0:T(1,128)S(1)}, u32[]{:S(2)}, u32[]{:S(2)}) async-start(s32[32,1,1,6]{3,2,1,0:T(1,128)} %broadcast_in_dim.60), calls=%async_computation | async-start | bytes 32768 | tf_op jit(solution)/shard_map/all_to_all | solution.py:14
  18.9 8.4 %all-to-all-done = s32[32,1,1,6]{3,2,1,0:T(1,128)S(1)} async-done(((s32[32,1,1,6]{3,2,1,0:T(1,128)}), s32[32,1,1,6]{3,2,1,0:T(1,128)S(1)}, u32[]{:S(2)}, u32[]{:S(2)}) %all-to-all-start) | async-done | bytes 800 | tf_op jit(solution)/shard_map/all_to_all | solution.py:14
  28.6 3.2 %sort.17 = (s32[192]{0:T(256)}, s32[192]{0:T(256)S(1)}) sort(s32[192]{0:T(256)S(1)} %get-tuple-element.24, s32[192]{0:T(256)S(1)} %iota.75), dimensions={0}, to_apply=%region_0.1 | sort | flops 1536 | bytes 3072 | tf_op jit(solution)/shard_map/jit(argsort)/sort | solution.py:108
  31.9 6.6 %gather_fusion = s32[1024]{0:T(1024)S(1)} fusion(s32[32]{0:T(128)S(1)} %rev.3, s32[1024]{0:T(1024)S(1)} %broadcast_clamp_fusion), kind=kCustom, calls=%fused_computation | custom fusion | bytes 12288 | tf_op jit(solution)/shard_map/gather | solution.py:112
  45.1 2.5 copy.170
  47.6 5.9 %all-to-all-start.2 = ((bf16[32,64,512]{2,1,0:T(8,128)(2,1)}), bf16[32,64,512]{2,1,0:T(8,128)(2,1)}, u32[]{:S(2)}, u32[]{:S(2)}) async-start(bf16[32,64,512]{2,1,0:T(8,128)(2,1)} %copy.170), calls=%async_computation.2 | async-start | bytes 4194304 | tf_op jit(solution)/shard_map/all_to_all | solution.py:163
  54.3 2.5 copy.166
  56.8 45.3 %all-to-all-done.2 = bf16[32,64,512]{2,1,0:T(8,128)(2,1)} async-done(((bf16[32,64,512]{2,1,0:T(8,128)(2,1)}), bf16[32,64,512]{2,1,0:T(8,128)(2,1)}, u32[]{:S(2)}, u32[]{:S(2)}) %all-to-all-start.2) | async-done | bytes 2097184 | tf_op jit(solution)/shard_map/all_to_all | solution.py:163
  102.1 6.5 %all-to-all-start.1 = ((bf16[32,64,512]{2,1,0:T(8,128)(2,1)}), bf16[32,64,512]{2,1,0:T(8,128)(2,1)}, u32[]{:S(2)}, u32[]{:S(2)}) async-start(bf16[32,64,512]{2,1,0:T(8,128)(2,1)} %copy.166), calls=%async_computation.1 | async-start | bytes 4194304 | tf_op jit(solution)/shard_map/all_to_all | solution.py:171
  110.5 2.9 fusion.93
  114.8 41.6 %all-to-all-done.1 = bf16[32,64,512]{2,1,0:T(8,128)(2,1)} async-done(((bf16[32,64,512]{2,1,0:T(8,128)(2,1)}), bf16[32,64,512]{2,1,0:T(8,128)(2,1)}, u32[]{:S(2)}, u32[]{:S(2)}) %all-to-all-start.1) | async-done | bytes 2097184 | tf_op jit(solution)/shard_map/all_to_all | solution.py:171
  156.4 2.9 fusion.21
  161.4 2.4 multiply_convert_fusion
  163.7 2.1 reshape.396
  165.8 2.1 fusion.91
  167.9 2.0 copy.208
  172.0 1.8 copy.207
  174.9 1.9 copy.182
  178.9 1.9 reshape.397
  180.8 1.9 reshape.405
  189.5 3.8 %copy.190 = f32[2,64,4,8,64]{4,3,2,1,0:T(8,128)} copy(f32[2,64,4,8,64]{1,4,3,0,2:T(8,128)} %add_convert_fusion) | data formatting | bytes 2097152 | tf_op jit(solution)/shard_map/transpose(jvp())/convert_element_type | solution.py:65
  193.3 2.1 reshape.406
  195.4 2.1 convolution_convert_fusion
  199.0 2.1 bitcast_convert_fusion
  204.0 1.9 fusion.41
  205.9 2.5 copy.197
  208.3 6.5 %all-to-all-start.3 = ((bf16[32,64,512]{2,1,0:T(8,128)(2,1)}), bf16[32,64,512]{2,1,0:T(8,128)(2,1)}, u32[]{:S(2)}, u32[]{:S(2)}) async-start(bf16[32,64,512]{2,1,0:T(8,128)(2,1)} %copy.197), calls=%async_computation.3 | async-start | bytes 4194304 | tf_op jit(solution)/shard_map/all_to_all | solution.py:178
  214.9 2.9 reduce-scatter.3.cloned.1.call-done
  217.8 47.3 %reduce-scatter.5.cloned.1.call-done = bf16[1,32,2048]{2,1,0:T(8,128)(2,1)} async-done(((bf16[8,32,2048]{2,1,0:T(8,128)(2,1)}), bf16[1,32,2048]{2,1,0:T(8,128)(2,1)}) %reduce-scatter.5.cloned.1.call-update) | async-done | bytes 131088 | tf_op jit(solution)/shard_map/reduce_scatter | solution.py:39
  267.2 9.8 %all-to-all-start.4 = ((bf16[32,2,1024]{2,1,0:T(2,128)(2,1)}), bf16[32,2,1024]{2,1,0:T(2,128)(2,1)S(1)}, u32[]{:S(2)}, u32[]{:S(2)}) async-start(bf16[32,2,1024]{2,1,0:T(2,128)(2,1)} %reshape.484), calls=%async_computation.6 | async-start | bytes 262144 | tf_op jit(solution)/shard_map/all_to_all | solution.py:44
  277.0 2.8 fusion.9
  280.7 5.9 %all-to-all-done.4 = bf16[32,2,1024]{2,1,0:T(2,128)(2,1)S(1)} async-done(((bf16[32,2,1024]{2,1,0:T(2,128)(2,1)}), bf16[32,2,1024]{2,1,0:T(2,128)(2,1)S(1)}, u32[]{:S(2)}, u32[]{:S(2)}) %all-to-all-start.4) | async-done | bytes 131104 | tf_op jit(solution)/shard_map/all_to_all | solution.py:44
  (125 shorter events, 35.2 us)
Async XLA Ops:
  7.2 154.2 %copy-start = (bf16[512,2048]{1,0:T(8,128)(2,1)S(1)}, bf16[512,2048]{1,0:T(8,128)(2,1)}, u32[]{:S(2)}) copy-start(bf16[512,2048]{1,0:T(8,128)(2,1)} %param.8) | copy-start | bytes 6291460
  8.6 18.7 %all-to-all-start = ((s32[32,1,1,6]{3,2,1,0:T(1,128)}), s32[32,1,1,6]{3,2,1,0:T(1,128)S(1)}, u32[]{:S(2)}, u32[]{:S(2)}) async-start(s32[32,1,1,6]{3,2,1,0:T(1,128)} %broadcast_in_dim.60), calls=%async_computation | async-start | bytes 32768 | tf_op jit(solution)/shard_map/all_to_all | solution.py:14
  31.9 12.3 %copy-start.10 = (bf16[1,1,6,64,512]{4,3,2,1,0:T(8,128)(2,1)S(1)}, bf16[1,1,6,64,512]{4,3,2,1,0:T(8,128)(2,1)}, u32[]{:S(2)}) copy-start(bf16[1,1,6,64,512]{4,3,2,1,0:T(8,128)(2,1)} %param.5) | copy-start | bytes 1179652
  47.6 5.9 %copy-start.11 = (bf16[1,1,6,64,512]{4,3,2,1,0:T(8,128)(2,1)S(1)}, bf16[1,1,6,64,512]{4,3,2,1,0:T(8,128)(2,1)}, u32[]{:S(2)}) copy-start(bf16[1,1,6,64,512]{4,3,2,1,0:T(8,128)(2,1)} %param.6) | copy-start | bytes 1179652
  47.6 54.5 %all-to-all-start.2 = ((bf16[32,64,512]{2,1,0:T(8,128)(2,1)}), bf16[32,64,512]{2,1,0:T(8,128)(2,1)}, u32[]{:S(2)}, u32[]{:S(2)}) async-start(bf16[32,64,512]{2,1,0:T(8,128)(2,1)} %copy.170), calls=%async_computation.2 | async-start | bytes 4194304 | tf_op jit(solution)/shard_map/all_to_all | solution.py:163
  102.1 54.3 %all-to-all-start.1 = ((bf16[32,64,512]{2,1,0:T(8,128)(2,1)}), bf16[32,64,512]{2,1,0:T(8,128)(2,1)}, u32[]{:S(2)}, u32[]{:S(2)}) async-start(bf16[32,64,512]{2,1,0:T(8,128)(2,1)} %copy.166), calls=%async_computation.1 | async-start | bytes 4194304 | tf_op jit(solution)/shard_map/all_to_all | solution.py:171
  108.6 109.2 %reduce-scatter.3.cloned.1.call-start = ((), (), s32[]{:S(2)}) async-start(), calls=%async_computation.7 | async-start | bytes 3145728 | tf_op jit(solution)/shard_map/reduce_scatter | solution.py:38
  114.2 45.8 %copy-start.12 = (bf16[512,512]{1,0:T(8,128)(2,1)S(1)}, bf16[512,512]{1,0:T(8,128)(2,1)}, u32[]{:S(2)}) copy-start(bf16[512,512]{1,0:T(8,128)(2,1)} %param.9) | copy-start | bytes 1572868
  159.3 0.6 copy-start.13
  160.3 0.7 copy-start.1
  167.9 3.1 %copy-start.6 = (bf16[2,64,1,8,64]{4,3,2,1,0:T(8,128)(2,1)}, bf16[2,64,1,8,64]{4,3,2,1,0:T(8,128)(2,1)S(1)}, u32[]{:S(2)}) copy-start(bf16[2,64,1,8,64]{4,3,2,1,0:T(8,128)(2,1)S(1)} %get-tuple-element.29) | copy-start | bytes 393220
  167.9 3.1 %copy-start.8 = (bf16[2,64,1,8,64]{4,3,2,1,0:T(8,128)(2,1)}, bf16[2,64,1,8,64]{4,3,2,1,0:T(8,128)(2,1)S(1)}, u32[]{:S(2)}) copy-start(bf16[2,64,1,8,64]{4,3,2,1,0:T(8,128)(2,1)S(1)} %get-tuple-element.28) | copy-start | bytes 393220
  169.9 1.8 copy-start.4
  171.0 0.7 copy-start.2
  185.5 1.8 copy-start.9
  185.5 2.1 copy-start.7
  185.5 2.4 copy-start.3
  201.1 0.7 copy-start.5
  208.3 58.9 %all-to-all-start.3 = ((bf16[32,64,512]{2,1,0:T(8,128)(2,1)}), bf16[32,64,512]{2,1,0:T(8,128)(2,1)}, u32[]{:S(2)}, u32[]{:S(2)}) async-start(bf16[32,64,512]{2,1,0:T(8,128)(2,1)} %copy.197), calls=%async_computation.3 | async-start | bytes 4194304 | tf_op jit(solution)/shard_map/all_to_all | solution.py:178
  214.9 50.3 %reduce-scatter.5.cloned.1.call-start = ((), (), s32[]{:S(2)}) async-start(), calls=%async_computation.8 | async-start | bytes 1179648 | tf_op jit(solution)/shard_map/reduce_scatter | solution.py:39
  267.2 19.3 %all-to-all-start.4 = ((bf16[32,2,1024]{2,1,0:T(2,128)(2,1)}), bf16[32,2,1024]{2,1,0:T(2,128)(2,1)S(1)}, u32[]{:S(2)}, u32[]{:S(2)}) async-start(bf16[32,2,1024]{2,1,0:T(2,128)(2,1)} %reshape.484), calls=%async_computation.6 | async-start | bytes 262144 | tf_op jit(solution)/shard_map/all_to_all | solution.py:44
Sparse Core Ops, SparseCore 0:
  199.2 18.5 reduce-scatter.2
  220.8 44.2 reduce-scatter.4
where the time goes:
time: 295 us; the launch traced here: 294 us
  waiting for transfers between devices  151 us (51%)
  local copies, waits for them, and re-layouts  50 us (17%)
  starting transfers between devices  38.9 us (13%)
  matrix products  24.1 us (8%)
  between operations  15.2 us (5%)
  other arithmetic  14.8 us (5%)
    reduce_scatter x1, waiting for transfers between devices, sum_by_chip(): return lax.psum_scatter(tiles, chips, scatter_dimension=0, tiled=True)[0]  47.3 us
    all_to_all x1, waiting for transfers between devices, shards(): lax.all_to_all(outgoing(histories), 'seq', split_axis=0, concat_axis=0, t...  45.3 us
    all_to_all x1, waiting for transfers between devices, shards(): lax.all_to_all(outgoing(cotangents), 'seq', split_axis=0, concat_axis=0,...  41.6 us
    all_to_all x1, starting transfers between devices, sent_to_all(): return lax.all_to_all(copies, axis, split_axis=0, concat_axis=0, tiled=True)  10.2 us
    all_to_all x1, starting transfers between devices, sum_at_owner(): tiles = lax.all_to_all(cut_along(shard, dim, count), axis, 0, 0, tiled=True)  9.78 us
    unnamed x33, local copies, waits for them, and re-layouts  8.57 us
    all_to_all x1, waiting for transfers between devices, sent_to_all(): return lax.all_to_all(copies, axis, split_axis=0, concat_axis=0, tiled=True)  8.39 us
    gather x1, local copies, waits for them, and re-layouts, assign(): trailing[(device_ids[None, :] + device_ids[:, None]) % devices]  6.56 us
  transfers between devices with their start and end apart: 7, of which 6 were waited for; matrix products, arithmetic and copies ran while one was open for 8% of the time, Pallas kernels for 0%

commit v1 on v0

--- a/solution.py
+++ b/solution.py
@@ -118,7 +118,7 @@
         jnp.zeros(slot_total, jnp.int32).at[leading].set(device_ids).at[partners].set(device_ids)
     )
     paired_slot = jnp.zeros(slot_total, jnp.int32).at[partners].set(1)
-    position = jnp.cumsum(is_live.astype(jnp.int32)) - 1
+    position = jnp.sum((is_live[None, :] & (slot_index[None, :] < slot_index[:, None])).astype(jnp.int32), axis=1)
     destination = jnp.where(is_live, jnp.where(usable, paired_dest, position % devices), -1)
     arrival = jnp.where(is_live, jnp.where(usable, paired_slot, position // devices), -1)
     return (destination, arrival)

time: 295 us -> 295 us (level)
  no operation moved by 1% of the time
where the time goes in v1:
time: 295 us; the launch traced here: 294 us
  waiting for transfers between devices  151 us (51%)
  local copies, waits for them, and re-layouts  49.8 us (17%)
  starting transfers between devices  39 us (13%)
  matrix products  24.1 us (8%)
  between operations  15.2 us (5%)
  other arithmetic  14.5 us (5%)
    reduce_scatter x1, waiting for transfers between devices, sum_by_chip(): return lax.psum_scatter(tiles, chips, scatter_dimension=0, tiled=True)[0]  47.3 us
    all_to_all x1, waiting for transfers between devices, shards(): lax.all_to_all(outgoing(histories), 'seq', split_axis=0, concat_axis=0, t...  45.3 us
    all_to_all x1, waiting for transfers between devices, shards(): lax.all_to_all(outgoing(cotangents), 'seq', split_axis=0, concat_axis=0,...  41.6 us
    all_to_all x1, starting transfers between devices, sent_to_all(): return lax.all_to_all(copies, axis, split_axis=0, concat_axis=0, tiled=True)  10.2 us
    all_to_all x1, starting transfers between devices, sum_at_owner(): tiles = lax.all_to_all(cut_along(shard, dim, count), axis, 0, 0, tiled=True)  9.84 us
    unnamed x33, local copies, waits for them, and re-layouts  8.57 us
    all_to_all x1, waiting for transfers between devices, sent_to_all(): return lax.all_to_all(copies, axis, split_axis=0, concat_axis=0, tiled=True)  8.39 us
    gather x1, local copies, waits for them, and re-layouts, assign(): trailing[(device_ids[None, :] + device_ids[:, None]) % devices]  6.56 us
  transfers between devices with their start and end apart: 7, of which 6 were waited for; matrix products, arithmetic and copies ran while one was open for 8% of the time, Pallas kernels for 0%

profile of v1, /device:TPU:8, one launch (start us, length us, event | category | flops | bytes accessed | tf_op | source)
XLA Modules:
  0.0 293.8 jit_solution(14641218354241894614)
XLA Ops:
  8.6 10.2 %all-to-all-start = ((s32[32,1,1,6]{3,2,1,0:T(1,128)}), s32[32,1,1,6]{3,2,1,0:T(1,128)S(1)}, u32[]{:S(2)}, u32[]{:S(2)}) async-start(s32[32,1,1,6]{3,2,1,0:T(1,128)} %broadcast_in_dim.62), calls=%async_computation | async-start | bytes 32768 | tf_op jit(solution)/shard_map/all_to_all | solution.py:14
  18.9 8.4 %all-to-all-done = s32[32,1,1,6]{3,2,1,0:T(1,128)S(1)} async-done(((s32[32,1,1,6]{3,2,1,0:T(1,128)}), s32[32,1,1,6]{3,2,1,0:T(1,128)S(1)}, u32[]{:S(2)}, u32[]{:S(2)}) %all-to-all-start) | async-done | bytes 800 | tf_op jit(solution)/shard_map/all_to_all | solution.py:14
  28.6 3.2 %sort.17 = (s32[192]{0:T(256)}, s32[192]{0:T(256)S(1)}) sort(s32[192]{0:T(256)S(1)} %get-tuple-element.24, s32[192]{0:T(256)S(1)} %iota.79), dimensions={0}, to_apply=%region_0.1 | sort | flops 1536 | bytes 3072 | tf_op jit(solution)/shard_map/jit(argsort)/sort | solution.py:108
  31.9 6.6 %gather_fusion = s32[1024]{0:T(1024)S(1)} fusion(s32[32]{0:T(128)S(1)} %rev.3, s32[1024]{0:T(1024)S(1)} %broadcast_clamp_fusion), kind=kCustom, calls=%fused_computation | custom fusion | bytes 12288 | tf_op jit(solution)/shard_map/gather | solution.py:112
  44.6 2.5 copy.170
  47.1 5.9 %all-to-all-start.2 = ((bf16[32,64,512]{2,1,0:T(8,128)(2,1)}), bf16[32,64,512]{2,1,0:T(8,128)(2,1)}, u32[]{:S(2)}, u32[]{:S(2)}) async-start(bf16[32,64,512]{2,1,0:T(8,128)(2,1)} %copy.170), calls=%async_computation.2 | async-start | bytes 4194304 | tf_op jit(solution)/shard_map/all_to_all | solution.py:163
  53.8 2.5 copy.166
  56.3 45.3 %all-to-all-done.2 = bf16[32,64,512]{2,1,0:T(8,128)(2,1)} async-done(((bf16[32,64,512]{2,1,0:T(8,128)(2,1)}), bf16[32,64,512]{2,1,0:T(8,128)(2,1)}, u32[]{:S(2)}, u32[]{:S(2)}) %all-to-all-start.2) | async-done | bytes 2097184 | tf_op jit(solution)/shard_map/all_to_all | solution.py:163
  101.6 6.5 %all-to-all-start.1 = ((bf16[32,64,512]{2,1,0:T(8,128)(2,1)}), bf16[32,64,512]{2,1,0:T(8,128)(2,1)}, u32[]{:S(2)}, u32[]{:S(2)}) async-start(bf16[32,64,512]{2,1,0:T(8,128)(2,1)} %copy.166), calls=%async_computation.1 | async-start | bytes 4194304 | tf_op jit(solution)/shard_map/all_to_all | solution.py:171
  110.0 2.9 fusion.93
  114.3 41.6 %all-to-all-done.1 = bf16[32,64,512]{2,1,0:T(8,128)(2,1)} async-done(((bf16[32,64,512]{2,1,0:T(8,128)(2,1)}), bf16[32,64,512]{2,1,0:T(8,128)(2,1)}, u32[]{:S(2)}, u32[]{:S(2)}) %all-to-all-start.1) | async-done | bytes 2097184 | tf_op jit(solution)/shard_map/all_to_all | solution.py:171
  155.9 2.9 fusion.21
  160.9 2.4 multiply_convert_fusion
  163.2 2.1 reshape.384
  165.3 2.1 fusion.91
  167.4 2.0 copy.208
  171.5 1.8 copy.207
  174.4 1.9 copy.182
  178.4 1.9 reshape.385
  180.3 1.9 reshape.392
  189.0 3.8 %copy.190 = f32[2,64,4,8,64]{4,3,2,1,0:T(8,128)} copy(f32[2,64,4,8,64]{1,4,3,0,2:T(8,128)} %add_convert_fusion) | data formatting | bytes 2097152 | tf_op jit(solution)/shard_map/transpose(jvp())/convert_element_type | solution.py:65
  192.8 2.1 reshape.393
  194.9 2.1 convolution_convert_fusion
  198.5 2.1 bitcast_convert_fusion
  203.5 1.9 fusion.42
  205.4 2.5 copy.197
  207.8 6.5 %all-to-all-start.3 = ((bf16[32,64,512]{2,1,0:T(8,128)(2,1)}), bf16[32,64,512]{2,1,0:T(8,128)(2,1)}, u32[]{:S(2)}, u32[]{:S(2)}) async-start(bf16[32,64,512]{2,1,0:T(8,128)(2,1)} %copy.197), calls=%async_computation.3 | async-start | bytes 4194304 | tf_op jit(solution)/shard_map/all_to_all | solution.py:178
  214.4 2.9 reduce-scatter.3.cloned.1.call-done
  217.3 47.3 %reduce-scatter.5.cloned.1.call-done = bf16[1,32,2048]{2,1,0:T(8,128)(2,1)} async-done(((bf16[8,32,2048]{2,1,0:T(8,128)(2,1)}), bf16[1,32,2048]{2,1,0:T(8,128)(2,1)}) %reduce-scatter.5.cloned.1.call-update) | async-done | bytes 131088 | tf_op jit(solution)/shard_map/reduce_scatter | solution.py:39
  266.7 9.8 %all-to-all-start.4 = ((bf16[32,2,1024]{2,1,0:T(2,128)(2,1)}), bf16[32,2,1024]{2,1,0:T(2,128)(2,1)S(1)}, u32[]{:S(2)}, u32[]{:S(2)}) async-start(bf16[32,2,1024]{2,1,0:T(2,128)(2,1)} %reshape.470), calls=%async_computation.6 | async-start | bytes 262144 | tf_op jit(solution)/shard_map/all_to_all | solution.py:44
  276.5 2.8 fusion.9
  280.2 5.9 %all-to-all-done.4 = bf16[32,2,1024]{2,1,0:T(2,128)(2,1)S(1)} async-done(((bf16[32,2,1024]{2,1,0:T(2,128)(2,1)}), bf16[32,2,1024]{2,1,0:T(2,128)(2,1)S(1)}, u32[]{:S(2)}, u32[]{:S(2)}) %all-to-all-start.4) | async-done | bytes 131104 | tf_op jit(solution)/shard_map/all_to_all | solution.py:44
  (120 shorter events, 34.7 us)
Async XLA Ops:
  7.2 153.7 %copy-start = (bf16[512,2048]{1,0:T(8,128)(2,1)S(1)}, bf16[512,2048]{1,0:T(8,128)(2,1)}, u32[]{:S(2)}) copy-start(bf16[512,2048]{1,0:T(8,128)(2,1)} %param.8) | copy-start | bytes 6291460
  8.6 18.7 %all-to-all-start = ((s32[32,1,1,6]{3,2,1,0:T(1,128)}), s32[32,1,1,6]{3,2,1,0:T(1,128)S(1)}, u32[]{:S(2)}, u32[]{:S(2)}) async-start(s32[32,1,1,6]{3,2,1,0:T(1,128)} %broadcast_in_dim.62), calls=%async_computation | async-start | bytes 32768 | tf_op jit(solution)/shard_map/all_to_all | solution.py:14
  31.9 11.8 %copy-start.10 = (bf16[1,1,6,64,512]{4,3,2,1,0:T(8,128)(2,1)S(1)}, bf16[1,1,6,64,512]{4,3,2,1,0:T(8,128)(2,1)}, u32[]{:S(2)}) copy-start(bf16[1,1,6,64,512]{4,3,2,1,0:T(8,128)(2,1)} %param.5) | copy-start | bytes 1179652
  47.1 5.9 %copy-start.11 = (bf16[1,1,6,64,512]{4,3,2,1,0:T(8,128)(2,1)S(1)}, bf16[1,1,6,64,512]{4,3,2,1,0:T(8,128)(2,1)}, u32[]{:S(2)}) copy-start(bf16[1,1,6,64,512]{4,3,2,1,0:T(8,128)(2,1)} %param.6) | copy-start | bytes 1179652
  47.1 54.5 %all-to-all-start.2 = ((bf16[32,64,512]{2,1,0:T(8,128)(2,1)}), bf16[32,64,512]{2,1,0:T(8,128)(2,1)}, u32[]{:S(2)}, u32[]{:S(2)}) async-start(bf16[32,64,512]{2,1,0:T(8,128)(2,1)} %copy.170), calls=%async_computation.2 | async-start | bytes 4194304 | tf_op jit(solution)/shard_map/all_to_all | solution.py:163
  101.6 54.3 %all-to-all-start.1 = ((bf16[32,64,512]{2,1,0:T(8,128)(2,1)}), bf16[32,64,512]{2,1,0:T(8,128)(2,1)}, u32[]{:S(2)}, u32[]{:S(2)}) async-start(bf16[32,64,512]{2,1,0:T(8,128)(2,1)} %copy.166), calls=%async_computation.1 | async-start | bytes 4194304 | tf_op jit(solution)/shard_map/all_to_all | solution.py:171
  108.1 109.1 %reduce-scatter.3.cloned.1.call-start = ((), (), s32[]{:S(2)}) async-start(), calls=%async_computation.7 | async-start | bytes 3145728 | tf_op jit(solution)/shard_map/reduce_scatter | solution.py:38
  113.7 45.8 %copy-start.12 = (bf16[512,512]{1,0:T(8,128)(2,1)S(1)}, bf16[512,512]{1,0:T(8,128)(2,1)}, u32[]{:S(2)}) copy-start(bf16[512,512]{1,0:T(8,128)(2,1)} %param.9) | copy-start | bytes 1572868
  158.8 0.6 copy-start.13
  159.8 0.7 copy-start.1
  167.3 3.1 %copy-start.6 = (bf16[2,64,1,8,64]{4,3,2,1,0:T(8,128)(2,1)}, bf16[2,64,1,8,64]{4,3,2,1,0:T(8,128)(2,1)S(1)}, u32[]{:S(2)}) copy-start(bf16[2,64,1,8,64]{4,3,2,1,0:T(8,128)(2,1)S(1)} %get-tuple-element.29) | copy-start | bytes 393220
  167.4 3.1 %copy-start.8 = (bf16[2,64,1,8,64]{4,3,2,1,0:T(8,128)(2,1)}, bf16[2,64,1,8,64]{4,3,2,1,0:T(8,128)(2,1)S(1)}, u32[]{:S(2)}) copy-start(bf16[2,64,1,8,64]{4,3,2,1,0:T(8,128)(2,1)S(1)} %get-tuple-element.28) | copy-start | bytes 393220
  169.4 1.9 copy-start.4
  170.5 0.7 copy-start.2
  185.0 1.8 copy-start.9
  185.0 2.1 copy-start.7
  185.0 2.4 copy-start.3
  200.6 0.7 copy-start.5
  207.8 58.8 %all-to-all-start.3 = ((bf16[32,64,512]{2,1,0:T(8,128)(2,1)}), bf16[32,64,512]{2,1,0:T(8,128)(2,1)}, u32[]{:S(2)}, u32[]{:S(2)}) async-start(bf16[32,64,512]{2,1,0:T(8,128)(2,1)} %copy.197), calls=%async_computation.3 | async-start | bytes 4194304 | tf_op jit(solution)/shard_map/all_to_all | solution.py:178
  214.4 50.2 %reduce-scatter.5.cloned.1.call-start = ((), (), s32[]{:S(2)}) async-start(), calls=%async_computation.8 | async-start | bytes 1179648 | tf_op jit(solution)/shard_map/reduce_scatter | solution.py:39
  266.7 19.4 %all-to-all-start.4 = ((bf16[32,2,1024]{2,1,0:T(2,128)(2,1)}), bf16[32,2,1024]{2,1,0:T(2,128)(2,1)S(1)}, u32[]{:S(2)}, u32[]{:S(2)}) async-start(bf16[32,2,1024]{2,1,0:T(2,128)(2,1)} %reshape.470), calls=%async_computation.6 | async-start | bytes 262144 | tf_op jit(solution)/shard_map/all_to_all | solution.py:44
Sparse Core Ops, SparseCore 0:
  198.7 18.5 reduce-scatter.2
  220.3 44.1 reduce-scatter.4

commit v2 on v1

v2 whole, which is shorter than its diff:
```python
import jax
import jax.numpy as jnp
from jax import lax
from jax.experimental import pallas as pl
from jax.experimental.pallas import tpu as pltpu
from jax.sharding import Mesh
from jax.sharding import PartitionSpec as P

HEADS = 8
EPS = 1e-06
AXES = ("yh", "yl", "x", "zh", "zl", "core")
F32 = jnp.float32
BF16 = jnp.bfloat16


def dot(a, b, contract=((1,), (0,))):
    return lax.dot_general(a, b, (contract, ((), ())), preferred_element_type=F32)


def sigmoid(values):
    return 0.5 * jnp.tanh(0.5 * values) + 0.5


def normalised(values):
    average = jnp.mean(values, axis=-1, keepdims=True)
    centered = values - average
    spread = jnp.mean(centered * centered, axis=-1, keepdims=True)
    scale = lax.rsqrt(spread + EPS)
    return centered * scale, scale


def norm_backward(grad, normed, scale):
    first = jnp.mean(grad, axis=-1, keepdims=True)
    second = jnp.mean(grad * normed, axis=-1, keepdims=True)
    return scale * (grad - first - normed * second)


def weight_kernel(
    length_ref,
    hist_ref,
    cot_ref,
    win_ref,
    wout_ref,
    tiles_ref,
    dpre_ref,
    normed_ref,
    turned_ref,
    seed_ref,
    proj_ref,
    slope_ref,
    mixed_ref,
    dgated_ref,
):
    slots, positions, features = hist_ref.shape
    pairs = features // 128
    rows = slots * positions
    half = positions

    def prepare(i, carry):
        at = pl.ds(pl.multiple_of(i * positions, positions), positions)
        normed, _ = normalised(hist_ref[i].astype(F32))
        normed_ref[at, :] = normed.astype(BF16)
        row = lax.broadcasted_iota(jnp.int32, (positions, features), 0)
        cot = cot_ref[i].astype(F32)
        seed_ref[at, :] = jnp.where(row < length_ref[i], cot, 0.0).astype(BF16)
        return carry

    lax.fori_loop(0, slots, prepare, 0)
    turned_ref[...] = normed_ref[...].T

    width = 256
    for j in range(4 * features // width):
        columns = slice(j * width, (j + 1) * width)
        pre = dot(normed_ref[...], win_ref[:, columns])
        gate = sigmoid(pre)
        value = pre * gate
        proj_ref[:, columns] = value.astype(BF16)
        slope_ref[:, columns] = gate + value * (1.0 - gate)
    dgated_ref[...] = dot(seed_ref[...], wout_ref[...], ((1,), (1,))).astype(BF16)

    lane = lax.broadcasted_iota(jnp.int32, (positions, 128), 1)
    time = lax.broadcasted_iota(jnp.int32, (positions, 128), 0)
    first = lane < half
    source = jnp.where(first, lane, lane - half)
    causal = source <= time

    def spread(block):
        zero = jnp.zeros_like(block)
        return jnp.concatenate([jnp.where(first, block, zero), jnp.where(first, zero, block)], 0)

    def attend(i, carry):
        at = pl.ds(pl.multiple_of(i * positions, positions), positions)
        length = length_ref[i]
        inverse = 1.0 / jnp.maximum(length, 1).astype(F32)
        allowed = causal & (source < length)
        weights, slopes = [], []
        for p in range(pairs):
            v_at = slice(features + p * 128, features + (p + 1) * 128)
            q_at = slice(2 * features + p * 128, 2 * features + (p + 1) * 128)
            k_at = slice(3 * features + p * 128, 3 * features + (p + 1) * 128)
            scores = dot(proj_ref[at, q_at], spread(proj_ref[at, k_at]), ((1,), (1,))) * 0.125
            gate = sigmoid(scores)
            value = scores * gate
            weights.append(jnp.where(allowed, value * inverse, 0.0).astype(BF16))
            slopes.append(
                jnp.where(allowed, (gate + value * (1.0 - gate)) * (inverse * 0.125), 0.0)
            )
            mixed_ref[:, p * 128 : (p + 1) * 128] = dot(weights[p], spread(proj_ref[at, v_at]))
        normed, scale = normalised(mixed_ref[...])
        dgated = dgated_ref[at, :].astype(F32)
        dgate = dgated * normed
        dpre_ref[at, :features] = (dgate * slope_ref[at, :features]).astype(BF16)
        dmixed = norm_backward(dgated * proj_ref[at, :features].astype(F32), normed, scale)
        dmixed = dmixed.astype(BF16)
        for p in range(pairs):
            v_at = slice(features + p * 128, features + (p + 1) * 128)
            q_at = slice(2 * features + p * 128, 2 * features + (p + 1) * 128)
            k_at = slice(3 * features + p * 128, 3 * features + (p + 1) * 128)
            down = dmixed[:, p * 128 : (p + 1) * 128]
            dweights = dot(down, spread(proj_ref[at, v_at]), ((1,), (1,)))
            dscores = (dweights * slopes[p]).astype(BF16)
            dv = dot(weights[p], down, ((0,), (0,)))
            dv = jnp.where(first, dv[:half], dv[half:])
            dq = dot(dscores, spread(proj_ref[at, k_at]))
            dk = dot(dscores, proj_ref[at, q_at], ((0,), (0,)))
            dk = jnp.where(first, dk[:half], dk[half:])
            dpre_ref[at, v_at] = (dv * slope_ref[at, v_at]).astype(BF16)
            dpre_ref[at, q_at] = (dq * slope_ref[at, q_at]).astype(BF16)
            dpre_ref[at, k_at] = (dk * slope_ref[at, k_at]).astype(BF16)
        return carry

    lax.fori_loop(0, slots, attend, 0)

    left = lax.broadcasted_iota(jnp.int32, (16, 128), 1) < 64
    for y in range(8):
        block = dot(turned_ref[...], dpre_ref[:, y * 256 : (y + 1) * 256])
        for pair in range(2):
            part = block[:, pair * 128 : (pair + 1) * 128]
            swapped = pltpu.roll(part, 64, 1)
            for r in range(16):
                upper = slice(r * 32, r * 32 + 16)
                lower = slice(r * 32 + 16, r * 32 + 32)
                z, core = r // 2, r % 2
                even = jnp.where(left, part[upper], swapped[lower])
                odd = jnp.where(left, swapped[upper], part[lower])
                for x, tile in ((2 * pair, even), (2 * pair + 1, odd)):
                    q = x * 4 + (y % 2) * 2 + z % 2
                    place = q * 16 + (y // 2) * 4 + z // 2
                    tiles_ref[core, place] = tile.astype(BF16)


def history_kernel(length_ref, hist_ref, cot_ref, win_ref, dpre_ref, out_ref):
    slots, positions, features = hist_ref.shape

    def finish(i, carry):
        at = pl.ds(pl.multiple_of(i * positions, positions), positions)
        grad = dot(dpre_ref[at, :], win_ref[...], ((1,), (1,)))
        normed, scale = normalised(hist_ref[i].astype(F32))
        row = lax.broadcasted_iota(jnp.int32, (positions, features), 0)
        seed = jnp.where(row < length_ref[i], cot_ref[i].astype(F32), 0.0)
        out_ref[i] = (seed + norm_backward(grad, normed, scale)).astype(BF16)
        return carry

    lax.fori_loop(0, slots, finish, 0)


VMEM = pl.BlockSpec(memory_space=pltpu.VMEM)
SMEM = pl.BlockSpec(memory_space=pltpu.SMEM)


def weight_tiles(lengths, hist, cot, w_in, w_out):
    slots, positions, features = hist.shape
    rows = slots * positions
    return pl.pallas_call(
        weight_kernel,
        out_shape=(
            jax.ShapeDtypeStruct((2, 256, 16, 128), BF16),
            jax.ShapeDtypeStruct((rows, 4 * features), BF16),
        ),
        in_specs=[SMEM, VMEM, VMEM, VMEM, VMEM],
        out_specs=(VMEM, VMEM),
        scratch_shapes=[
            pltpu.VMEM((rows, features), BF16),
            pltpu.VMEM((features, rows), BF16),
            pltpu.VMEM((rows, features), BF16),
            pltpu.VMEM((rows, 4 * features), BF16),
            pltpu.VMEM((rows, 4 * features), F32),
            pltpu.VMEM((positions, features), F32),
            pltpu.VMEM((rows, features), BF16),
        ],
        compiler_params=pltpu.CompilerParams(vmem_limit_bytes=40 * 2**20),
        cost_estimate=pl.CostEstimate(
            flops=2 * rows * features * features * 9, bytes_accessed=8 * 2**20, transcendentals=10**6
        ),
    )(lengths, hist, cot, w_in, w_out)


def history_grads(lengths, hist, cot, w_in, dpre):
    return pl.pallas_call(
        history_kernel,
        out_shape=jax.ShapeDtypeStruct(hist.shape, BF16),
        in_specs=[SMEM, VMEM, VMEM, VMEM, VMEM],
        out_specs=VMEM,
        compiler_params=pltpu.CompilerParams(vmem_limit_bytes=24 * 2**20),
        cost_estimate=pl.CostEstimate(
            flops=2 * dpre.shape[0] * dpre.shape[1] * hist.shape[-1],
            bytes_accessed=6 * 2**20,
            transcendentals=1000,
        ),
    )(lengths, hist, cot, w_in, dpre)


STEPS = (("x", "yl", "zl"), ("yh", "zh"))


def summed(parts):
    return jnp.sum(parts.astype(F32), axis=0)


def reduced(tiles):
    tiles = lax.all_to_all(tiles, "core", 0, 0, tiled=True)
    for axes in STEPS:
        tiles = summed(tiles).astype(BF16)
        tiles = tiles.reshape(16, -1, *tiles.shape[1:])
        tiles = lax.all_to_all(tiles, axes, 0, 0, tiled=True)
    return summed(tiles)[0]


def shards(histories, cotangents, lengths, w_in, w_out):
    hist, cot, slot_lengths = histories[0, 0], cotangents[0, 0], lengths[0, 0]
    tiles, dpre = weight_tiles(slot_lengths, hist, cot, w_in, w_out)
    grads = history_grads(slot_lengths, hist, cot, w_in, dpre)
    tile = reduced(tiles)
    block = jnp.concatenate([tile[:, :64], tile[:, 64:]], axis=0)
    return (grads[None, None], block)


def solution(mesh):
    torus = Mesh(mesh.devices.reshape(4, 2, 4, 4, 2, 2), AXES)
    seq, rep = ("yh", "yl", "x"), ("zh", "zl", "core")
    placed = (
        P(rep, seq, None, None, None),
        P(rep, seq, None, None, None),
        P(rep, seq, None),
        P(),
        P(),
    )
    return jax.shard_map(
        shards,
        mesh=torus,
        in_specs=placed,
        out_specs=(P(rep, seq, None, None, None), P(rep, seq)),
        check_vma=False,
    )
```

time: 295 us -> 81.8 us (0.28)
  waiting for transfers between devices: 151 us -> 4.56 us
  local copies, waits for them, and re-layouts: 49.8 us -> 7.91 us
  blocking collectives: 0 us -> 31.1 us
  starting transfers between devices: 39 us -> 11.2 us
  matrix products: 24.1 us -> 0 us
  Pallas kernels: 0 us -> 21.5 us
  between operations: 15.2 us -> 0.72 us
  other arithmetic: 14.5 us -> 4.28 us
    all_to_all x5 -> x1, waiting for transfers between devices: 101 us -> 4.56 us  [reduced(): tiles = lax.all_to_all(tiles, axes, 0, 0, tiled=True)]
    reduce_scatter x2 -> x0, waiting for transfers between devices: 50.1 us -> none  [the longest x1 47.3 us: sum_by_chip(): return lax.psum_scatter(tiles, chips, scatter_dimension=0, tiled=True)[0]]
    all_to_all x0 -> x2, blocking collectives: none -> 31.1 us  [the longest x1 25.7 us: reduced(): tiles = lax.all_to_all(tiles, axes, 0, 0, tiled=True)]
    all_to_all x5 -> x1, starting transfers between devices: 38.9 us -> 11.2 us  [reduced(): tiles = lax.all_to_all(tiles, axes, 0, 0, tiled=True)]
    dot_general x16 -> x0, matrix products: 24.1 us -> none  [the longest x3 6.53 us: forward(): jnp.dot(normed.reshape(count_slots * positions, features), weight_in, pre...]
    pallas_call x0 -> x2, Pallas kernels: none -> 21.5 us  [the longest x1 15.1 us: weight_tiles(): pl.pallas_call(weight_kernel, out_shape=(jax.ShapeDtypeStruct((2, 256, 16...]
    convert_element_type x7 -> x0, local copies, waits for them, and re-layouts: 10.7 us -> none  [the longest x2 5.85 us: forward(): projected = jax.nn.silu(jnp.dot(normed.reshape(count_slots * positions, f...]
    gather x3 -> x0, local copies, waits for them, and re-layouts: 7.9 us -> none  [the longest x1 6.56 us: assign(): trailing[(device_ids[None, :] + device_ids[:, None]) % devices]]
  transfers between devices with their start and end apart: 7 -> 1, of which waited for: 6 -> 1; matrix products, arithmetic and copies ran while one was open for 8% -> 0% of each run, Pallas kernels for 0% -> 8%
where the time goes in v2:
time: 81.8 us; the launch traced here: 81.3 us
  blocking collectives  31.1 us (38%)
  Pallas kernels  21.5 us (26%)
  starting transfers between devices  11.2 us (14%)
  local copies, waits for them, and re-layouts  7.91 us (10%)
  waiting for transfers between devices  4.56 us (6%)
  other arithmetic  4.28 us (5%)
    all_to_all x1, blocking collectives, reduced(): tiles = lax.all_to_all(tiles, axes, 0, 0, tiled=True)  25.7 us
    pallas_call x1, Pallas kernels, weight_tiles(): pl.pallas_call(weight_kernel, out_shape=(jax.ShapeDtypeStruct((2, 256, 16...  15.1 us
    all_to_all x1, starting transfers between devices, reduced(): tiles = lax.all_to_all(tiles, axes, 0, 0, tiled=True)  11.2 us
    unnamed x22, local copies, waits for them, and re-layouts  7.83 us
    pallas_call x1, Pallas kernels, history_grads(): pl.pallas_call(history_kernel, out_shape=jax.ShapeDtypeStruct(hist.shape,...  6.42 us
    all_to_all x1, blocking collectives, reduced(): tiles = lax.all_to_all(tiles, 'core', 0, 0, tiled=True)  5.41 us
    all_to_all x1, waiting for transfers between devices, reduced(): tiles = lax.all_to_all(tiles, axes, 0, 0, tiled=True)  4.56 us
    reduce_sum x3, other arithmetic, summed(): return jnp.sum(parts.astype(F32), axis=0)  3.67 us
  transfers between devices with their start and end apart: 1, of which 1 were waited for; matrix products, arithmetic and copies ran while one was open for 0% of the time, Pallas kernels for 8%

profile of v2, /device:TPU:8, one launch (start us, length us, event | category | flops | bytes accessed | tf_op | source)
XLA Modules:
  0.0 81.3 jit_solution(12969951098603483670)
XLA Ops:
  0.6 0.0 copy-start
  0.6 1.6 %copy-done = bf16[512,2048]{1,0:T(8,128)(2,1)S(1)} copy-done((bf16[512,2048]{1,0:T(8,128)(2,1)S(1)}, bf16[512,2048]{1,0:T(8,128)(2,1)}, u32[]{:S(2)}) %copy-start) | copy-done | bytes 2097176
  2.2 0.0 copy-start.4
  2.2 1.0 %copy-done.4 = bf16[1,1,6,64,512]{4,3,2,1,0:T(8,128)(2,1)S(1)} copy-done((bf16[1,1,6,64,512]{4,3,2,1,0:T(8,128)(2,1)S(1)}, bf16[1,1,6,64,512]{4,3,2,1,0:T(8,128)(2,1)}, u32[]{:S(2)}) %copy-start.4) | copy-done | bytes 393240
  3.2 0.0 copy-start.6
  3.2 1.0 %copy-done.6 = bf16[1,1,6,64,512]{4,3,2,1,0:T(8,128)(2,1)S(1)} copy-done((bf16[1,1,6,64,512]{4,3,2,1,0:T(8,128)(2,1)S(1)}, bf16[1,1,6,64,512]{4,3,2,1,0:T(8,128)(2,1)}, u32[]{:S(2)}) %copy-start.6) | copy-done | bytes 393240
  4.2 0.0 copy-start.8
  4.2 0.7 copy-done.8
  4.9 0.0 copy-start.10
  4.9 1.0 %copy-done.10 = bf16[512,512]{1,0:T(8,128)(2,1)S(1)} copy-done((bf16[512,512]{1,0:T(8,128)(2,1)S(1)}, bf16[512,512]{1,0:T(8,128)(2,1)}, u32[]{:S(2)}) %copy-start.10) | copy-done | bytes 524312
  5.9 15.1 %shard_map.68 = (bf16[2,256,16,128]{3,2,1,0:T(8,128)(2,1)S(1)}, bf16[384,2048]{1,0:T(8,128)(2,1)S(1)}) custom-call(s32[6]{0:T(128)S(1)} %bitcast.12, bf16[6,64,512]{2,1,0:T(8,128)(2,1)S(1)} %bitcast.8, bf16[6,64,512]{2,1,0:T(8,128)(2,1)S(1)} %bitcast.10, bf16[512,2048]{1,0:T(8,128)(2,1)S(1)} %copy-done, bf16[512,512]{1,0:T(8,128)(2,1)S(1)} %copy-done.10), custom_call_target="tpu_custom_call" | custom-call | flops 1811939328 | bytes 8388608 | tf_op jit(solution)/shard_map/pallas_call | solution.py:174
  21.0 0.0 copy-start.2
  21.0 1.1 %copy-done.2 = bf16[384,2048]{1,0:T(8,128)(2,1)} copy-done((bf16[384,2048]{1,0:T(8,128)(2,1)}, bf16[384,2048]{1,0:T(8,128)(2,1)S(1)}, u32[]{:S(2)}) %copy-start.2) | copy-done | bytes 1572888
  22.2 5.4 %all_to_all.15 = bf16[2,256,16,128]{3,2,1,0:T(8,128)(2,1)S(1)} all-to-all(bf16[2,256,16,128]{3,2,1,0:T(8,128)(2,1)S(1)} %get-tuple-element.5), channel_id=1, replica_groups=mesh['yh'=4,'yl'=2,'x'=4,'zh'=4,'zl'=2,'core'=2] {'core'}, dimensions={0} | all-to-all | bytes 4194304 | tf_op jit(solution)/shard_map/all_to_all | solution.py:221
  27.6 1.6 %reduce_sum.33 = bf16[256,16,128]{2,1,0:T(8,128)(2,1)} reduce(bf16[2,256,16,128]{3,2,1,0:T(8,128)(2,1)S(1)} %all_to_all.15, bf16[]{:T(256)} %constant.3.clone.1), dimensions={0}, to_apply=%region_0.0 | reduce | flops 524288 | bytes 3145730 | tf_op jit(solution)/shard_map/reduce_sum | solution.py:217
  29.2 0.0 copy-start.1
  29.2 0.0 copy-start.5
  29.2 0.0 copy-start.7
  29.2 0.0 copy-start.9
  29.2 25.7 %all_to_all.16 = bf16[16,16,16,128]{3,2,1,0:T(8,128)(2,1)} all-to-all(bf16[16,16,16,128]{3,2,1,0:T(8,128)(2,1)} %bitcast.14), channel_id=1, replica_groups=mesh['yh'=4,'yl'=2,'x'=4,'zh'=4,'zl'=2,'core'=2] {'x','yl','zl'}, dimensions={0} | all-to-all | bytes 2097152 | tf_op jit(solution)/shard_map/all_to_all | solution.py:225
  55.0 2.0 %reduce_sum.34 = bf16[16,16,128]{2,1,0:T(8,128)(2,1)} reduce(bf16[16,16,16,128]{3,2,1,0:T(8,128)(2,1)} %all_to_all.16, bf16[]{:T(256)} %constant.3.clone.1), dimensions={0}, to_apply=%region_1.0 | reduce | flops 491520 | bytes 1114114 | tf_op jit(solution)/shard_map/reduce_sum | solution.py:217
  57.0 11.2 %all-to-all-start.2 = ((bf16[16,1,16,128]{3,2,1,0:T(8,128)(2,1)}), bf16[16,1,16,128]{3,2,1,0:T(8,128)(2,1)S(1)}, u32[]{:S(2)}, u32[]{:S(2)}) async-start(bf16[16,1,16,128]{3,2,1,0:T(8,128)(2,1)} %bitcast.6), calls=%async_computation.2 | async-start | bytes 131072 | tf_op jit(solution)/shard_map/all_to_all | solution.py:225
  68.2 0.0 copy-done.1
  68.2 0.0 copy-done.5
  68.2 0.0 copy-done.7
  68.2 0.0 copy-done.9
  68.2 0.0 copy-start.3
  68.2 1.4 %copy-done.3 = bf16[384,2048]{1,0:T(8,128)(2,1)S(1)} copy-done((bf16[384,2048]{1,0:T(8,128)(2,1)S(1)}, bf16[384,2048]{1,0:T(8,128)(2,1)}, u32[]{:S(2)}) %copy-start.3) | copy-done | bytes 1572888
  69.6 6.4 %shard_map.69 = bf16[6,64,512]{2,1,0:T(8,128)(2,1)} custom-call(s32[6]{0:T(128)S(1)} %bitcast.13, bf16[6,64,512]{2,1,0:T(8,128)(2,1)S(1)} %bitcast.9, bf16[6,64,512]{2,1,0:T(8,128)(2,1)S(1)} %bitcast.11, bf16[512,2048]{1,0:T(8,128)(2,1)S(1)} %copy-done.1, bf16[384,2048]{1,0:T(8,128)(2,1)S(1)} %copy-done.3), custom_call_target="tpu_custom_call" | custom-call | flops 805306368 | bytes 6291456 | tf_op jit(solution)/shard_map/pallas_call | solution.py:199
  76.0 4.6 %all-to-all-done.2 = bf16[16,1,16,128]{3,2,1,0:T(8,128)(2,1)S(1)} async-done(((bf16[16,1,16,128]{3,2,1,0:T(8,128)(2,1)}), bf16[16,1,16,128]{3,2,1,0:T(8,128)(2,1)S(1)}, u32[]{:S(2)}, u32[]{:S(2)}) %all-to-all-start.2) | async-done | bytes 65568 | tf_op jit(solution)/shard_map/all_to_all | solution.py:225
  80.6 0.1 fusion
  80.7 0.6 pad_maximum_fusion
  (1 shorter events, 0.0 us)
Async XLA Ops:
  0.6 1.6 %copy-start = (bf16[512,2048]{1,0:T(8,128)(2,1)S(1)}, bf16[512,2048]{1,0:T(8,128)(2,1)}, u32[]{:S(2)}) copy-start(bf16[512,2048]{1,0:T(8,128)(2,1)} %win_ref.3) | copy-start | bytes 6291460
  2.2 1.0 %copy-start.4 = (bf16[1,1,6,64,512]{4,3,2,1,0:T(8,128)(2,1)S(1)}, bf16[1,1,6,64,512]{4,3,2,1,0:T(8,128)(2,1)}, u32[]{:S(2)}) copy-start(bf16[1,1,6,64,512]{4,3,2,1,0:T(8,128)(2,1)} %param.5) | copy-start | bytes 1179652
  3.2 1.0 %copy-start.6 = (bf16[1,1,6,64,512]{4,3,2,1,0:T(8,128)(2,1)S(1)}, bf16[1,1,6,64,512]{4,3,2,1,0:T(8,128)(2,1)}, u32[]{:S(2)}) copy-start(bf16[1,1,6,64,512]{4,3,2,1,0:T(8,128)(2,1)} %param.6) | copy-start | bytes 1179652
  4.2 0.7 copy-start.8
  4.9 1.0 %copy-start.10 = (bf16[512,512]{1,0:T(8,128)(2,1)S(1)}, bf16[512,512]{1,0:T(8,128)(2,1)}, u32[]{:S(2)}) copy-start(bf16[512,512]{1,0:T(8,128)(2,1)} %wout_ref.1) | copy-start | bytes 1572868
  21.0 1.2 %copy-start.2 = (bf16[384,2048]{1,0:T(8,128)(2,1)}, bf16[384,2048]{1,0:T(8,128)(2,1)S(1)}, u32[]{:S(2)}) copy-start(bf16[384,2048]{1,0:T(8,128)(2,1)S(1)} %get-tuple-element.4.dpre_ref) | copy-start | bytes 4718596
  29.2 38.9 %copy-start.1 = (bf16[512,2048]{1,0:T(8,128)(2,1)S(1)}, bf16[512,2048]{1,0:T(8,128)(2,1)}, u32[]{:S(2)}) copy-start(bf16[512,2048]{1,0:T(8,128)(2,1)} %win_ref.3) | copy-start | bytes 6291460
  29.2 38.9 %copy-start.5 = (bf16[1,1,6,64,512]{4,3,2,1,0:T(8,128)(2,1)S(1)}, bf16[1,1,6,64,512]{4,3,2,1,0:T(8,128)(2,1)}, u32[]{:S(2)}) copy-start(bf16[1,1,6,64,512]{4,3,2,1,0:T(8,128)(2,1)} %param.5) | copy-start | bytes 1179652
  29.2 38.9 %copy-start.7 = (bf16[1,1,6,64,512]{4,3,2,1,0:T(8,128)(2,1)S(1)}, bf16[1,1,6,64,512]{4,3,2,1,0:T(8,128)(2,1)}, u32[]{:S(2)}) copy-start(bf16[1,1,6,64,512]{4,3,2,1,0:T(8,128)(2,1)} %param.6) | copy-start | bytes 1179652
  29.2 39.0 %copy-start.9 = (s32[1,1,6]{2,1,0:T(1,128)S(1)}, s32[1,1,6]{2,1,0:T(1,128)}, u32[]{:S(2)}) copy-start(s32[1,1,6]{2,1,0:T(1,128)} %param.7) | copy-start | bytes 76
  57.0 23.6 %all-to-all-start.2 = ((bf16[16,1,16,128]{3,2,1,0:T(8,128)(2,1)}), bf16[16,1,16,128]{3,2,1,0:T(8,128)(2,1)S(1)}, u32[]{:S(2)}, u32[]{:S(2)}) async-start(bf16[16,1,16,128]{3,2,1,0:T(8,128)(2,1)} %bitcast.6), calls=%async_computation.2 | async-start | bytes 131072 | tf_op jit(solution)/shard_map/all_to_all | solution.py:225
  68.2 1.4 %copy-start.3 = (bf16[384,2048]{1,0:T(8,128)(2,1)S(1)}, bf16[384,2048]{1,0:T(8,128)(2,1)}, u32[]{:S(2)}) copy-start(bf16[384,2048]{1,0:T(8,128)(2,1)} %copy-done.2) | copy-start | bytes 4718596

commit v3 on v2

--- a/solution.py
+++ b/solution.py
@@ -37,12 +37,19 @@
 
 def weight_kernel(
     length_ref,
+    hist_hbm,
+    cot_hbm,
+    win_hbm,
+    wout_hbm,
+    tiles_hbm,
+    dpre_hbm,
+    done_ref,
+    tiles_ref,
+    dpre_ref,
     hist_ref,
     cot_ref,
     win_ref,
     wout_ref,
-    tiles_ref,
-    dpre_ref,
     normed_ref,
     turned_ref,
     seed_ref,
@@ -50,19 +57,33 @@
     slope_ref,
     mixed_ref,
     dgated_ref,
+    arrived,
+    sent,
 ):
     slots, positions, features = hist_ref.shape
     pairs = features // 128
-    rows = slots * positions
     half = positions
+
+    def columns_of(ref, j):
+        return ref.at[:, j * features : (j + 1) * features]
+
+    hist_copy = pltpu.make_async_copy(hist_hbm, hist_ref, arrived.at[0])
+    win_copies = [
+        pltpu.make_async_copy(columns_of(win_hbm, j), columns_of(win_ref, j), arrived.at[1 + j])
+        for j in range(4)
+    ]
+    cot_copy = pltpu.make_async_copy(cot_hbm, cot_ref, arrived.at[5])
+    wout_copy = pltpu.make_async_copy(wout_hbm, wout_ref, arrived.at[6])
+    for copy in (hist_copy, *win_copies, cot_copy, wout_copy):
+        copy.start()
+
+    done_ref[...] = jnp.zeros_like(done_ref)
+    hist_copy.wait()
 
     def prepare(i, carry):
         at = pl.ds(pl.multiple_of(i * positions, positions), positions)
         normed, _ = normalised(hist_ref[i].astype(F32))
         normed_ref[at, :] = normed.astype(BF16)
-        row = lax.broadcasted_iota(jnp.int32, (positions, features), 0)
-        cot = cot_ref[i].astype(F32)
-        seed_ref[at, :] = jnp.where(row < length_ref[i], cot, 0.0).astype(BF16)
         return carry
 
     lax.fori_loop(0, slots, prepare, 0)
@@ -70,12 +91,25 @@
 
     width = 256
     for j in range(4 * features // width):
+        if (j * width) % features == 0:
+            win_copies[j * width // features].wait()
         columns = slice(j * width, (j + 1) * width)
         pre = dot(normed_ref[...], win_ref[:, columns])
         gate = sigmoid(pre)
         value = pre * gate
         proj_ref[:, columns] = value.astype(BF16)
         slope_ref[:, columns] = gate + value * (1.0 - gate)
+    cot_copy.wait()
+
+    def mask(i, carry):
+        at = pl.ds(pl.multiple_of(i * positions, positions), positions)
+        row = lax.broadcasted_iota(jnp.int32, (positions, features), 0)
+        cot = cot_ref[i].astype(F32)
+        seed_ref[at, :] = jnp.where(row < length_ref[i], cot, 0.0).astype(BF16)
+        return carry
+
+    lax.fori_loop(0, slots, mask, 0)
+    wout_copy.wait()
     dgated_ref[...] = dot(seed_ref[...], wout_ref[...], ((1,), (1,))).astype(BF16)
 
     lane = lax.broadcasted_iota(jnp.int32, (positions, 128), 1)
@@ -131,6 +165,9 @@
 
     lax.fori_loop(0, slots, attend, 0)
 
+    dpre_copy = pltpu.make_async_copy(dpre_ref, dpre_hbm, sent.at[8])
+    dpre_copy.start()
+    tile_copies = []
     left = lax.broadcasted_iota(jnp.int32, (16, 128), 1) < 64
     for y in range(8):
         block = dot(turned_ref[...], dpre_ref[:, y * 256 : (y + 1) * 256])
@@ -144,28 +181,64 @@
                 even = jnp.where(left, part[upper], swapped[lower])
                 odd = jnp.where(left, swapped[upper], part[lower])
                 for x, tile in ((2 * pair, even), (2 * pair + 1, odd)):
-                    q = x * 4 + (y % 2) * 2 + z % 2
-                    place = q * 16 + (y // 2) * 4 + z // 2
-                    tiles_ref[core, place] = tile.astype(BF16)
-
-
-def history_kernel(length_ref, hist_ref, cot_ref, win_ref, dpre_ref, out_ref):
+                    place = (x, y % 2, z % 2, y // 2, z // 2)
+                    tiles_ref[(core, *place)] = tile.astype(BF16)
+        part = (slice(None), slice(None), y % 2, slice(None), y // 2)
+        tile_copies.append(
+            pltpu.make_async_copy(tiles_ref.at[part], tiles_hbm.at[part], sent.at[y])
+        )
+        tile_copies[y].start()
+    for copy in (dpre_copy, *tile_copies):
+        copy.wait()
+
+
+def history_kernel(
+    length_ref, hist_ref, cot_ref, win_ref, dpre_ref, after_ref, out_ref, done_ref, grad_ref
+):
     slots, positions, features = hist_ref.shape
+    grad_ref[...] = dot(dpre_ref[...], win_ref[...], ((1,), (1,)))
 
     def finish(i, carry):
         at = pl.ds(pl.multiple_of(i * positions, positions), positions)
-        grad = dot(dpre_ref[at, :], win_ref[...], ((1,), (1,)))
         normed, scale = normalised(hist_ref[i].astype(F32))
         row = lax.broadcasted_iota(jnp.int32, (positions, features), 0)
         seed = jnp.where(row < length_ref[i], cot_ref[i].astype(F32), 0.0)
-        out_ref[i] = (seed + norm_backward(grad, normed, scale)).astype(BF16)
+        out_ref[i] = (seed + norm_backward(grad_ref[at, :], normed, scale)).astype(BF16)
         return carry
 
     lax.fori_loop(0, slots, finish, 0)
+    done_ref[...] = jnp.zeros_like(done_ref)
+
+
+def sum_kernel(parts_ref, after_ref, out_ref, done_ref):
+    parts, count = parts_ref.shape[:2]
+    step = min(count, 8)
+
+    def add(i, carry):
+        at = pl.ds(i * step, step)
+        total = parts_ref[0, at].astype(F32)
+        for p in range(1, parts):
+            total += parts_ref[p, at].astype(F32)
+        out_ref[at] = total.astype(BF16)
+        return carry
+
+    lax.fori_loop(0, count // step, add, 0)
+    done_ref[...] = jnp.zeros_like(done_ref)
+
+
+def last_kernel(parts_ref, out_ref):
+    total = parts_ref[0, 0].astype(F32)
+    for p in range(1, parts_ref.shape[0]):
+        total += parts_ref[p, 0].astype(F32)
+    out_ref[:16, :] = total[:, :64]
+    out_ref[16:, :] = total[:, 64:]
 
 
 VMEM = pl.BlockSpec(memory_space=pltpu.VMEM)
 SMEM = pl.BlockSpec(memory_space=pltpu.SMEM)
+HBM = pl.BlockSpec(memory_space=pltpu.HBM)
+TILES = (2, 4, 2, 2, 4, 4, 16, 128)
+DONE = jax.ShapeDtypeStruct((8, 128), F32)
 
 
 def weight_tiles(lengths, hist, cot, w_in, w_out):
@@ -174,12 +247,19 @@
     return pl.pallas_call(
         weight_kernel,
         out_shape=(
-            jax.ShapeDtypeStruct((2, 256, 16, 128), BF16),
+            jax.ShapeDtypeStruct(TILES, BF16),
             jax.ShapeDtypeStruct((rows, 4 * features), BF16),
+            DONE,
         ),
-        in_specs=[SMEM, VMEM, VMEM, VMEM, VMEM],
-        out_specs=(VMEM, VMEM),
+        in_specs=[SMEM, HBM, HBM, HBM, HBM],
+        out_specs=(HBM, HBM, VMEM),
         scratch_shapes=[
+            pltpu.VMEM(TILES, BF16),
+            pltpu.VMEM((rows, 4 * features), BF16),
+            pltpu.VMEM(hist.shape, BF16),
+            pltpu.VMEM(hist.shape, BF16),
+            pltpu.VMEM(w_in.shape, BF16),
+            pltpu.VMEM(w_out.shape, BF16),
             pltpu.VMEM((rows, features), BF16),
             pltpu.VMEM((features, rows), BF16),
             pltpu.VMEM((rows, features), BF16),
@@ -187,51 +267,65 @@
             pltpu.VMEM((rows, 4 * features), F32),
             pltpu.VMEM((positions, features), F32),
             pltpu.VMEM((rows, features), BF16),
+            pltpu.SemaphoreType.DMA((7,)),
+            pltpu.SemaphoreType.DMA((9,)),
         ],
-        compiler_params=pltpu.CompilerParams(vmem_limit_bytes=40 * 2**20),
+        compiler_params=pltpu.CompilerParams(vmem_limit_bytes=56 * 2**20),
         cost_estimate=pl.CostEstimate(
             flops=2 * rows * features * features * 9, bytes_accessed=8 * 2**20, transcendentals=10**6
         ),
     )(lengths, hist, cot, w_in, w_out)
 
 
-def history_grads(lengths, hist, cot, w_in, dpre):
+def history_grads(lengths, hist, cot, w_in, dpre, after):
+    rows = dpre.shape[0]
     return pl.pallas_call(
         history_kernel,
-        out_shape=jax.ShapeDtypeStruct(hist.shape, BF16),
-        in_specs=[SMEM, VMEM, VMEM, VMEM, VMEM],
-        out_specs=VMEM,
-        compiler_params=pltpu.CompilerParams(vmem_limit_bytes=24 * 2**20),
+        out_shape=(jax.ShapeDtypeStruct(hist.shape, BF16), DONE),
+        in_specs=[SMEM, VMEM, VMEM, VMEM, VMEM, VMEM],
+        out_specs=(VMEM, VMEM),
+        scratch_shapes=[pltpu.VMEM((rows, hist.shape[-1]), F32)],
+        compiler_params=pltpu.CompilerParams(vmem_limit_bytes=16 * 2**20),
         cost_estimate=pl.CostEstimate(
-            flops=2 * dpre.shape[0] * dpre.shape[1] * hist.shape[-1],
+            flops=2 * rows * dpre.shape[1] * hist.shape[-1],
             bytes_accessed=6 * 2**20,
             transcendentals=1000,
         ),
-    )(lengths, hist, cot, w_in, dpre)
-
-
-STEPS = (("x", "yl", "zl"), ("yh", "zh"))
-
-
-def summed(parts):
-    return jnp.sum(parts.astype(F32), axis=0)
-
-
-def reduced(tiles):
-    tiles = lax.all_to_all(tiles, "core", 0, 0, tiled=True)
-    for axes in STEPS:
-        tiles = summed(tiles).astype(BF16)
-        tiles = tiles.reshape(16, -1, *tiles.shape[1:])
-        tiles = lax.all_to_all(tiles, axes, 0, 0, tiled=True)
-    return summed(tiles)[0]
+    )(lengths, hist, cot, w_in, dpre, after)
+
+
+def summed(parts, after):
+    return pl.pallas_call(
+        sum_kernel,
+        out_shape=(jax.ShapeDtypeStruct(parts.shape[1:], BF16), DONE),
+        in_specs=[VMEM, VMEM],
+        out_specs=(VMEM, VMEM),
+        compiler_params=pltpu.CompilerParams(vmem_limit_bytes=8 * 2**20),
+    )(parts, after)
+
+
+def last_sum(parts):
+    return pl.pallas_call(
+        last_kernel,
+        out_shape=jax.ShapeDtypeStruct((32, 64), F32),
+        in_specs=[VMEM],
+        out_specs=VMEM,
+        compiler_params=pltpu.CompilerParams(vmem_limit_bytes=2 * 2**20),
+    )(parts)
+
+
+def exchanged(tiles, axes):
+    return lax.all_to_all(tiles, axes, 0, 0, tiled=True)
 
 
 def shards(histories, cotangents, lengths, w_in, w_out):
     hist, cot, slot_lengths = histories[0, 0], cotangents[0, 0], lengths[0, 0]
-    tiles, dpre = weight_tiles(slot_lengths, hist, cot, w_in, w_out)
-    grads = history_grads(slot_lengths, hist, cot, w_in, dpre)
-    tile = reduced(tiles)
-    block = jnp.concatenate([tile[:, :64], tile[:, 64:]], axis=0)
+    tiles, dpre, done = weight_tiles(slot_lengths, hist, cot, w_in, w_out)
+    tiles, done = summed(exchanged(tiles.reshape(2, 256, 16, 128), "core"), done)
+    near = exchanged(tiles.reshape(16, 16, 16, 128), ("x", "yl", "zl"))
+    grads, done = history_grads(slot_lengths, hist, cot, w_in, dpre, done)
+    tiles, done = summed(near, done)
+    block = last_sum(exchanged(tiles.reshape(16, 1, 16, 128), ("yh", "zh")))
     return (grads[None, None], block)
 
 

time: 81.8 us -> 80.5 us (0.984)
  Pallas kernels: 21.5 us -> 27.1 us
  local copies, waits for them, and re-layouts: 7.91 us -> 3.38 us
  other arithmetic: 4.28 us -> 0 us
  waiting for transfers between devices: 4.56 us -> 8.78 us
  starting transfers between devices: 11.2 us -> 9.27 us
    pallas_call x2 -> x5, Pallas kernels: 21.5 us -> 27.1 us  [the longest x1 21.4 us: weight_tiles(): pl.pallas_call(weight_kernel, out_shape=(jax.ShapeDtypeStruct(TILES, BF16...]
    unnamed x22 -> x14, local copies, waits for them, and re-layouts: 7.83 us -> 3.38 us
    all_to_all x1, waiting for transfers between devices: 4.56 us -> 8.78 us  [exchanged(): return lax.all_to_all(tiles, axes, 0, 0, tiled=True)]
    reduce_sum x3 -> x0, other arithmetic: 3.67 us -> none  [summed(): return jnp.sum(parts.astype(F32), axis=0)]
    all_to_all x1, starting transfers between devices: 11.2 us -> 9.27 us  [exchanged(): return lax.all_to_all(tiles, axes, 0, 0, tiled=True)]
  transfers between devices with their start and end apart: 1 -> 1, of which waited for: 1 -> 1; matrix products, arithmetic and copies ran while one was open for 0% -> 0% of each run, Pallas kernels for 8% -> 5%
where the time goes in v3:
time: 80.5 us; the launch traced here: 80.1 us
  blocking collectives  30.8 us (38%)
  Pallas kernels  27.1 us (34%)
  starting transfers between devices  9.27 us (12%)
  waiting for transfers between devices  8.78 us (11%)
  local copies, waits for them, and re-layouts  3.38 us (4%)
    all_to_all x2, blocking collectives, exchanged(): return lax.all_to_all(tiles, axes, 0, 0, tiled=True)  30.8 us
    pallas_call x1, Pallas kernels, weight_tiles(): pl.pallas_call(weight_kernel, out_shape=(jax.ShapeDtypeStruct(TILES, BF16...  21.4 us
    all_to_all x1, starting transfers between devices, exchanged(): return lax.all_to_all(tiles, axes, 0, 0, tiled=True)  9.27 us
    all_to_all x1, waiting for transfers between devices, exchanged(): return lax.all_to_all(tiles, axes, 0, 0, tiled=True)  8.78 us
    pallas_call x1, Pallas kernels, history_grads(): pl.pallas_call(history_kernel, out_shape=(jax.ShapeDtypeStruct(hist.shape...  3.94 us
    unnamed x14, local copies, waits for them, and re-layouts  3.38 us
  transfers between devices with their start and end apart: 1, of which 1 were waited for; matrix products, arithmetic and copies ran while one was open for 0% of the time, Pallas kernels for 5%

profile of v3, /device:TPU:8, one launch (start us, length us, event | category | flops | bytes accessed | tf_op | source)
XLA Modules:
  0.0 80.1 jit_solution(17358077729899036599)
XLA Ops:
  0.6 21.4 %shard_map.68 = (bf16[2,4,2,2,4,4,16,128]{7,6,5,4,3,2,1,0:T(8,128)(2,1)}, bf16[384,2048]{1,0:T(8,128)(2,1)}, f32[8,128]{1,0:T(8,128)}) custom-call(s32[6]{0:T(128)} %bitcast.13, bf16[6,64,512]{2,1,0:T(8,128)(2,1)} %bitcast.8, bf16[6,64,512]{2,1,0:T(8,128)(2,1)} %bitcast.10, bf16[512,2048]{1,0:T(8,128)(2,1)} %win_ref.1, bf16[512,512]{1,0:T(8,128)(2,1)} %wout_hbm.1), custom_call_target="tpu_custom_call" | custom-call | flops 1811939328 | bytes 8388608 | tf_op jit(solution)/shard_map/pallas_call | solution.py:247
  22.0 0.0 copy-start.5
  22.1 6.6 %all_to_all.15.parts_ref = bf16[2,256,16,128]{3,2,1,0:T(8,128)(2,1)S(1)} all-to-all(bf16[2,256,16,128]{3,2,1,0:T(8,128)(2,1)} %bitcast.15), channel_id=1, replica_groups=mesh['yh'=4,'yl'=2,'x'=4,'zh'=4,'zl'=2,'core'=2] {'core'}, dimensions={0} | all-to-all | bytes 4194304 | tf_op jit(solution)/shard_map/all_to_all | solution.py:318
  28.7 0.0 copy-done.5
  28.7 0.0 copy-start
  28.7 0.0 copy-start.3
  28.7 0.0 copy-start.6
  28.7 0.4 shard_map.69
  29.1 0.0 copy-start.2
  29.1 1.0 %copy-done.2 = bf16[256,16,128]{2,1,0:T(8,128)(2,1)} copy-done((bf16[256,16,128]{2,1,0:T(8,128)(2,1)}, bf16[256,16,128]{2,1,0:T(8,128)(2,1)S(1)}, u32[]{:S(2)}) %copy-start.2) | copy-done | bytes 1048600
  30.1 9.3 %all-to-all-start.1 = ((bf16[16,16,16,128]{3,2,1,0:T(8,128)(2,1)}), bf16[16,16,16,128]{3,2,1,0:T(8,128)(2,1)S(1)}, u32[]{:S(2)}, u32[]{:S(2)}) async-start(bf16[16,16,16,128]{3,2,1,0:T(8,128)(2,1)} %bitcast.7), calls=%async_computation.1 | async-start | bytes 2097152 | tf_op jit(solution)/shard_map/all_to_all | solution.py:318
  39.3 0.0 copy-done
  39.3 0.0 copy-done.3
  39.3 0.0 copy-done.6
  39.3 0.0 copy-start.1
  39.4 1.4 %copy-done.1 = bf16[384,2048]{1,0:T(8,128)(2,1)S(1)} copy-done((bf16[384,2048]{1,0:T(8,128)(2,1)S(1)}, bf16[384,2048]{1,0:T(8,128)(2,1)}, u32[]{:S(2)}) %copy-start.1) | copy-done | bytes 1572888
  40.8 0.0 copy-start.4
  40.8 1.0 %copy-done.4 = bf16[1,1,6,64,512]{4,3,2,1,0:T(8,128)(2,1)S(1)} copy-done((bf16[1,1,6,64,512]{4,3,2,1,0:T(8,128)(2,1)S(1)}, bf16[1,1,6,64,512]{4,3,2,1,0:T(8,128)(2,1)}, u32[]{:S(2)}) %copy-start.4) | copy-done | bytes 393240
  41.8 3.9 %shard_map.70 = (bf16[6,64,512]{2,1,0:T(8,128)(2,1)}, f32[8,128]{1,0:T(8,128)S(1)}) custom-call(s32[6]{0:T(128)S(1)} %bitcast.14, bf16[6,64,512]{2,1,0:T(8,128)(2,1)S(1)} %bitcast.9, bf16[6,64,512]{2,1,0:T(8,128)(2,1)S(1)} %bitcast.11, bf16[512,2048]{1,0:T(8,128)(2,1)S(1)} %copy-done, bf16[384,2048]{1,0:T(8,128)(2,1)S(1)} %copy-done.1, ...), custom_call_target="tpu_custom_call" | custom-call | flops 805306368 | bytes 6291456 | tf_op jit(solution)/shard_map/pallas_call | solution.py:282
  45.7 8.8 %all-to-all-done.1.parts_ref = bf16[16,16,16,128]{3,2,1,0:T(8,128)(2,1)S(1)} async-done(((bf16[16,16,16,128]{3,2,1,0:T(8,128)(2,1)}), bf16[16,16,16,128]{3,2,1,0:T(8,128)(2,1)S(1)}, u32[]{:S(2)}, u32[]{:S(2)}) %all-to-all-start.1) | async-done | bytes 1048608 | tf_op jit(solution)/shard_map/all_to_all | solution.py:318
  54.5 0.7 shard_map.71
  55.2 24.2 %all_to_all.16.parts_ref = bf16[16,1,16,128]{3,2,1,0:T(8,128)(2,1)S(1)} all-to-all(bf16[16,1,16,128]{3,2,1,0:T(8,128)(2,1)S(1)} %bitcast.12), channel_id=1, replica_groups=mesh['yh'=4,'yl'=2,'x'=4,'zh'=4,'zl'=2,'core'=2] {'yh','zh'}, dimensions={0} | all-to-all | bytes 131072 | tf_op jit(solution)/shard_map/all_to_all | solution.py:318
  79.4 0.7 shard_map.72
Async XLA Ops:
  22.0 6.6 %copy-start.5 = (f32[8,128]{1,0:T(8,128)S(1)}, f32[8,128]{1,0:T(8,128)}, u32[]{:S(2)}) copy-start(f32[8,128]{1,0:T(8,128)} %get-tuple-element.12.after_ref) | copy-start | bytes 12292
  28.7 10.6 %copy-start = (bf16[512,2048]{1,0:T(8,128)(2,1)S(1)}, bf16[512,2048]{1,0:T(8,128)(2,1)}, u32[]{:S(2)}) copy-start(bf16[512,2048]{1,0:T(8,128)(2,1)} %win_ref.1) | copy-start | bytes 6291460
  28.7 10.6 %copy-start.3 = (bf16[1,1,6,64,512]{4,3,2,1,0:T(8,128)(2,1)S(1)}, bf16[1,1,6,64,512]{4,3,2,1,0:T(8,128)(2,1)}, u32[]{:S(2)}) copy-start(bf16[1,1,6,64,512]{4,3,2,1,0:T(8,128)(2,1)} %param.5) | copy-start | bytes 1179652
  28.7 10.7 %copy-start.6 = (s32[1,1,6]{2,1,0:T(1,128)S(1)}, s32[1,1,6]{2,1,0:T(1,128)}, u32[]{:S(2)}) copy-start(s32[1,1,6]{2,1,0:T(1,128)} %param.7) | copy-start | bytes 76
  29.1 1.0 %copy-start.2 = (bf16[256,16,128]{2,1,0:T(8,128)(2,1)}, bf16[256,16,128]{2,1,0:T(8,128)(2,1)S(1)}, u32[]{:S(2)}) copy-start(bf16[256,16,128]{2,1,0:T(8,128)(2,1)S(1)} %get-tuple-element.15) | copy-start | bytes 3145732
  30.1 24.4 %all-to-all-start.1 = ((bf16[16,16,16,128]{3,2,1,0:T(8,128)(2,1)}), bf16[16,16,16,128]{3,2,1,0:T(8,128)(2,1)S(1)}, u32[]{:S(2)}, u32[]{:S(2)}) async-start(bf16[16,16,16,128]{3,2,1,0:T(8,128)(2,1)} %bitcast.7), calls=%async_computation.1 | async-start | bytes 2097152 | tf_op jit(solution)/shard_map/all_to_all | solution.py:318
  39.3 1.4 %copy-start.1 = (bf16[384,2048]{1,0:T(8,128)(2,1)S(1)}, bf16[384,2048]{1,0:T(8,128)(2,1)}, u32[]{:S(2)}) copy-start(bf16[384,2048]{1,0:T(8,128)(2,1)} %get-tuple-element.10.dpre_ref) | copy-start | bytes 4718596
  40.8 1.0 %copy-start.4 = (bf16[1,1,6,64,512]{4,3,2,1,0:T(8,128)(2,1)S(1)}, bf16[1,1,6,64,512]{4,3,2,1,0:T(8,128)(2,1)}, u32[]{:S(2)}) copy-start(bf16[1,1,6,64,512]{4,3,2,1,0:T(8,128)(2,1)} %param.6) | copy-start | bytes 1179652

commit v4 on v3

--- a/solution.py
+++ b/solution.py
@@ -8,6 +8,7 @@
 
 HEADS = 8
 EPS = 1e-06
+UNROLL = 6
 AXES = ("yh", "yl", "x", "zh", "zl", "core")
 F32 = jnp.float32
 BF16 = jnp.bfloat16
@@ -41,9 +42,9 @@
     cot_hbm,
     win_hbm,
     wout_hbm,
-    tiles_hbm,
+    keep_hbm,
+    send_hbm,
     dpre_hbm,
-    done_ref,
     tiles_ref,
     dpre_ref,
     hist_ref,
@@ -57,6 +58,10 @@
     slope_ref,
     mixed_ref,
     dgated_ref,
+    scores_ref,
+    weights_ref,
+    dmixed_ref,
+    dscores_ref,
     arrived,
     sent,
 ):
@@ -77,7 +82,6 @@
     for copy in (hist_copy, *win_copies, cot_copy, wout_copy):
         copy.start()
 
-    done_ref[...] = jnp.zeros_like(done_ref)
     hist_copy.wait()
 
     def prepare(i, carry):
@@ -86,7 +90,7 @@
         normed_ref[at, :] = normed.astype(BF16)
         return carry
 
-    lax.fori_loop(0, slots, prepare, 0)
+    lax.fori_loop(0, slots, prepare, 0, unroll=UNROLL)
     turned_ref[...] = normed_ref[...].T
 
     width = 256
@@ -108,66 +112,86 @@
         seed_ref[at, :] = jnp.where(row < length_ref[i], cot, 0.0).astype(BF16)
         return carry
 
-    lax.fori_loop(0, slots, mask, 0)
+    lax.fori_loop(0, slots, mask, 0, unroll=UNROLL)
     wout_copy.wait()
     dgated_ref[...] = dot(seed_ref[...], wout_ref[...], ((1,), (1,))).astype(BF16)
 
     lane = lax.broadcasted_iota(jnp.int32, (positions, 128), 1)
-    time = lax.broadcasted_iota(jnp.int32, (positions, 128), 0)
     first = lane < half
-    source = jnp.where(first, lane, lane - half)
-    causal = source <= time
+    early = jnp.where(first, 1.0, 0.0).astype(BF16)
+    late = jnp.where(first, 0.0, 1.0).astype(BF16)
 
     def spread(block):
-        zero = jnp.zeros_like(block)
-        return jnp.concatenate([jnp.where(first, block, zero), jnp.where(first, zero, block)], 0)
-
-    def attend(i, carry):
-        at = pl.ds(pl.multiple_of(i * positions, positions), positions)
+        return jnp.concatenate([block * early, block * late], 0)
+
+    def blocks(p):
+        return [slice(b * features + p * 128, b * features + (p + 1) * 128) for b in range(4)]
+
+    def for_slots(body):
+        def step(i, carry):
+            body(i, pl.ds(pl.multiple_of(i * positions, positions), positions))
+            return carry
+
+        lax.fori_loop(0, slots, step, 0, unroll=UNROLL)
+
+    def score(i, at):
+        for p in range(pairs):
+            _, _, q_at, k_at = blocks(p)
+            scores_ref[at, blocks(p)[0]] = dot(
+                proj_ref[at, q_at], spread(proj_ref[at, k_at]), ((1,), (1,))
+            )
+
+    def weigh(i, at):
         length = length_ref[i]
         inverse = 1.0 / jnp.maximum(length, 1).astype(F32)
-        allowed = causal & (source < length)
-        weights, slopes = [], []
+        source = lax.broadcasted_iota(jnp.int32, (positions, features), 1) % half
+        time = lax.broadcasted_iota(jnp.int32, (positions, features), 0)
+        allowed = (source <= time) & (source < length)
+        scores = scores_ref[at, :] * 0.125
+        gate = sigmoid(scores)
+        value = scores * gate
+        weights_ref[at, :] = jnp.where(allowed, value * inverse, 0.0).astype(BF16)
+        slopes = (gate + value * (1.0 - gate)) * (inverse * 0.125)
+        scores_ref[at, :] = jnp.where(allowed, slopes, 0.0)
+
+    def mix(i, at):
         for p in range(pairs):
-            v_at = slice(features + p * 128, features + (p + 1) * 128)
-            q_at = slice(2 * features + p * 128, 2 * features + (p + 1) * 128)
-            k_at = slice(3 * features + p * 128, 3 * features + (p + 1) * 128)
-            scores = dot(proj_ref[at, q_at], spread(proj_ref[at, k_at]), ((1,), (1,))) * 0.125
-            gate = sigmoid(scores)
-            value = scores * gate
-            weights.append(jnp.where(allowed, value * inverse, 0.0).astype(BF16))
-            slopes.append(
-                jnp.where(allowed, (gate + value * (1.0 - gate)) * (inverse * 0.125), 0.0)
-            )
-            mixed_ref[:, p * 128 : (p + 1) * 128] = dot(weights[p], spread(proj_ref[at, v_at]))
-        normed, scale = normalised(mixed_ref[...])
+            here, v_at, _, _ = blocks(p)
+            mixed_ref[at, here] = dot(weights_ref[at, here], spread(proj_ref[at, v_at]))
+
+    def turn(i, at):
+        normed, scale = normalised(mixed_ref[at, :])
         dgated = dgated_ref[at, :].astype(F32)
-        dgate = dgated * normed
-        dpre_ref[at, :features] = (dgate * slope_ref[at, :features]).astype(BF16)
+        dpre_ref[at, :features] = (dgated * normed * slope_ref[at, :features]).astype(BF16)
         dmixed = norm_backward(dgated * proj_ref[at, :features].astype(F32), normed, scale)
-        dmixed = dmixed.astype(BF16)
+        dmixed_ref[at, :] = dmixed.astype(BF16)
+
+    def value_back(i, at):
         for p in range(pairs):
-            v_at = slice(features + p * 128, features + (p + 1) * 128)
-            q_at = slice(2 * features + p * 128, 2 * features + (p + 1) * 128)
-            k_at = slice(3 * features + p * 128, 3 * features + (p + 1) * 128)
-            down = dmixed[:, p * 128 : (p + 1) * 128]
+            here, v_at, _, _ = blocks(p)
+            down = dmixed_ref[at, here]
             dweights = dot(down, spread(proj_ref[at, v_at]), ((1,), (1,)))
-            dscores = (dweights * slopes[p]).astype(BF16)
-            dv = dot(weights[p], down, ((0,), (0,)))
+            dscores_ref[at, here] = (dweights * scores_ref[at, here]).astype(BF16)
+            dv = dot(weights_ref[at, here], down, ((0,), (0,)))
             dv = jnp.where(first, dv[:half], dv[half:])
-            dq = dot(dscores, spread(proj_ref[at, k_at]))
-            dk = dot(dscores, proj_ref[at, q_at], ((0,), (0,)))
+            dpre_ref[at, v_at] = (dv * slope_ref[at, v_at]).astype(BF16)
+
+    def score_back(i, at):
+        for p in range(pairs):
+            here, _, q_at, k_at = blocks(p)
+            dq = dot(dscores_ref[at, here], spread(proj_ref[at, k_at]))
+            dk = dot(dscores_ref[at, here], proj_ref[at, q_at], ((0,), (0,)))
             dk = jnp.where(first, dk[:half], dk[half:])
-            dpre_ref[at, v_at] = (dv * slope_ref[at, v_at]).astype(BF16)
             dpre_ref[at, q_at] = (dq * slope_ref[at, q_at]).astype(BF16)
             dpre_ref[at, k_at] = (dk * slope_ref[at, k_at]).astype(BF16)
-        return carry
-
-    lax.fori_loop(0, slots, attend, 0)
-
-    dpre_copy = pltpu.make_async_copy(dpre_ref, dpre_hbm, sent.at[8])
+
+    for body in (score, weigh, mix, turn, value_back, score_back):
+        for_slots(body)
+
+    dpre_copy = pltpu.make_async_copy(dpre_ref, dpre_hbm, sent.at[64])
     dpre_copy.start()
     tile_copies = []
+    core = lax.axis_index("core")
     left = lax.broadcasted_iota(jnp.int32, (16, 128), 1) < 64
     for y in range(8):
         block = dot(turned_ref[...], dpre_ref[:, y * 256 : (y + 1) * 256])
@@ -177,23 +201,26 @@
             for r in range(16):
                 upper = slice(r * 32, r * 32 + 16)
                 lower = slice(r * 32 + 16, r * 32 + 32)
-                z, core = r // 2, r % 2
+                z = r // 2
                 even = jnp.where(left, part[upper], swapped[lower])
                 odd = jnp.where(left, swapped[upper], part[lower])
                 for x, tile in ((2 * pair, even), (2 * pair + 1, odd)):
                     place = (x, y % 2, z % 2, y // 2, z // 2)
-                    tiles_ref[(core, *place)] = tile.astype(BF16)
-        part = (slice(None), slice(None), y % 2, slice(None), y // 2)
-        tile_copies.append(
-            pltpu.make_async_copy(tiles_ref.at[part], tiles_hbm.at[part], sent.at[y])
-        )
-        tile_copies[y].start()
+                    tiles_ref[(r % 2, *place)] = tile.astype(BF16)
+        for x in range(4):
+            for side, out_hbm in ((core, keep_hbm), (1 - core, send_hbm)):
+                part = (x, y % 2, slice(None), y // 2)
+                copy = pltpu.make_async_copy(
+                    tiles_ref.at[(side, *part)], out_hbm.at[part], sent.at[len(tile_copies)]
+                )
+                copy.start()
+                tile_copies.append(copy)
     for copy in (dpre_copy, *tile_copies):
         copy.wait()
 
 
 def history_kernel(
-    length_ref, hist_ref, cot_ref, win_ref, dpre_ref, after_ref, out_ref, done_ref, grad_ref
+    length_ref, hist_ref, cot_ref, win_ref, dpre_ref, after_ref, out_ref, grad_ref
 ):
     slots, positions, features = hist_ref.shape
     grad_ref[...] = dot(dpre_ref[...], win_ref[...], ((1,), (1,)))
@@ -206,13 +233,23 @@
         out_ref[i] = (seed + norm_backward(grad_ref[at, :], normed, scale)).astype(BF16)
         return carry
 
-    lax.fori_loop(0, slots, finish, 0)
-    done_ref[...] = jnp.zeros_like(done_ref)
-
-
-def sum_kernel(parts_ref, after_ref, out_ref, done_ref):
+    lax.fori_loop(0, slots, finish, 0, unroll=UNROLL)
+
+
+def pair_kernel(one_ref, other_ref, out_ref):
+    step = 16
+
+    def add(i, carry):
+        at = pl.ds(i * step, step)
+        out_ref[at] = (one_ref[at].astype(F32) + other_ref[at].astype(F32)).astype(BF16)
+        return carry
+
+    lax.fori_loop(0, out_ref.shape[0] // step, add, 0)
+
+
+def sum_kernel(parts_ref, out_ref, done_ref):
     parts, count = parts_ref.shape[:2]
-    step = min(count, 8)
+    step = 4
 
     def add(i, carry):
         at = pl.ds(i * step, step)
@@ -237,7 +274,7 @@
 VMEM = pl.BlockSpec(memory_space=pltpu.VMEM)
 SMEM = pl.BlockSpec(memory_space=pltpu.SMEM)
 HBM = pl.BlockSpec(memory_space=pltpu.HBM)
-TILES = (2, 4, 2, 2, 4, 4, 16, 128)
+TILES = (4, 2, 2, 4, 4, 16, 128)
 DONE = jax.ShapeDtypeStruct((8, 128), F32)
 
 
@@ -248,13 +285,13 @@
         weight_kernel,
         out_shape=(
             jax.ShapeDtypeStruct(TILES, BF16),
+            jax.ShapeDtypeStruct(TILES, BF16),
             jax.ShapeDtypeStruct((rows, 4 * features), BF16),
-            DONE,
         ),
         in_specs=[SMEM, HBM, HBM, HBM, HBM],
-        out_specs=(HBM, HBM, VMEM),
+        out_specs=(HBM, HBM, HBM),
         scratch_shapes=[
-            pltpu.VMEM(TILES, BF16),
+            pltpu.VMEM((2, *TILES), BF16),
             pltpu.VMEM((rows, 4 * features), BF16),
             pltpu.VMEM(hist.shape, BF16),
             pltpu.VMEM(hist.shape, BF16),
@@ -265,10 +302,14 @@
             pltpu.VMEM((rows, features), BF16),
             pltpu.VMEM((rows, 4 * features), BF16),
             pltpu.VMEM((rows, 4 * features), F32),
-            pltpu.VMEM((positions, features), F32),
+            pltpu.VMEM((rows, features), F32),
+            pltpu.VMEM((rows, features), BF16),
+            pltpu.VMEM((rows, features), F32),
+            pltpu.VMEM((rows, features), BF16),
+            pltpu.VMEM((rows, features), BF16),
             pltpu.VMEM((rows, features), BF16),
             pltpu.SemaphoreType.DMA((7,)),
-            pltpu.SemaphoreType.DMA((9,)),
+            pltpu.SemaphoreType.DMA((65,)),
         ],
         compiler_params=pltpu.CompilerParams(vmem_limit_bytes=56 * 2**20),
         cost_estimate=pl.CostEstimate(
@@ -281,9 +322,9 @@
     rows = dpre.shape[0]
     return pl.pallas_call(
         history_kernel,
-        out_shape=(jax.ShapeDtypeStruct(hist.shape, BF16), DONE),
+        out_shape=jax.ShapeDtypeStruct(hist.shape, BF16),
         in_specs=[SMEM, VMEM, VMEM, VMEM, VMEM, VMEM],
-        out_specs=(VMEM, VMEM),
+        out_specs=VMEM,
         scratch_shapes=[pltpu.VMEM((rows, hist.shape[-1]), F32)],
         compiler_params=pltpu.CompilerParams(vmem_limit_bytes=16 * 2**20),
         cost_estimate=pl.CostEstimate(
@@ -294,14 +335,24 @@
     )(lengths, hist, cot, w_in, dpre, after)
 
 
-def summed(parts, after):
+def pair_sum(one, other):
+    return pl.pallas_call(
+        pair_kernel,
+        out_shape=jax.ShapeDtypeStruct(one.shape, BF16),
+        in_specs=[VMEM, VMEM],
+        out_specs=VMEM,
+        compiler_params=pltpu.CompilerParams(vmem_limit_bytes=8 * 2**20),
+    )(one, other)
+
+
+def summed(parts):
     return pl.pallas_call(
         sum_kernel,
         out_shape=(jax.ShapeDtypeStruct(parts.shape[1:], BF16), DONE),
-        in_specs=[VMEM, VMEM],
+        in_specs=[VMEM],
         out_specs=(VMEM, VMEM),
         compiler_params=pltpu.CompilerParams(vmem_limit_bytes=8 * 2**20),
-    )(parts, after)
+    )(parts)
 
 
 def last_sum(parts):
@@ -320,11 +371,11 @@
 
 def shards(histories, cotangents, lengths, w_in, w_out):
     hist, cot, slot_lengths = histories[0, 0], cotangents[0, 0], lengths[0, 0]
-    tiles, dpre, done = weight_tiles(slot_lengths, hist, cot, w_in, w_out)
-    tiles, done = summed(exchanged(tiles.reshape(2, 256, 16, 128), "core"), done)
-    near = exchanged(tiles.reshape(16, 16, 16, 128), ("x", "yl", "zl"))
-    grads, done = history_grads(slot_lengths, hist, cot, w_in, dpre, done)
-    tiles, done = summed(near, done)
+    keep, send, dpre = weight_tiles(slot_lengths, hist, cot, w_in, w_out)
+    other = lax.ppermute(send.reshape(256, 16, 128), "core", [(0, 1), (1, 0)])
+    tiles = pair_sum(keep.reshape(256, 16, 128), other)
+    tiles, done = summed(exchanged(tiles.reshape(16, 16, 16, 128), ("x", "yl", "zl")))
+    grads = history_grads(slot_lengths, hist, cot, w_in, dpre, done)
     block = last_sum(exchanged(tiles.reshape(16, 1, 16, 128), ("yh", "zh")))
     return (grads[None, None], block)
 

time: 80.5 us -> 67.6 us (0.84)
  Pallas kernels: 27.1 us -> 14.1 us
  blocking collectives: 30.8 us -> 24 us
  starting transfers between devices: 9.27 us -> 14.5 us
  waiting for transfers between devices: 8.78 us -> 11.3 us
    pallas_call x1, Pallas kernels: 21.4 us -> 9.78 us  [weight_tiles(): pl.pallas_call(weight_kernel, out_shape=(jax.ShapeDtypeStruct(TILES, BF16...]
    all_to_all x2 -> x1, blocking collectives: 30.8 us -> 24 us  [exchanged(): return lax.all_to_all(tiles, axes, 0, 0, tiled=True)]
    all_to_all x1, starting transfers between devices: 9.27 us -> 12.6 us  [exchanged(): return lax.all_to_all(tiles, axes, 0, 0, tiled=True)]
    ppermute x0 -> x1, waiting for transfers between devices: none -> 2.84 us  [shards(): other = lax.ppermute(send.reshape(256, 16, 128), 'core', [(0, 1), (1, 0)])]
    ppermute x0 -> x1, starting transfers between devices: none -> 1.92 us  [shards(): other = lax.ppermute(send.reshape(256, 16, 128), 'core', [(0, 1), (1, 0)])]
    pallas_call x1 -> x2, Pallas kernels: 3.94 us -> 2.85 us  [the longest x1 2.55 us: history_grads(): pl.pallas_call(history_kernel, out_shape=jax.ShapeDtypeStruct(hist.shape,...]
    unnamed x14 -> x12, local copies, waits for them, and re-layouts: 3.38 us -> 2.65 us
  transfers between devices with their start and end apart: 1 -> 2, of which waited for: 1 -> 2; matrix products, arithmetic and copies ran while one was open for 0% -> 0% of each run, Pallas kernels for 5% -> 4%
where the time goes in v4:
time: 67.6 us; the launch traced here: 67.3 us
  blocking collectives  24 us (36%)
  starting transfers between devices  14.5 us (21%)
  Pallas kernels  14.1 us (21%)
  waiting for transfers between devices  11.3 us (17%)
  local copies, waits for them, and re-layouts  2.65 us (4%)
  between operations  0.74 us (1%)
    all_to_all x1, blocking collectives, exchanged(): return lax.all_to_all(tiles, axes, 0, 0, tiled=True)  24 us
    all_to_all x1, starting transfers between devices, exchanged(): return lax.all_to_all(tiles, axes, 0, 0, tiled=True)  12.6 us
    pallas_call x1, Pallas kernels, weight_tiles(): pl.pallas_call(weight_kernel, out_shape=(jax.ShapeDtypeStruct(TILES, BF16...  9.78 us
    all_to_all x1, waiting for transfers between devices, exchanged(): return lax.all_to_all(tiles, axes, 0, 0, tiled=True)  8.43 us
    ppermute x1, waiting for transfers between devices, shards(): other = lax.ppermute(send.reshape(256, 16, 128), 'core', [(0, 1), (1, 0)])  2.84 us
    unnamed x12, local copies, waits for them, and re-layouts  2.65 us
    pallas_call x1, Pallas kernels, history_grads(): pl.pallas_call(history_kernel, out_shape=jax.ShapeDtypeStruct(hist.shape,...  2.55 us
    ppermute x1, starting transfers between devices, shards(): other = lax.ppermute(send.reshape(256, 16, 128), 'core', [(0, 1), (1, 0)])  1.92 us
  transfers between devices with their start and end apart: 2, of which 2 were waited for; matrix products, arithmetic and copies ran while one was open for 0% of the time, Pallas kernels for 4%

profile of v4, /device:TPU:8, one launch (start us, length us, event | category | flops | bytes accessed | tf_op | source)
XLA Modules:
  0.0 67.3 jit_solution(16944034776928275758)
XLA Ops:
  0.6 9.8 %shard_map.68 = (bf16[4,2,2,4,4,16,128]{6,5,4,3,2,1,0:T(8,128)(2,1)}, bf16[4,2,2,4,4,16,128]{6,5,4,3,2,1,0:T(8,128)(2,1)}, bf16[384,2048]{1,0:T(8,128)(2,1)}) custom-call(s32[6]{0:T(128)} %bitcast.14, bf16[6,64,512]{2,1,0:T(8,128)(2,1)} %bitcast.10, bf16[6,64,512]{2,1,0:T(8,128)(2,1)} %bitcast.12, bf16[512,2048]{1,0:T(8,128)(2,1)} %win_ref.1, ...), custom_call_target="tpu_custom_call" | custom-call | flops 1811939328 | bytes 8388608 | tf_op jit(solution)/shard_map/pallas_call | solution.py:284
  10.4 1.9 %collective-permute-start = (bf16[256,16,128]{2,1,0:T(8,128)(2,1)}, bf16[256,16,128]{2,1,0:T(8,128)(2,1)S(1)}, u32[]{:S(2)}, u32[]{:S(2)}) collective-permute-start(bf16[256,16,128]{2,1,0:T(8,128)(2,1)} %bitcast.17), channel_id=1, source_target_pairs={{0,1},{1,0},{2,3},{3,2},{4,5},{5,4},{6,7},{7,6},{8,9},{9,8},{10,11... | collective-permute-start | bytes 3145736 | tf_op jit(solution)/shard_map/ppermute | solution.py:375
  12.3 2.8 %collective-permute-done.other_ref = bf16[256,16,128]{2,1,0:T(8,128)(2,1)S(1)} collective-permute-done((bf16[256,16,128]{2,1,0:T(8,128)(2,1)}, bf16[256,16,128]{2,1,0:T(8,128)(2,1)S(1)}, u32[]{:S(2)}, u32[]{:S(2)}) %collective-permute-start) | collective-permute-done | bytes 1048608 | tf_op jit(solution)/shard_map/ppermute | solution.py:375
  15.2 0.0 copy-start.2
  15.2 1.2 %copy-done.2 = bf16[4,2,2,4,4,16,128]{6,5,4,3,2,1,0:T(8,128)(2,1)S(1)} copy-done((bf16[4,2,2,4,4,16,128]{6,5,4,3,2,1,0:T(8,128)(2,1)S(1)}, bf16[4,2,2,4,4,16,128]{6,5,4,3,2,1,0:T(8,128)(2,1)}, u32[]{:S(2)}) %copy-start.2) | copy-done | bytes 1048600
  16.4 0.3 shard_map.69
  16.7 0.0 copy-start
  16.7 0.0 copy-start.3
  16.7 0.0 copy-start.4
  16.7 0.0 copy-start.5
  16.8 24.0 %all_to_all.10.parts_ref = bf16[16,16,16,128]{3,2,1,0:T(8,128)(2,1)S(1)} all-to-all(bf16[16,16,16,128]{3,2,1,0:T(8,128)(2,1)S(1)} %bitcast.8), channel_id=1, replica_groups=mesh['yh'=4,'yl'=2,'x'=4,'zh'=4,'zl'=2,'core'=2] {'x','yl','zl'}, dimensions={0} | all-to-all | bytes 2097152 | tf_op jit(solution)/shard_map/all_to_all | solution.py:369
  40.8 0.8 %shard_map.70 = (bf16[16,16,128]{2,1,0:T(8,128)(2,1)}, f32[8,128]{1,0:T(8,128)S(1)}) custom-call(bf16[16,16,16,128]{3,2,1,0:T(8,128)(2,1)S(1)} %all_to_all.10.parts_ref), custom_call_target="tpu_custom_call" | custom-call | tf_op jit(solution)/shard_map/pallas_call | solution.py:349
  41.5 12.6 %all-to-all-start.1 = ((bf16[16,1,16,128]{3,2,1,0:T(8,128)(2,1)}), bf16[16,1,16,128]{3,2,1,0:T(8,128)(2,1)S(1)}, u32[]{:S(2)}, u32[]{:S(2)}) async-start(bf16[16,1,16,128]{3,2,1,0:T(8,128)(2,1)} %bitcast.7), calls=%async_computation.1 | async-start | bytes 131072 | tf_op jit(solution)/shard_map/all_to_all | solution.py:369
  54.2 0.0 copy-done
  54.2 0.0 copy-done.3
  54.2 0.0 copy-done.4
  54.2 0.0 copy-done.5
  54.2 0.0 copy-start.1
  54.2 1.4 %copy-done.1 = bf16[384,2048]{1,0:T(8,128)(2,1)S(1)} copy-done((bf16[384,2048]{1,0:T(8,128)(2,1)S(1)}, bf16[384,2048]{1,0:T(8,128)(2,1)}, u32[]{:S(2)}) %copy-start.1) | copy-done | bytes 1572888
  55.6 2.6 %shard_map.71 = bf16[6,64,512]{2,1,0:T(8,128)(2,1)} custom-call(s32[6]{0:T(128)S(1)} %bitcast.15, bf16[6,64,512]{2,1,0:T(8,128)(2,1)S(1)} %bitcast.11, bf16[6,64,512]{2,1,0:T(8,128)(2,1)S(1)} %bitcast.13, bf16[512,2048]{1,0:T(8,128)(2,1)S(1)} %copy-done, bf16[384,2048]{1,0:T(8,128)(2,1)S(1)} %copy-done.1, f32[8,128]{1,0:T(8,128)S(1)} %get-tuple-element.10.after_ref), custom_call_target="tpu_custom_call" | custom-call | flops 805306368 | bytes 6291456 | tf_op jit(solution)/shard_map/pallas_call | solution.py:323
  58.2 8.4 %all-to-all-done.1.parts_ref = bf16[16,1,16,128]{3,2,1,0:T(8,128)(2,1)S(1)} async-done(((bf16[16,1,16,128]{3,2,1,0:T(8,128)(2,1)}), bf16[16,1,16,128]{3,2,1,0:T(8,128)(2,1)S(1)}, u32[]{:S(2)}, u32[]{:S(2)}) %all-to-all-start.1) | async-done | bytes 65568 | tf_op jit(solution)/shard_map/all_to_all | solution.py:369
  66.6 0.7 %shard_map.72 = f32[32,64]{1,0:T(8,128)} custom-call(bf16[16,1,16,128]{3,2,1,0:T(8,128)(2,1)S(1)} %all-to-all-done.1.parts_ref), custom_call_target="tpu_custom_call" | custom-call | tf_op jit(solution)/shard_map/pallas_call | solution.py:359
Async XLA Ops:
  10.4 4.8 %collective-permute-start = (bf16[256,16,128]{2,1,0:T(8,128)(2,1)}, bf16[256,16,128]{2,1,0:T(8,128)(2,1)S(1)}, u32[]{:S(2)}, u32[]{:S(2)}) collective-permute-start(bf16[256,16,128]{2,1,0:T(8,128)(2,1)} %bitcast.17), channel_id=1, source_target_pairs={{0,1},{1,0},{2,3},{3,2},{4,5},{5,4},{6,7},{7,6},{8,9},{9,8},{10,11... | collective-permute-start | bytes 3145736 | tf_op jit(solution)/shard_map/ppermute | solution.py:375
  15.2 1.2 %copy-start.2 = (bf16[4,2,2,4,4,16,128]{6,5,4,3,2,1,0:T(8,128)(2,1)S(1)}, bf16[4,2,2,4,4,16,128]{6,5,4,3,2,1,0:T(8,128)(2,1)}, u32[]{:S(2)}) copy-start(bf16[4,2,2,4,4,16,128]{6,5,4,3,2,1,0:T(8,128)(2,1)} %get-tuple-element.8) | copy-start | bytes 3145732
  16.7 37.4 %copy-start = (bf16[512,2048]{1,0:T(8,128)(2,1)S(1)}, bf16[512,2048]{1,0:T(8,128)(2,1)}, u32[]{:S(2)}) copy-start(bf16[512,2048]{1,0:T(8,128)(2,1)} %win_ref.1) | copy-start | bytes 6291460
  16.7 37.4 %copy-start.3 = (bf16[1,1,6,64,512]{4,3,2,1,0:T(8,128)(2,1)S(1)}, bf16[1,1,6,64,512]{4,3,2,1,0:T(8,128)(2,1)}, u32[]{:S(2)}) copy-start(bf16[1,1,6,64,512]{4,3,2,1,0:T(8,128)(2,1)} %param.5) | copy-start | bytes 1179652
  16.7 37.4 %copy-start.4 = (bf16[1,1,6,64,512]{4,3,2,1,0:T(8,128)(2,1)S(1)}, bf16[1,1,6,64,512]{4,3,2,1,0:T(8,128)(2,1)}, u32[]{:S(2)}) copy-start(bf16[1,1,6,64,512]{4,3,2,1,0:T(8,128)(2,1)} %param.6) | copy-start | bytes 1179652
  16.7 37.4 %copy-start.5 = (s32[1,1,6]{2,1,0:T(1,128)S(1)}, s32[1,1,6]{2,1,0:T(1,128)}, u32[]{:S(2)}) copy-start(s32[1,1,6]{2,1,0:T(1,128)} %param.7) | copy-start | bytes 76
  41.5 25.0 %all-to-all-start.1 = ((bf16[16,1,16,128]{3,2,1,0:T(8,128)(2,1)}), bf16[16,1,16,128]{3,2,1,0:T(8,128)(2,1)S(1)}, u32[]{:S(2)}, u32[]{:S(2)}) async-start(bf16[16,1,16,128]{3,2,1,0:T(8,128)(2,1)} %bitcast.7), calls=%async_computation.1 | async-start | bytes 131072 | tf_op jit(solution)/shard_map/all_to_all | solution.py:369
  54.2 1.4 %copy-start.1 = (bf16[384,2048]{1,0:T(8,128)(2,1)S(1)}, bf16[384,2048]{1,0:T(8,128)(2,1)}, u32[]{:S(2)}) copy-start(bf16[384,2048]{1,0:T(8,128)(2,1)} %get-tuple-element.7.dpre_ref) | copy-start | bytes 4718596

commit v5 on v4

--- a/solution.py
+++ b/solution.py
@@ -42,8 +42,8 @@
     cot_hbm,
     win_hbm,
     wout_hbm,
-    keep_hbm,
     send_hbm,
+    turned_hbm,
     dpre_hbm,
     tiles_ref,
     dpre_ref,
@@ -91,7 +91,12 @@
         return carry
 
     lax.fori_loop(0, slots, prepare, 0, unroll=UNROLL)
-    turned_ref[...] = normed_ref[...].T
+    turned = normed_ref[...].T
+    for r in range(16):
+        place = (r % 2) * 8 + r // 2
+        turned_ref[place * 32 : (place + 1) * 32, :] = turned[r * 32 : (r + 1) * 32, :]
+    turned_copy = pltpu.make_async_copy(turned_ref, turned_hbm, sent.at[33])
+    turned_copy.start()
 
     width = 256
     for j in range(4 * features // width):
@@ -188,42 +193,80 @@
     for body in (score, weigh, mix, turn, value_back, score_back):
         for_slots(body)
 
-    dpre_copy = pltpu.make_async_copy(dpre_ref, dpre_hbm, sent.at[64])
+    dpre_copy = pltpu.make_async_copy(dpre_ref, dpre_hbm, sent.at[32])
     dpre_copy.start()
-    tile_copies = []
-    core = lax.axis_index("core")
+    copies = [dpre_copy, turned_copy]
+    other = 1 - lax.axis_index("core")
+    for y in range(8):
+        half_tiles(other, y, turned_ref, dpre_ref, tiles_ref)
+        for x in range(4):
+            part = (x, y % 2, slice(None), y // 2)
+            copy = pltpu.make_async_copy(
+                tiles_ref.at[part], send_hbm.at[part], sent.at[y * 4 + x]
+            )
+            copy.start()
+            copies.append(copy)
+    for copy in copies:
+        copy.wait()
+
+
+def half_tiles(core, y, turned_ref, dpre_ref, tiles_ref):
+    rows = turned_ref.shape[0] // 2
+    mine = pl.ds(pl.multiple_of(core * rows, rows), rows)
     left = lax.broadcasted_iota(jnp.int32, (16, 128), 1) < 64
+    block = dot(turned_ref[mine, :], dpre_ref[:, y * 256 : (y + 1) * 256])
+    for pair in range(2):
+        part = block[:, pair * 128 : (pair + 1) * 128]
+        swapped = pltpu.roll(part, 64, 1)
+        for z in range(8):
+            upper = slice(z * 32, z * 32 + 16)
+            lower = slice(z * 32 + 16, z * 32 + 32)
+            even = jnp.where(left, part[upper], swapped[lower])
+            odd = jnp.where(left, swapped[upper], part[lower])
+            for x, tile in ((2 * pair, even), (2 * pair + 1, odd)):
+                tiles_ref[x, y % 2, z % 2, y // 2, z // 2] = tile.astype(BF16)
+
+
+def keep_kernel(turned_ref, dpre_ref, tiles_ref):
     for y in range(8):
-        block = dot(turned_ref[...], dpre_ref[:, y * 256 : (y + 1) * 256])
-        for pair in range(2):
-            part = block[:, pair * 128 : (pair + 1) * 128]
-            swapped = pltpu.roll(part, 64, 1)
-            for r in range(16):
-                upper = slice(r * 32, r * 32 + 16)
-                lower = slice(r * 32 + 16, r * 32 + 32)
-                z = r // 2
-                even = jnp.where(left, part[upper], swapped[lower])
-                odd = jnp.where(left, swapped[upper], part[lower])
-                for x, tile in ((2 * pair, even), (2 * pair + 1, odd)):
-                    place = (x, y % 2, z % 2, y // 2, z // 2)
-                    tiles_ref[(r % 2, *place)] = tile.astype(BF16)
-        for x in range(4):
-            for side, out_hbm in ((core, keep_hbm), (1 - core, send_hbm)):
-                part = (x, y % 2, slice(None), y // 2)
-                copy = pltpu.make_async_copy(
-                    tiles_ref.at[(side, *part)], out_hbm.at[part], sent.at[len(tile_copies)]
-                )
-                copy.start()
-                tile_copies.append(copy)
-    for copy in (dpre_copy, *tile_copies):
-        copy.wait()
+        half_tiles(lax.axis_index("core"), y, turned_ref, dpre_ref, tiles_ref)
 
 
 def history_kernel(
-    length_ref, hist_ref, cot_ref, win_ref, dpre_ref, after_ref, out_ref, grad_ref
+    length_ref,
+    hist_hbm,
+    cot_hbm,
+    win_hbm,
+    dpre_hbm,
+    after_ref,
+    out_ref,
+    hist_ref,
+    cot_ref,
+    win_ref,
+    dpre_ref,
+    grad_ref,
+    arrived,
 ):
     slots, positions, features = hist_ref.shape
-    grad_ref[...] = dot(dpre_ref[...], win_ref[...], ((1,), (1,)))
+    copies = []
+
+    def fetch(source, target):
+        copies.append(pltpu.make_async_copy(source, target, arrived.at[len(copies)]))
+        copies[-1].start()
+
+    parts = [slice(j * features, (j + 1) * features) for j in range(4)]
+    for part in parts:
+        fetch(dpre_hbm.at[:, part], dpre_ref.at[:, part])
+        fetch(win_hbm.at[:, part], win_ref.at[:, part])
+    fetch(hist_hbm, hist_ref)
+    fetch(cot_hbm, cot_ref)
+    for j, part in enumerate(parts):
+        copies[2 * j].wait()
+        copies[2 * j + 1].wait()
+        share = dot(dpre_ref[:, part], win_ref[:, part], ((1,), (1,)))
+        grad_ref[...] = share if j == 0 else grad_ref[...] + share
+    copies[-2].wait()
+    copies[-1].wait()
 
     def finish(i, carry):
         at = pl.ds(pl.multiple_of(i * positions, positions), positions)
@@ -275,6 +318,7 @@
 SMEM = pl.BlockSpec(memory_space=pltpu.SMEM)
 HBM = pl.BlockSpec(memory_space=pltpu.HBM)
 TILES = (4, 2, 2, 4, 4, 16, 128)
+ANY = pl.BlockSpec(memory_space=pl.ANY)
 DONE = jax.ShapeDtypeStruct((8, 128), F32)
 
 
@@ -285,13 +329,13 @@
         weight_kernel,
         out_shape=(
             jax.ShapeDtypeStruct(TILES, BF16),
-            jax.ShapeDtypeStruct(TILES, BF16),
+            jax.ShapeDtypeStruct((features, rows), BF16),
             jax.ShapeDtypeStruct((rows, 4 * features), BF16),
         ),
         in_specs=[SMEM, HBM, HBM, HBM, HBM],
         out_specs=(HBM, HBM, HBM),
         scratch_shapes=[
-            pltpu.VMEM((2, *TILES), BF16),
+            pltpu.VMEM(TILES, BF16),
             pltpu.VMEM((rows, 4 * features), BF16),
             pltpu.VMEM(hist.shape, BF16),
             pltpu.VMEM(hist.shape, BF16),
@@ -309,7 +353,7 @@
             pltpu.VMEM((rows, features), BF16),
             pltpu.VMEM((rows, features), BF16),
             pltpu.SemaphoreType.DMA((7,)),
-            pltpu.SemaphoreType.DMA((65,)),
+            pltpu.SemaphoreType.DMA((34,)),
         ],
         compiler_params=pltpu.CompilerParams(vmem_limit_bytes=56 * 2**20),
         cost_estimate=pl.CostEstimate(
@@ -318,15 +362,37 @@
     )(lengths, hist, cot, w_in, w_out)
 
 
+def kept_tiles(turned, dpre):
+    return pl.pallas_call(
+        keep_kernel,
+        out_shape=jax.ShapeDtypeStruct(TILES, BF16),
+        in_specs=[VMEM, VMEM],
+        out_specs=VMEM,
+        compiler_params=pltpu.CompilerParams(vmem_limit_bytes=12 * 2**20),
+        cost_estimate=pl.CostEstimate(
+            flops=turned.shape[0] * dpre.shape[0] * dpre.shape[1],
+            bytes_accessed=3 * 2**20,
+            transcendentals=0,
+        ),
+    )(turned, dpre)
+
+
 def history_grads(lengths, hist, cot, w_in, dpre, after):
     rows = dpre.shape[0]
     return pl.pallas_call(
         history_kernel,
         out_shape=jax.ShapeDtypeStruct(hist.shape, BF16),
-        in_specs=[SMEM, VMEM, VMEM, VMEM, VMEM, VMEM],
+        in_specs=[SMEM, HBM, HBM, HBM, HBM, ANY],
         out_specs=VMEM,
-        scratch_shapes=[pltpu.VMEM((rows, hist.shape[-1]), F32)],
-        compiler_params=pltpu.CompilerParams(vmem_limit_bytes=16 * 2**20),
+        scratch_shapes=[
+            pltpu.VMEM(hist.shape, BF16),
+            pltpu.VMEM(hist.shape, BF16),
+            pltpu.VMEM(w_in.shape, BF16),
+            pltpu.VMEM(dpre.shape, BF16),
+            pltpu.VMEM((rows, hist.shape[-1]), F32),
+            pltpu.SemaphoreType.DMA((10,)),
+        ],
+        compiler_params=pltpu.CompilerParams(vmem_limit_bytes=56 * 2**20),
         cost_estimate=pl.CostEstimate(
             flops=2 * rows * dpre.shape[1] * hist.shape[-1],
             bytes_accessed=6 * 2**20,
@@ -371,8 +437,9 @@
 
 def shards(histories, cotangents, lengths, w_in, w_out):
     hist, cot, slot_lengths = histories[0, 0], cotangents[0, 0], lengths[0, 0]
-    keep, send, dpre = weight_tiles(slot_lengths, hist, cot, w_in, w_out)
+    send, turned, dpre = weight_tiles(slot_lengths, hist, cot, w_in, w_out)
     other = lax.ppermute(send.reshape(256, 16, 128), "core", [(0, 1), (1, 0)])
+    keep = kept_tiles(turned, dpre)
     tiles = pair_sum(keep.reshape(256, 16, 128), other)
     tiles, done = summed(exchanged(tiles.reshape(16, 16, 16, 128), ("x", "yl", "zl")))
     grads = history_grads(slot_lengths, hist, cot, w_in, dpre, done)

time: 67.6 us -> 66.6 us (0.985)
  waiting for transfers between devices: 11.3 us -> 8 us
  Pallas kernels: 14.1 us -> 15.9 us
    ppermute x1, waiting for transfers between devices: 2.84 us -> 0.01 us  [shards(): other = lax.ppermute(send.reshape(256, 16, 128), 'core', [(0, 1), (1, 0)])]
    pallas_call x1, Pallas kernels: 2.55 us -> 4.46 us  [history_grads(): pl.pallas_call(history_kernel, out_shape=jax.ShapeDtypeStruct(hist.shape,...]
    pallas_call x1, Pallas kernels: 9.78 us -> 8.9 us  [weight_tiles(): pl.pallas_call(weight_kernel, out_shape=(jax.ShapeDtypeStruct(TILES, BF16...]
    pallas_call x0 -> x1, Pallas kernels: none -> 0.78 us  [kept_tiles(): pl.pallas_call(keep_kernel, out_shape=jax.ShapeDtypeStruct(TILES, BF16),...]
    unnamed x12 -> x6, local copies, waits for them, and re-layouts: 2.65 us -> 2.99 us
  transfers between devices with their start and end apart: 2 -> 2, of which waited for: 2 -> 1; matrix products, arithmetic and copies ran while one was open for 0% -> 0% of each run, Pallas kernels for 4% -> 8%
where the time goes in v5:
time: 66.6 us; the launch traced here: 66.2 us
  blocking collectives  23.8 us (36%)
  Pallas kernels  15.9 us (24%)
  starting transfers between devices  14.9 us (22%)
  waiting for transfers between devices  8 us (12%)
  local copies, waits for them, and re-layouts  2.99 us (4%)
  between operations  0.7 us (1%)
    all_to_all x1, blocking collectives, exchanged(): return lax.all_to_all(tiles, axes, 0, 0, tiled=True)  23.8 us
    all_to_all x1, starting transfers between devices, exchanged(): return lax.all_to_all(tiles, axes, 0, 0, tiled=True)  12.9 us
    pallas_call x1, Pallas kernels, weight_tiles(): pl.pallas_call(weight_kernel, out_shape=(jax.ShapeDtypeStruct(TILES, BF16...  8.9 us
    all_to_all x1, waiting for transfers between devices, exchanged(): return lax.all_to_all(tiles, axes, 0, 0, tiled=True)  7.99 us
    pallas_call x1, Pallas kernels, history_grads(): pl.pallas_call(history_kernel, out_shape=jax.ShapeDtypeStruct(hist.shape,...  4.46 us
    unnamed x6, local copies, waits for them, and re-layouts  2.99 us
    ppermute x1, starting transfers between devices, shards(): other = lax.ppermute(send.reshape(256, 16, 128), 'core', [(0, 1), (1, 0)])  1.92 us
  transfers between devices with their start and end apart: 2, of which 1 were waited for; matrix products, arithmetic and copies ran while one was open for 0% of the time, Pallas kernels for 8%

profile of v5, /device:TPU:8, one launch (start us, length us, event | category | flops | bytes accessed | tf_op | source)
XLA Modules:
  0.0 66.2 jit_solution(9891046186871325565)
XLA Ops:
  0.6 8.9 %shard_map.68 = (bf16[4,2,2,4,4,16,128]{6,5,4,3,2,1,0:T(8,128)(2,1)}, bf16[512,384]{1,0:T(8,128)(2,1)}, bf16[384,2048]{1,0:T(8,128)(2,1)}) custom-call(s32[6]{0:T(128)} %bitcast.15, bf16[6,64,512]{2,1,0:T(8,128)(2,1)} %bitcast.10, bf16[6,64,512]{2,1,0:T(8,128)(2,1)} %bitcast.12, bf16[512,2048]{1,0:T(8,128)(2,1)} %win_hbm.3, bf16[512,512]{1,0:T(8,128)(2,1)} %wout_hbm.1), custom_call_target="tpu_custom_call" | custom-call | flops 1811939328 | bytes 8388608 | tf_op jit(solution)/shard_map/pallas_call | solution.py:328
  9.5 1.9 %collective-permute-start = (bf16[256,16,128]{2,1,0:T(8,128)(2,1)}, bf16[256,16,128]{2,1,0:T(8,128)(2,1)S(1)}, u32[]{:S(2)}, u32[]{:S(2)}) collective-permute-start(bf16[256,16,128]{2,1,0:T(8,128)(2,1)} %bitcast.17), channel_id=1, source_target_pairs={{0,1},{1,0},{2,3},{3,2},{4,5},{5,4},{6,7},{7,6},{8,9},{9,8},{10,11... | collective-permute-start | bytes 3145736 | tf_op jit(solution)/shard_map/ppermute | solution.py:441
  11.5 0.0 copy-start
  11.5 1.4 %copy-done = bf16[384,2048]{1,0:T(8,128)(2,1)S(1)} copy-done((bf16[384,2048]{1,0:T(8,128)(2,1)S(1)}, bf16[384,2048]{1,0:T(8,128)(2,1)}, u32[]{:S(2)}) %copy-start) | copy-done | bytes 1572888
  12.9 0.0 copy-start.1
  12.9 1.0 %copy-done.1 = bf16[512,384]{1,0:T(8,128)(2,1)S(1)} copy-done((bf16[512,384]{1,0:T(8,128)(2,1)S(1)}, bf16[512,384]{1,0:T(8,128)(2,1)}, u32[]{:S(2)}) %copy-start.1) | copy-done | bytes 393240
  13.9 0.8 %shard_map.69 = bf16[4,2,2,4,4,16,128]{6,5,4,3,2,1,0:T(8,128)(2,1)S(1)} custom-call(bf16[512,384]{1,0:T(8,128)(2,1)S(1)} %copy-done.1, bf16[384,2048]{1,0:T(8,128)(2,1)S(1)} %copy-done), custom_call_target="tpu_custom_call" | custom-call | flops 402653184 | bytes 3145728 | tf_op jit(solution)/shard_map/pallas_call | solution.py:366
  14.7 0.0 collective-permute-done.other_ref
  14.7 0.3 shard_map.70
  15.0 23.8 %all_to_all.10.parts_ref = bf16[16,16,16,128]{3,2,1,0:T(8,128)(2,1)S(1)} all-to-all(bf16[16,16,16,128]{3,2,1,0:T(8,128)(2,1)S(1)} %bitcast.9), channel_id=1, replica_groups=mesh['yh'=4,'yl'=2,'x'=4,'zh'=4,'zl'=2,'core'=2] {'x','yl','zl'}, dimensions={0} | all-to-all | bytes 2097152 | tf_op jit(solution)/shard_map/all_to_all | solution.py:435
  38.8 0.8 %shard_map.71 = (bf16[16,16,128]{2,1,0:T(8,128)(2,1)}, f32[8,128]{1,0:T(8,128)S(1)}) custom-call(bf16[16,16,16,128]{3,2,1,0:T(8,128)(2,1)S(1)} %all_to_all.10.parts_ref), custom_call_target="tpu_custom_call" | custom-call | tf_op jit(solution)/shard_map/pallas_call | solution.py:415
  39.5 0.0 copy-start.2
  39.5 0.6 copy-done.2
  40.1 12.9 %all-to-all-start.1 = ((bf16[16,1,16,128]{3,2,1,0:T(8,128)(2,1)}), bf16[16,1,16,128]{3,2,1,0:T(8,128)(2,1)S(1)}, u32[]{:S(2)}, u32[]{:S(2)}) async-start(bf16[16,1,16,128]{3,2,1,0:T(8,128)(2,1)} %bitcast.7), calls=%async_computation.1 | async-start | bytes 131072 | tf_op jit(solution)/shard_map/all_to_all | solution.py:435
  53.1 4.5 %shard_map.72 = bf16[6,64,512]{2,1,0:T(8,128)(2,1)} custom-call(s32[6]{0:T(128)} %bitcast.16, bf16[6,64,512]{2,1,0:T(8,128)(2,1)} %bitcast.11, bf16[6,64,512]{2,1,0:T(8,128)(2,1)} %bitcast.13, bf16[512,2048]{1,0:T(8,128)(2,1)} %win_hbm.3, bf16[384,2048]{1,0:T(8,128)(2,1)} %get-tuple-element.7.dpre_ref.dpre_hbm, f32[8,128]{1,0:T(8,128)} %copy-done.2), custom_call_target="tpu_custom_call" | custom-call | flops 805306368 | bytes 6291456 | tf_op jit(solution)/shard_map/pallas_call | solution.py:382
  57.6 8.0 %all-to-all-done.1.parts_ref = bf16[16,1,16,128]{3,2,1,0:T(8,128)(2,1)S(1)} async-done(((bf16[16,1,16,128]{3,2,1,0:T(8,128)(2,1)}), bf16[16,1,16,128]{3,2,1,0:T(8,128)(2,1)S(1)}, u32[]{:S(2)}, u32[]{:S(2)}) %all-to-all-start.1) | async-done | bytes 65568 | tf_op jit(solution)/shard_map/all_to_all | solution.py:435
  65.5 0.7 %shard_map.73 = f32[32,64]{1,0:T(8,128)} custom-call(bf16[16,1,16,128]{3,2,1,0:T(8,128)(2,1)S(1)} %all-to-all-done.1.parts_ref), custom_call_target="tpu_custom_call" | custom-call | tf_op jit(solution)/shard_map/pallas_call | solution.py:425
Async XLA Ops:
  9.5 5.1 %collective-permute-start = (bf16[256,16,128]{2,1,0:T(8,128)(2,1)}, bf16[256,16,128]{2,1,0:T(8,128)(2,1)S(1)}, u32[]{:S(2)}, u32[]{:S(2)}) collective-permute-start(bf16[256,16,128]{2,1,0:T(8,128)(2,1)} %bitcast.17), channel_id=1, source_target_pairs={{0,1},{1,0},{2,3},{3,2},{4,5},{5,4},{6,7},{7,6},{8,9},{9,8},{10,11... | collective-permute-start | bytes 3145736 | tf_op jit(solution)/shard_map/ppermute | solution.py:441
  11.5 1.4 %copy-start = (bf16[384,2048]{1,0:T(8,128)(2,1)S(1)}, bf16[384,2048]{1,0:T(8,128)(2,1)}, u32[]{:S(2)}) copy-start(bf16[384,2048]{1,0:T(8,128)(2,1)} %get-tuple-element.7.dpre_ref.dpre_hbm) | copy-start | bytes 4718596
  12.9 1.0 %copy-start.1 = (bf16[512,384]{1,0:T(8,128)(2,1)S(1)}, bf16[512,384]{1,0:T(8,128)(2,1)}, u32[]{:S(2)}) copy-start(bf16[512,384]{1,0:T(8,128)(2,1)} %get-tuple-element.8.turned_ref) | copy-start | bytes 1179652
  39.5 0.6 copy-start.2
  40.1 25.4 %all-to-all-start.1 = ((bf16[16,1,16,128]{3,2,1,0:T(8,128)(2,1)}), bf16[16,1,16,128]{3,2,1,0:T(8,128)(2,1)S(1)}, u32[]{:S(2)}, u32[]{:S(2)}) async-start(bf16[16,1,16,128]{3,2,1,0:T(8,128)(2,1)} %bitcast.7), calls=%async_computation.1 | async-start | bytes 131072 | tf_op jit(solution)/shard_map/all_to_all | solution.py:435

commit v6 on v5

--- a/solution.py
+++ b/solution.py
@@ -69,39 +69,35 @@
     pairs = features // 128
     half = positions
 
-    def columns_of(ref, j):
-        return ref.at[:, j * features : (j + 1) * features]
-
-    hist_copy = pltpu.make_async_copy(hist_hbm, hist_ref, arrived.at[0])
-    win_copies = [
-        pltpu.make_async_copy(columns_of(win_hbm, j), columns_of(win_ref, j), arrived.at[1 + j])
-        for j in range(4)
-    ]
-    cot_copy = pltpu.make_async_copy(cot_hbm, cot_ref, arrived.at[5])
-    wout_copy = pltpu.make_async_copy(wout_hbm, wout_ref, arrived.at[6])
-    for copy in (hist_copy, *win_copies, cot_copy, wout_copy):
+    started = []
+
+    def fetch(source, target):
+        copy = pltpu.make_async_copy(source, target, arrived.at[len(started)])
         copy.start()
+        started.append(copy)
+        return copy
+
+    hist_copy = fetch(hist_hbm, hist_ref)
+    width = 256
+    quarters = [slice(j * features // 4, (j + 1) * features // 4) for j in range(4)]
+    win_copies = [fetch(win_hbm.at[part, :], win_ref.at[part, :]) for part in quarters]
+    cot_copy = fetch(cot_hbm, cot_ref)
+    wout_copy = fetch(wout_hbm, wout_ref)
 
     hist_copy.wait()
-
-    def prepare(i, carry):
-        at = pl.ds(pl.multiple_of(i * positions, positions), positions)
+    for i in range(slots):
         normed, _ = normalised(hist_ref[i].astype(F32))
-        normed_ref[at, :] = normed.astype(BF16)
-        return carry
-
-    lax.fori_loop(0, slots, prepare, 0, unroll=UNROLL)
+        normed_ref[i * positions : (i + 1) * positions, :] = normed.astype(BF16)
     turned = normed_ref[...].T
     for r in range(16):
         place = (r % 2) * 8 + r // 2
         turned_ref[place * 32 : (place + 1) * 32, :] = turned[r * 32 : (r + 1) * 32, :]
-    turned_copy = pltpu.make_async_copy(turned_ref, turned_hbm, sent.at[33])
+    turned_copy = pltpu.make_async_copy(turned_ref, turned_hbm, sent.at[32])
     turned_copy.start()
 
-    width = 256
+    for copy in win_copies:
+        copy.wait()
     for j in range(4 * features // width):
-        if (j * width) % features == 0:
-            win_copies[j * width // features].wait()
         columns = slice(j * width, (j + 1) * width)
         pre = dot(normed_ref[...], win_ref[:, columns])
         gate = sigmoid(pre)
@@ -109,15 +105,10 @@
         proj_ref[:, columns] = value.astype(BF16)
         slope_ref[:, columns] = gate + value * (1.0 - gate)
     cot_copy.wait()
-
-    def mask(i, carry):
-        at = pl.ds(pl.multiple_of(i * positions, positions), positions)
-        row = lax.broadcasted_iota(jnp.int32, (positions, features), 0)
-        cot = cot_ref[i].astype(F32)
-        seed_ref[at, :] = jnp.where(row < length_ref[i], cot, 0.0).astype(BF16)
-        return carry
-
-    lax.fori_loop(0, slots, mask, 0, unroll=UNROLL)
+    row = lax.broadcasted_iota(jnp.int32, (positions, features), 0)
+    for i in range(slots):
+        seed = jnp.where(row < length_ref[i], cot_ref[i].astype(F32), 0.0)
+        seed_ref[i * positions : (i + 1) * positions, :] = seed.astype(BF16)
     wout_copy.wait()
     dgated_ref[...] = dot(seed_ref[...], wout_ref[...], ((1,), (1,))).astype(BF16)
 
@@ -190,12 +181,24 @@
             dpre_ref[at, q_at] = (dq * slope_ref[at, q_at]).astype(BF16)
             dpre_ref[at, k_at] = (dk * slope_ref[at, k_at]).astype(BF16)
 
-    for body in (score, weigh, mix, turn, value_back, score_back):
+    copies = [turned_copy]
+
+    def send_on(first_column, end_column):
+        part = (slice(None), slice(first_column, end_column))
+        copy = pltpu.make_async_copy(
+            dpre_ref.at[part], dpre_hbm.at[part], sent.at[32 + len(copies)]
+        )
+        copy.start()
+        copies.append(copy)
+
+    for body in (score, weigh, mix, turn):
         for_slots(body)
-
-    dpre_copy = pltpu.make_async_copy(dpre_ref, dpre_hbm, sent.at[32])
-    dpre_copy.start()
-    copies = [dpre_copy, turned_copy]
+    send_on(0, features)
+    for_slots(value_back)
+    send_on(features, 2 * features)
+    for_slots(score_back)
+    send_on(2 * features, 4 * features)
+
     other = 1 - lax.axis_index("core")
     for y in range(8):
         half_tiles(other, y, turned_ref, dpre_ref, tiles_ref)
@@ -290,20 +293,13 @@
     lax.fori_loop(0, out_ref.shape[0] // step, add, 0)
 
 
-def sum_kernel(parts_ref, out_ref, done_ref):
+def sum_kernel(parts_ref, out_ref):
     parts, count = parts_ref.shape[:2]
-    step = 4
-
-    def add(i, carry):
-        at = pl.ds(i * step, step)
-        total = parts_ref[0, at].astype(F32)
+    for i in range(count):
+        total = parts_ref[0, i].astype(F32)
         for p in range(1, parts):
-            total += parts_ref[p, at].astype(F32)
-        out_ref[at] = total.astype(BF16)
-        return carry
-
-    lax.fori_loop(0, count // step, add, 0)
-    done_ref[...] = jnp.zeros_like(done_ref)
+            total += parts_ref[p, i].astype(F32)
+        out_ref[i] = total.astype(BF16)
 
 
 def last_kernel(parts_ref, out_ref):
@@ -319,7 +315,6 @@
 HBM = pl.BlockSpec(memory_space=pltpu.HBM)
 TILES = (4, 2, 2, 4, 4, 16, 128)
 ANY = pl.BlockSpec(memory_space=pl.ANY)
-DONE = jax.ShapeDtypeStruct((8, 128), F32)
 
 
 def weight_tiles(lengths, hist, cot, w_in, w_out):
@@ -353,7 +348,7 @@
             pltpu.VMEM((rows, features), BF16),
             pltpu.VMEM((rows, features), BF16),
             pltpu.SemaphoreType.DMA((7,)),
-            pltpu.SemaphoreType.DMA((34,)),
+            pltpu.SemaphoreType.DMA((36,)),
         ],
         compiler_params=pltpu.CompilerParams(vmem_limit_bytes=56 * 2**20),
         cost_estimate=pl.CostEstimate(
@@ -414,9 +409,9 @@
 def summed(parts):
     return pl.pallas_call(
         sum_kernel,
-        out_shape=(jax.ShapeDtypeStruct(parts.shape[1:], BF16), DONE),
+        out_shape=jax.ShapeDtypeStruct(parts.shape[1:], BF16),
         in_specs=[VMEM],
-        out_specs=(VMEM, VMEM),
+        out_specs=VMEM,
         compiler_params=pltpu.CompilerParams(vmem_limit_bytes=8 * 2**20),
     )(parts)
 
@@ -441,8 +436,8 @@
     other = lax.ppermute(send.reshape(256, 16, 128), "core", [(0, 1), (1, 0)])
     keep = kept_tiles(turned, dpre)
     tiles = pair_sum(keep.reshape(256, 16, 128), other)
-    tiles, done = summed(exchanged(tiles.reshape(16, 16, 16, 128), ("x", "yl", "zl")))
-    grads = history_grads(slot_lengths, hist, cot, w_in, dpre, done)
+    tiles = summed(exchanged(tiles.reshape(16, 16, 16, 128), ("x", "yl", "zl")))
+    grads = history_grads(slot_lengths, hist, cot, w_in, dpre, tiles)
     block = last_sum(exchanged(tiles.reshape(16, 1, 16, 128), ("yh", "zh")))
     return (grads[None, None], block)
 

time: 66.6 us -> 65.3 us (0.980)
    unnamed x6 -> x4, local copies, waits for them, and re-layouts: 2.99 us -> 2.4 us
where the time goes in v6:
time: 65.3 us; the launch traced here: 65 us
  blocking collectives  23.8 us (36%)
  Pallas kernels  15.3 us (23%)
  starting transfers between devices  14.9 us (23%)
  waiting for transfers between devices  7.99 us (12%)
  local copies, waits for them, and re-layouts  2.4 us (4%)
  between operations  0.7 us (1%)
    all_to_all x1, blocking collectives, exchanged(): return lax.all_to_all(tiles, axes, 0, 0, tiled=True)  23.8 us
    all_to_all x1, starting transfers between devices, exchanged(): return lax.all_to_all(tiles, axes, 0, 0, tiled=True)  12.9 us
    pallas_call x1, Pallas kernels, weight_tiles(): pl.pallas_call(weight_kernel, out_shape=(jax.ShapeDtypeStruct(TILES, BF16...  8.27 us
    all_to_all x1, waiting for transfers between devices, exchanged(): return lax.all_to_all(tiles, axes, 0, 0, tiled=True)  7.99 us
    pallas_call x1, Pallas kernels, history_grads(): pl.pallas_call(history_kernel, out_shape=jax.ShapeDtypeStruct(hist.shape,...  4.47 us
    unnamed x4, local copies, waits for them, and re-layouts  2.4 us
    ppermute x1, starting transfers between devices, shards(): other = lax.ppermute(send.reshape(256, 16, 128), 'core', [(0, 1), (1, 0)])  1.92 us
  transfers between devices with their start and end apart: 2, of which 1 were waited for; matrix products, arithmetic and copies ran while one was open for 0% of the time, Pallas kernels for 8%

profile of v6, /device:TPU:8, one launch (start us, length us, event | category | flops | bytes accessed | tf_op | source)
XLA Modules:
  0.0 65.0 jit_solution(13107464794039352904)
XLA Ops:
  0.6 8.3 %shard_map.68 = (bf16[4,2,2,4,4,16,128]{6,5,4,3,2,1,0:T(8,128)(2,1)}, bf16[512,384]{1,0:T(8,128)(2,1)}, bf16[384,2048]{1,0:T(8,128)(2,1)}) custom-call(s32[6]{0:T(128)} %bitcast.15, bf16[6,64,512]{2,1,0:T(8,128)(2,1)} %bitcast.10, bf16[6,64,512]{2,1,0:T(8,128)(2,1)} %bitcast.12, bf16[512,2048]{1,0:T(8,128)(2,1)} %win_hbm.3, bf16[512,512]{1,0:T(8,128)(2,1)} %wout_hbm.1), custom_call_target="tpu_custom_call" | custom-call | flops 1811939328 | bytes 8388608 | tf_op jit(solution)/shard_map/pallas_call | solution.py:323
  8.9 1.9 %collective-permute-start = (bf16[256,16,128]{2,1,0:T(8,128)(2,1)}, bf16[256,16,128]{2,1,0:T(8,128)(2,1)S(1)}, u32[]{:S(2)}, u32[]{:S(2)}) collective-permute-start(bf16[256,16,128]{2,1,0:T(8,128)(2,1)} %bitcast.17), channel_id=1, source_target_pairs={{0,1},{1,0},{2,3},{3,2},{4,5},{5,4},{6,7},{7,6},{8,9},{9,8},{10,11... | collective-permute-start | bytes 3145736 | tf_op jit(solution)/shard_map/ppermute | solution.py:436
  10.8 0.0 copy-start
  10.8 1.4 %copy-done = bf16[384,2048]{1,0:T(8,128)(2,1)S(1)} copy-done((bf16[384,2048]{1,0:T(8,128)(2,1)S(1)}, bf16[384,2048]{1,0:T(8,128)(2,1)}, u32[]{:S(2)}) %copy-start) | copy-done | bytes 1572888
  12.2 0.0 copy-start.1
  12.2 1.0 %copy-done.1 = bf16[512,384]{1,0:T(8,128)(2,1)S(1)} copy-done((bf16[512,384]{1,0:T(8,128)(2,1)S(1)}, bf16[512,384]{1,0:T(8,128)(2,1)}, u32[]{:S(2)}) %copy-start.1) | copy-done | bytes 393240
  13.2 0.8 %shard_map.69 = bf16[4,2,2,4,4,16,128]{6,5,4,3,2,1,0:T(8,128)(2,1)S(1)} custom-call(bf16[512,384]{1,0:T(8,128)(2,1)S(1)} %copy-done.1, bf16[384,2048]{1,0:T(8,128)(2,1)S(1)} %copy-done), custom_call_target="tpu_custom_call" | custom-call | flops 402653184 | bytes 3145728 | tf_op jit(solution)/shard_map/pallas_call | solution.py:361
  14.0 0.0 collective-permute-done.other_ref
  14.0 0.3 shard_map.70
  14.3 23.8 %all_to_all.10.parts_ref = bf16[16,16,16,128]{3,2,1,0:T(8,128)(2,1)S(1)} all-to-all(bf16[16,16,16,128]{3,2,1,0:T(8,128)(2,1)S(1)} %bitcast.9), channel_id=1, replica_groups=mesh['yh'=4,'yl'=2,'x'=4,'zh'=4,'zl'=2,'core'=2] {'x','yl','zl'}, dimensions={0} | all-to-all | bytes 2097152 | tf_op jit(solution)/shard_map/all_to_all | solution.py:430
  38.1 0.8 %shard_map.71.after_ref = bf16[16,16,128]{2,1,0:T(8,128)(2,1)} custom-call(bf16[16,16,16,128]{3,2,1,0:T(8,128)(2,1)S(1)} %all_to_all.10.parts_ref), custom_call_target="tpu_custom_call" | custom-call | tf_op jit(solution)/shard_map/pallas_call | solution.py:410
  38.9 12.9 %all-to-all-start.1 = ((bf16[16,1,16,128]{3,2,1,0:T(8,128)(2,1)}), bf16[16,1,16,128]{3,2,1,0:T(8,128)(2,1)S(1)}, u32[]{:S(2)}, u32[]{:S(2)}) async-start(bf16[16,1,16,128]{3,2,1,0:T(8,128)(2,1)} %bitcast.7), calls=%async_computation.1 | async-start | bytes 131072 | tf_op jit(solution)/shard_map/all_to_all | solution.py:430
  51.9 4.5 %shard_map.72 = bf16[6,64,512]{2,1,0:T(8,128)(2,1)} custom-call(s32[6]{0:T(128)} %bitcast.16, bf16[6,64,512]{2,1,0:T(8,128)(2,1)} %bitcast.11, bf16[6,64,512]{2,1,0:T(8,128)(2,1)} %bitcast.13, bf16[512,2048]{1,0:T(8,128)(2,1)} %win_hbm.3, bf16[384,2048]{1,0:T(8,128)(2,1)} %get-tuple-element.5.dpre_ref.dpre_hbm, bf16[16,16,128]{2,1,0:T(8,128)(2,1)} %shard_map.71.after_ref), custom_call_target="tpu_custom_call" | custom-call | flops 805306368 | bytes 6291456 | tf_op jit(solution)/shard_map/pallas_call | solution.py:377
  56.3 8.0 %all-to-all-done.1.parts_ref = bf16[16,1,16,128]{3,2,1,0:T(8,128)(2,1)S(1)} async-done(((bf16[16,1,16,128]{3,2,1,0:T(8,128)(2,1)}), bf16[16,1,16,128]{3,2,1,0:T(8,128)(2,1)S(1)}, u32[]{:S(2)}, u32[]{:S(2)}) %all-to-all-start.1) | async-done | bytes 65568 | tf_op jit(solution)/shard_map/all_to_all | solution.py:430
  64.3 0.7 %shard_map.73 = f32[32,64]{1,0:T(8,128)} custom-call(bf16[16,1,16,128]{3,2,1,0:T(8,128)(2,1)S(1)} %all-to-all-done.1.parts_ref), custom_call_target="tpu_custom_call" | custom-call | tf_op jit(solution)/shard_map/pallas_call | solution.py:420
Async XLA Ops:
  8.9 5.1 %collective-permute-start = (bf16[256,16,128]{2,1,0:T(8,128)(2,1)}, bf16[256,16,128]{2,1,0:T(8,128)(2,1)S(1)}, u32[]{:S(2)}, u32[]{:S(2)}) collective-permute-start(bf16[256,16,128]{2,1,0:T(8,128)(2,1)} %bitcast.17), channel_id=1, source_target_pairs={{0,1},{1,0},{2,3},{3,2},{4,5},{5,4},{6,7},{7,6},{8,9},{9,8},{10,11... | collective-permute-start | bytes 3145736 | tf_op jit(solution)/shard_map/ppermute | solution.py:436
  10.8 1.4 %copy-start = (bf16[384,2048]{1,0:T(8,128)(2,1)S(1)}, bf16[384,2048]{1,0:T(8,128)(2,1)}, u32[]{:S(2)}) copy-start(bf16[384,2048]{1,0:T(8,128)(2,1)} %get-tuple-element.5.dpre_ref.dpre_hbm) | copy-start | bytes 4718596
  12.2 1.0 %copy-start.1 = (bf16[512,384]{1,0:T(8,128)(2,1)S(1)}, bf16[512,384]{1,0:T(8,128)(2,1)}, u32[]{:S(2)}) copy-start(bf16[512,384]{1,0:T(8,128)(2,1)} %get-tuple-element.6.turned_ref) | copy-start | bytes 1179652
  38.9 25.4 %all-to-all-start.1 = ((bf16[16,1,16,128]{3,2,1,0:T(8,128)(2,1)}), bf16[16,1,16,128]{3,2,1,0:T(8,128)(2,1)S(1)}, u32[]{:S(2)}, u32[]{:S(2)}) async-start(bf16[16,1,16,128]{3,2,1,0:T(8,128)(2,1)} %bitcast.7), calls=%async_computation.1 | async-start | bytes 131072 | tf_op jit(solution)/shard_map/all_to_all | solution.py:430

commit v7 on v6

--- a/solution.py
+++ b/solution.py
@@ -43,16 +43,14 @@
     win_hbm,
     wout_hbm,
     send_hbm,
-    turned_hbm,
-    dpre_hbm,
+    both_hbm,
     tiles_ref,
-    dpre_ref,
+    both_ref,
     hist_ref,
     cot_ref,
     win_ref,
     wout_ref,
     normed_ref,
-    turned_ref,
     seed_ref,
     proj_ref,
     slope_ref,
@@ -68,6 +66,8 @@
     slots, positions, features = hist_ref.shape
     pairs = features // 128
     half = positions
+    rows = slots * positions
+    dpre_ref = both_ref.at[:rows]
 
     started = []
 
@@ -91,8 +91,10 @@
     turned = normed_ref[...].T
     for r in range(16):
         place = (r % 2) * 8 + r // 2
-        turned_ref[place * 32 : (place + 1) * 32, :] = turned[r * 32 : (r + 1) * 32, :]
-    turned_copy = pltpu.make_async_copy(turned_ref, turned_hbm, sent.at[32])
+        at, column = rows + place % 4 * 32, place // 4 * rows
+        both_ref[at : at + 32, column : column + rows] = turned[r * 32 : (r + 1) * 32, :]
+    below = (slice(rows, rows + 128), slice(0, 4 * rows))
+    turned_copy = pltpu.make_async_copy(both_ref.at[below], both_hbm.at[below], sent.at[32])
     turned_copy.start()
 
     for copy in win_copies:
@@ -184,9 +186,9 @@
     copies = [turned_copy]
 
     def send_on(first_column, end_column):
-        part = (slice(None), slice(first_column, end_column))
+        part = (slice(0, rows), slice(first_column, end_column))
         copy = pltpu.make_async_copy(
-            dpre_ref.at[part], dpre_hbm.at[part], sent.at[32 + len(copies)]
+            both_ref.at[part], both_hbm.at[part], sent.at[32 + len(copies)]
         )
         copy.start()
         copies.append(copy)
@@ -201,7 +203,7 @@
 
     other = 1 - lax.axis_index("core")
     for y in range(8):
-        half_tiles(other, y, turned_ref, dpre_ref, tiles_ref)
+        half_tiles(other, y, both_ref, tiles_ref)
         for x in range(4):
             part = (x, y % 2, slice(None), y // 2)
             copy = pltpu.make_async_copy(
@@ -213,11 +215,17 @@
         copy.wait()
 
 
-def half_tiles(core, y, turned_ref, dpre_ref, tiles_ref):
-    rows = turned_ref.shape[0] // 2
-    mine = pl.ds(pl.multiple_of(core * rows, rows), rows)
+def half_tiles(core, y, both_ref, tiles_ref):
+    rows = both_ref.shape[0] - 128
     left = lax.broadcasted_iota(jnp.int32, (16, 128), 1) < 64
-    block = dot(turned_ref[mine, :], dpre_ref[:, y * 256 : (y + 1) * 256])
+    turned = jnp.concatenate(
+        [
+            both_ref[rows:, pl.ds(pl.multiple_of((2 * core + k) * rows, rows), rows)]
+            for k in range(2)
+        ],
+        0,
+    )
+    block = dot(turned, both_ref[:rows, y * 256 : (y + 1) * 256])
     for pair in range(2):
         part = block[:, pair * 128 : (pair + 1) * 128]
         swapped = pltpu.roll(part, 64, 1)
@@ -230,9 +238,9 @@
                 tiles_ref[x, y % 2, z % 2, y // 2, z // 2] = tile.astype(BF16)
 
 
-def keep_kernel(turned_ref, dpre_ref, tiles_ref):
+def keep_kernel(both_ref, tiles_ref):
     for y in range(8):
-        half_tiles(lax.axis_index("core"), y, turned_ref, dpre_ref, tiles_ref)
+        half_tiles(lax.axis_index("core"), y, both_ref, tiles_ref)
 
 
 def history_kernel(
@@ -240,7 +248,7 @@
     hist_hbm,
     cot_hbm,
     win_hbm,
-    dpre_hbm,
+    both_hbm,
     after_ref,
     out_ref,
     hist_ref,
@@ -259,7 +267,7 @@
 
     parts = [slice(j * features, (j + 1) * features) for j in range(4)]
     for part in parts:
-        fetch(dpre_hbm.at[:, part], dpre_ref.at[:, part])
+        fetch(both_hbm.at[: slots * positions, part], dpre_ref.at[:, part])
         fetch(win_hbm.at[:, part], win_ref.at[:, part])
     fetch(hist_hbm, hist_ref)
     fetch(cot_hbm, cot_ref)
@@ -324,20 +332,18 @@
         weight_kernel,
         out_shape=(
             jax.ShapeDtypeStruct(TILES, BF16),
-            jax.ShapeDtypeStruct((features, rows), BF16),
-            jax.ShapeDtypeStruct((rows, 4 * features), BF16),
+            jax.ShapeDtypeStruct((rows + 128, 4 * features), BF16),
         ),
         in_specs=[SMEM, HBM, HBM, HBM, HBM],
-        out_specs=(HBM, HBM, HBM),
+        out_specs=(HBM, HBM),
         scratch_shapes=[
             pltpu.VMEM(TILES, BF16),
-            pltpu.VMEM((rows, 4 * features), BF16),
+            pltpu.VMEM((rows + 128, 4 * features), BF16),
             pltpu.VMEM(hist.shape, BF16),
             pltpu.VMEM(hist.shape, BF16),
             pltpu.VMEM(w_in.shape, BF16),
             pltpu.VMEM(w_out.shape, BF16),
             pltpu.VMEM((rows, features), BF16),
-            pltpu.VMEM((features, rows), BF16),
             pltpu.VMEM((rows, features), BF16),
             pltpu.VMEM((rows, 4 * features), BF16),
             pltpu.VMEM((rows, 4 * features), F32),
@@ -357,23 +363,23 @@
     )(lengths, hist, cot, w_in, w_out)
 
 
-def kept_tiles(turned, dpre):
+def kept_tiles(both):
     return pl.pallas_call(
         keep_kernel,
         out_shape=jax.ShapeDtypeStruct(TILES, BF16),
-        in_specs=[VMEM, VMEM],
+        in_specs=[VMEM],
         out_specs=VMEM,
         compiler_params=pltpu.CompilerParams(vmem_limit_bytes=12 * 2**20),
         cost_estimate=pl.CostEstimate(
-            flops=turned.shape[0] * dpre.shape[0] * dpre.shape[1],
+            flops=both.shape[0] * both.shape[1] * 512,
             bytes_accessed=3 * 2**20,
             transcendentals=0,
         ),
-    )(turned, dpre)
-
-
-def history_grads(lengths, hist, cot, w_in, dpre, after):
-    rows = dpre.shape[0]
+    )(both)
+
+
+def history_grads(lengths, hist, cot, w_in, both, after):
+    rows = hist.shape[0] * hist.shape[1]
     return pl.pallas_call(
         history_kernel,
         out_shape=jax.ShapeDtypeStruct(hist.shape, BF16),
@@ -383,17 +389,17 @@
             pltpu.VMEM(hist.shape, BF16),
             pltpu.VMEM(hist.shape, BF16),
             pltpu.VMEM(w_in.shape, BF16),
-            pltpu.VMEM(dpre.shape, BF16),
+            pltpu.VMEM((rows, w_in.shape[1]), BF16),
             pltpu.VMEM((rows, hist.shape[-1]), F32),
             pltpu.SemaphoreType.DMA((10,)),
         ],
         compiler_params=pltpu.CompilerParams(vmem_limit_bytes=56 * 2**20),
         cost_estimate=pl.CostEstimate(
-            flops=2 * rows * dpre.shape[1] * hist.shape[-1],
+            flops=2 * rows * w_in.shape[1] * hist.shape[-1],
             bytes_accessed=6 * 2**20,
             transcendentals=1000,
         ),
-    )(lengths, hist, cot, w_in, dpre, after)
+    )(lengths, hist, cot, w_in, both, after)
 
 
 def pair_sum(one, other):
@@ -432,12 +438,12 @@
 
 def shards(histories, cotangents, lengths, w_in, w_out):
     hist, cot, slot_lengths = histories[0, 0], cotangents[0, 0], lengths[0, 0]
-    send, turned, dpre = weight_tiles(slot_lengths, hist, cot, w_in, w_out)
+    send, both = weight_tiles(slot_lengths, hist, cot, w_in, w_out)
     other = lax.ppermute(send.reshape(256, 16, 128), "core", [(0, 1), (1, 0)])
-    keep = kept_tiles(turned, dpre)
+    keep = kept_tiles(both)
     tiles = pair_sum(keep.reshape(256, 16, 128), other)
     tiles = summed(exchanged(tiles.reshape(16, 16, 16, 128), ("x", "yl", "zl")))
-    grads = history_grads(slot_lengths, hist, cot, w_in, dpre, tiles)
+    grads = history_grads(slot_lengths, hist, cot, w_in, both, tiles)
     block = last_sum(exchanged(tiles.reshape(16, 1, 16, 128), ("yh", "zh")))
     return (grads[None, None], block)
 

time: 65.3 us -> 64.5 us (0.988)
  local copies, waits for them, and re-layouts: 2.4 us -> 1.58 us
    unnamed x4 -> x2, local copies, waits for them, and re-layouts: 2.4 us -> 1.58 us
  transfers between devices with their start and end apart: 2 -> 2, of which waited for: 1 -> 2; matrix products, arithmetic and copies ran while one was open for 0% -> 0% of each run, Pallas kernels for 8% -> 8%
where the time goes in v7:
time: 64.5 us; the launch traced here: 64.2 us
  blocking collectives  23.7 us (37%)
  Pallas kernels  15.3 us (24%)
  starting transfers between devices  14.5 us (22%)
  waiting for transfers between devices  8.42 us (13%)
  local copies, waits for them, and re-layouts  1.58 us (2%)
  between operations  0.69 us (1%)
    all_to_all x1, blocking collectives, exchanged(): return lax.all_to_all(tiles, axes, 0, 0, tiled=True)  23.7 us
    all_to_all x1, starting transfers between devices, exchanged(): return lax.all_to_all(tiles, axes, 0, 0, tiled=True)  12.6 us
    pallas_call x1, Pallas kernels, weight_tiles(): pl.pallas_call(weight_kernel, out_shape=(jax.ShapeDtypeStruct(TILES, BF16...  8.29 us
    all_to_all x1, waiting for transfers between devices, exchanged(): return lax.all_to_all(tiles, axes, 0, 0, tiled=True)  7.97 us
    pallas_call x1, Pallas kernels, history_grads(): pl.pallas_call(history_kernel, out_shape=jax.ShapeDtypeStruct(hist.shape,...  4.45 us
    ppermute x1, starting transfers between devices, shards(): other = lax.ppermute(send.reshape(256, 16, 128), 'core', [(0, 1), (1, 0)])  1.92 us
    unnamed x2, local copies, waits for them, and re-layouts  1.58 us
  transfers between devices with their start and end apart: 2, of which 2 were waited for; matrix products, arithmetic and copies ran while one was open for 0% of the time, Pallas kernels for 8%

profile of v7, /device:TPU:8, one launch (start us, length us, event | category | flops | bytes accessed | tf_op | source)
XLA Modules:
  0.0 64.2 jit_solution(5708081075647900693)
XLA Ops:
  0.6 8.3 %shard_map.68 = (bf16[4,2,2,4,4,16,128]{6,5,4,3,2,1,0:T(8,128)(2,1)}, bf16[512,2048]{1,0:T(8,128)(2,1)}) custom-call(s32[6]{0:T(128)} %bitcast.15, bf16[6,64,512]{2,1,0:T(8,128)(2,1)} %bitcast.10, bf16[6,64,512]{2,1,0:T(8,128)(2,1)} %bitcast.12, bf16[512,2048]{1,0:T(8,128)(2,1)} %win_hbm.3, bf16[512,512]{1,0:T(8,128)(2,1)} %wout_hbm.1), custom_call_target="tpu_custom_call" | custom-call | flops 1811939328 | bytes 8388608 | tf_op jit(solution)/shard_map/pallas_call | solution.py:331
  8.9 1.9 %collective-permute-start = (bf16[256,16,128]{2,1,0:T(8,128)(2,1)}, bf16[256,16,128]{2,1,0:T(8,128)(2,1)S(1)}, u32[]{:S(2)}, u32[]{:S(2)}) collective-permute-start(bf16[256,16,128]{2,1,0:T(8,128)(2,1)} %bitcast.17), channel_id=1, source_target_pairs={{0,1},{1,0},{2,3},{3,2},{4,5},{5,4},{6,7},{7,6},{8,9},{9,8},{10,11... | collective-permute-start | bytes 3145736 | tf_op jit(solution)/shard_map/ppermute | solution.py:442
  10.9 0.0 copy-start
  10.9 1.6 %copy-done = bf16[512,2048]{1,0:T(8,128)(2,1)S(1)} copy-done((bf16[512,2048]{1,0:T(8,128)(2,1)S(1)}, bf16[512,2048]{1,0:T(8,128)(2,1)}, u32[]{:S(2)}) %copy-start) | copy-done | bytes 2097176
  12.5 0.8 %shard_map.69 = bf16[4,2,2,4,4,16,128]{6,5,4,3,2,1,0:T(8,128)(2,1)S(1)} custom-call(bf16[512,2048]{1,0:T(8,128)(2,1)S(1)} %copy-done), custom_call_target="tpu_custom_call" | custom-call | flops 536870912 | bytes 3145728 | tf_op jit(solution)/shard_map/pallas_call | solution.py:367
  13.2 0.4 collective-permute-done.other_ref
  13.7 0.3 shard_map.70
  14.0 23.7 %all_to_all.10.parts_ref = bf16[16,16,16,128]{3,2,1,0:T(8,128)(2,1)S(1)} all-to-all(bf16[16,16,16,128]{3,2,1,0:T(8,128)(2,1)S(1)} %bitcast.9), channel_id=1, replica_groups=mesh['yh'=4,'yl'=2,'x'=4,'zh'=4,'zl'=2,'core'=2] {'x','yl','zl'}, dimensions={0} | all-to-all | bytes 2097152 | tf_op jit(solution)/shard_map/all_to_all | solution.py:436
  37.7 0.8 %shard_map.71.after_ref = bf16[16,16,128]{2,1,0:T(8,128)(2,1)} custom-call(bf16[16,16,16,128]{3,2,1,0:T(8,128)(2,1)S(1)} %all_to_all.10.parts_ref), custom_call_target="tpu_custom_call" | custom-call | tf_op jit(solution)/shard_map/pallas_call | solution.py:416
  38.5 12.6 %all-to-all-start.1 = ((bf16[16,1,16,128]{3,2,1,0:T(8,128)(2,1)}), bf16[16,1,16,128]{3,2,1,0:T(8,128)(2,1)S(1)}, u32[]{:S(2)}, u32[]{:S(2)}) async-start(bf16[16,1,16,128]{3,2,1,0:T(8,128)(2,1)} %bitcast.7), calls=%async_computation.1 | async-start | bytes 131072 | tf_op jit(solution)/shard_map/all_to_all | solution.py:436
  51.1 4.5 %shard_map.72 = bf16[6,64,512]{2,1,0:T(8,128)(2,1)} custom-call(s32[6]{0:T(128)} %bitcast.16, bf16[6,64,512]{2,1,0:T(8,128)(2,1)} %bitcast.11, bf16[6,64,512]{2,1,0:T(8,128)(2,1)} %bitcast.13, bf16[512,2048]{1,0:T(8,128)(2,1)} %win_hbm.3, bf16[512,2048]{1,0:T(8,128)(2,1)} %get-tuple-element.4.both_ref.both_hbm, bf16[16,16,128]{2,1,0:T(8,128)(2,1)} %shard_map.71.after_ref), custom_call_target="tpu_custom_call" | custom-call | flops 805306368 | bytes 6291456 | tf_op jit(solution)/shard_map/pallas_call | solution.py:383
  55.6 8.0 %all-to-all-done.1.parts_ref = bf16[16,1,16,128]{3,2,1,0:T(8,128)(2,1)S(1)} async-done(((bf16[16,1,16,128]{3,2,1,0:T(8,128)(2,1)}), bf16[16,1,16,128]{3,2,1,0:T(8,128)(2,1)S(1)}, u32[]{:S(2)}, u32[]{:S(2)}) %all-to-all-start.1) | async-done | bytes 65568 | tf_op jit(solution)/shard_map/all_to_all | solution.py:436
  63.5 0.7 %shard_map.73 = f32[32,64]{1,0:T(8,128)} custom-call(bf16[16,1,16,128]{3,2,1,0:T(8,128)(2,1)S(1)} %all-to-all-done.1.parts_ref), custom_call_target="tpu_custom_call" | custom-call | tf_op jit(solution)/shard_map/pallas_call | solution.py:426
Async XLA Ops:
  8.9 4.8 %collective-permute-start = (bf16[256,16,128]{2,1,0:T(8,128)(2,1)}, bf16[256,16,128]{2,1,0:T(8,128)(2,1)S(1)}, u32[]{:S(2)}, u32[]{:S(2)}) collective-permute-start(bf16[256,16,128]{2,1,0:T(8,128)(2,1)} %bitcast.17), channel_id=1, source_target_pairs={{0,1},{1,0},{2,3},{3,2},{4,5},{5,4},{6,7},{7,6},{8,9},{9,8},{10,11... | collective-permute-start | bytes 3145736 | tf_op jit(solution)/shard_map/ppermute | solution.py:442
  10.9 1.6 %copy-start = (bf16[512,2048]{1,0:T(8,128)(2,1)S(1)}, bf16[512,2048]{1,0:T(8,128)(2,1)}, u32[]{:S(2)}) copy-start(bf16[512,2048]{1,0:T(8,128)(2,1)} %get-tuple-element.4.both_ref.both_hbm) | copy-start | bytes 6291460
  38.5 25.0 %all-to-all-start.1 = ((bf16[16,1,16,128]{3,2,1,0:T(8,128)(2,1)}), bf16[16,1,16,128]{3,2,1,0:T(8,128)(2,1)S(1)}, u32[]{:S(2)}, u32[]{:S(2)}) async-start(bf16[16,1,16,128]{3,2,1,0:T(8,128)(2,1)} %bitcast.7), calls=%async_computation.1 | async-start | bytes 131072 | tf_op jit(solution)/shard_map/all_to_all | solution.py:436

commit v8 on v7

v8 whole, which is shorter than its diff:
```python
import jax
import jax.numpy as jnp
from jax import lax
from jax.experimental import pallas as pl
from jax.experimental.pallas import tpu as pltpu
from jax.sharding import Mesh
from jax.sharding import PartitionSpec as P

HEADS = 8
EPS = 1e-06
LIGHT = 4
AXES = ("yh", "yl", "x", "zh", "zl", "core")
F32 = jnp.float32
BF16 = jnp.bfloat16


def dot(a, b, contract=((1,), (0,))):
    return lax.dot_general(a, b, (contract, ((), ())), preferred_element_type=F32)


def sigmoid(values):
    return 0.5 * jnp.tanh(0.5 * values) + 0.5


def normalised(values):
    average = jnp.mean(values, axis=-1, keepdims=True)
    centered = values - average
    spread = jnp.mean(centered * centered, axis=-1, keepdims=True)
    scale = lax.rsqrt(spread + EPS)
    return centered * scale, scale


def norm_backward(grad, normed, scale):
    first = jnp.mean(grad, axis=-1, keepdims=True)
    second = jnp.mean(grad * normed, axis=-1, keepdims=True)
    return scale * (grad - first - normed * second)


def slot_order(length_ref, slots):
    live = [jnp.where(length_ref[i] > 0, 1, 0) for i in range(slots)]
    count = sum(live)
    ahead, behind, places = 0, count, []
    for i in range(slots):
        places.append(jnp.where(live[i] > 0, ahead, behind))
        ahead, behind = ahead + live[i], behind + 1 - live[i]
    order = [sum(jnp.where(places[i] == n, i, 0) for i in range(slots)) for n in range(slots)]
    return count, places, order


def weight_kernel(
    length_ref,
    hist_hbm,
    cot_hbm,
    win_hbm,
    wout_hbm,
    send_hbm,
    both_hbm,
    tiles_ref,
    both_ref,
    hist_ref,
    cot_ref,
    win_ref,
    wout_ref,
    normed_ref,
    seed_ref,
    proj_ref,
    slope_ref,
    mixed_ref,
    dgated_ref,
    scores_ref,
    weights_ref,
    dmixed_ref,
    dscores_ref,
    sorted_ref,
    arrived,
    sent,
):
    every, positions, features = hist_ref.shape
    pairs = features // 128
    half = positions
    live, _, order = slot_order(length_ref, every)

    def work(slots):
        rows = slots * positions
        dpre_ref = both_ref.at[:rows]
        for i in range(slots):
            sorted_ref[i] = length_ref[order[i] if slots < every else i]
        started = []

        def fetch(source, target):
            copy = pltpu.make_async_copy(source, target, arrived.at[len(started)])
            copy.start()
            started.append(copy)
            return copy

        if slots < every:
            hist_copies = [fetch(hist_hbm.at[order[i]], hist_ref.at[i]) for i in range(slots)]
        else:
            hist_copies = [fetch(hist_hbm, hist_ref)]
        width = 256
        quarters = [slice(j * features // 4, (j + 1) * features // 4) for j in range(4)]
        win_copies = [fetch(win_hbm.at[part, :], win_ref.at[part, :]) for part in quarters]
        if slots < every:
            cot_copies = [fetch(cot_hbm.at[order[i]], cot_ref.at[i]) for i in range(slots)]
        else:
            cot_copies = [fetch(cot_hbm, cot_ref)]
        wout_copy = fetch(wout_hbm, wout_ref)

        for copy in hist_copies:
            copy.wait()
        for i in range(slots):
            normed, _ = normalised(hist_ref[i].astype(F32))
            normed_ref[i * positions : (i + 1) * positions, :] = normed.astype(BF16)
        turned = normed_ref[:rows, :].T
        for r in range(16):
            place = (r % 2) * 8 + r // 2
            at, column = every * positions + place % 4 * 32, place // 4 * every * positions
            both_ref[at : at + 32, column : column + rows] = turned[r * 32 : (r + 1) * 32, :]
        total = every * positions
        below = (slice(total, total + 128), slice(0, 4 * total))
        turned_copy = pltpu.make_async_copy(both_ref.at[below], both_hbm.at[below], sent.at[32])
        turned_copy.start()

        for copy in win_copies:
            copy.wait()
        for j in range(4 * features // width):
            columns = slice(j * width, (j + 1) * width)
            pre = dot(normed_ref[:rows, :], win_ref[:, columns])
            gate = sigmoid(pre)
            value = pre * gate
            proj_ref[:rows, columns] = value.astype(BF16)
            slope_ref[:rows, columns] = gate + value * (1.0 - gate)
        for copy in cot_copies:
            copy.wait()
        row = lax.broadcasted_iota(jnp.int32, (positions, features), 0)
        for i in range(slots):
            seed = jnp.where(row < sorted_ref[i], cot_ref[i].astype(F32), 0.0)
            seed_ref[i * positions : (i + 1) * positions, :] = seed.astype(BF16)
        wout_copy.wait()
        dgated = dot(seed_ref[:rows, :], wout_ref[...], ((1,), (1,)))
        dgated_ref[:rows, :] = dgated.astype(BF16)

        lane = lax.broadcasted_iota(jnp.int32, (positions, 128), 1)
        first = lane < half
        early = jnp.where(first, 1.0, 0.0).astype(BF16)
        late = jnp.where(first, 0.0, 1.0).astype(BF16)

        def spread(block):
            return jnp.concatenate([block * early, block * late], 0)

        def blocks(p):
            return [slice(b * features + p * 128, b * features + (p + 1) * 128) for b in range(4)]

        def for_slots(body):
            def step(i, carry):
                body(i, pl.ds(pl.multiple_of(i * positions, positions), positions))
                return carry

            lax.fori_loop(0, slots, step, 0, unroll=slots)

        def score(i, at):
            for p in range(pairs):
                _, _, q_at, k_at = blocks(p)
                scores_ref[at, blocks(p)[0]] = dot(
                    proj_ref[at, q_at], spread(proj_ref[at, k_at]), ((1,), (1,))
                )

        def weigh(i, at):
            length = sorted_ref[i]
            inverse = 1.0 / jnp.maximum(length, 1).astype(F32)
            source = lax.broadcasted_iota(jnp.int32, (positions, features), 1) % half
            time = lax.broadcasted_iota(jnp.int32, (positions, features), 0)
            allowed = (source <= time) & (source < length)
            scores = scores_ref[at, :] * 0.125
            gate = sigmoid(scores)
            value = scores * gate
            weights_ref[at, :] = jnp.where(allowed, value * inverse, 0.0).astype(BF16)
            slopes = (gate + value * (1.0 - gate)) * (inverse * 0.125)
            scores_ref[at, :] = jnp.where(allowed, slopes, 0.0)

        def mix(i, at):
            for p in range(pairs):
                here, v_at, _, _ = blocks(p)
                mixed_ref[at, here] = dot(weights_ref[at, here], spread(proj_ref[at, v_at]))

        def turn(i, at):
            normed, scale = normalised(mixed_ref[at, :])
            dgated = dgated_ref[at, :].astype(F32)
            dpre_ref[at, :features] = (dgated * normed * slope_ref[at, :features]).astype(BF16)
            dmixed = norm_backward(dgated * proj_ref[at, :features].astype(F32), normed, scale)
            dmixed_ref[at, :] = dmixed.astype(BF16)

        def value_back(i, at):
            for p in range(pairs):
                here, v_at, _, _ = blocks(p)
                down = dmixed_ref[at, here]
                dweights = dot(down, spread(proj_ref[at, v_at]), ((1,), (1,)))
                dscores_ref[at, here] = (dweights * scores_ref[at, here]).astype(BF16)
                dv = dot(weights_ref[at, here], down, ((0,), (0,)))
                dv = jnp.where(first, dv[:half], dv[half:])
                dpre_ref[at, v_at] = (dv * slope_ref[at, v_at]).astype(BF16)

        def score_back(i, at):
            for p in range(pairs):
                here, _, q_at, k_at = blocks(p)
                dq = dot(dscores_ref[at, here], spread(proj_ref[at, k_at]))
                dk = dot(dscores_ref[at, here], proj_ref[at, q_at], ((0,), (0,)))
                dk = jnp.where(first, dk[:half], dk[half:])
                dpre_ref[at, q_at] = (dq * slope_ref[at, q_at]).astype(BF16)
                dpre_ref[at, k_at] = (dk * slope_ref[at, k_at]).astype(BF16)

        copies = [turned_copy]

        def send_on(first_column, end_column):
            part = (slice(0, rows), slice(first_column, end_column))
            copy = pltpu.make_async_copy(
                both_ref.at[part], both_hbm.at[part], sent.at[32 + len(copies)]
            )
            copy.start()
            copies.append(copy)

        for body in (score, weigh, mix, turn):
            for_slots(body)
        send_on(0, features)
        for_slots(value_back)
        send_on(features, 2 * features)
        for_slots(score_back)
        send_on(2 * features, 4 * features)

        other = 1 - lax.axis_index("core")
        for y in range(8):
            half_tiles(other, y, both_ref, tiles_ref, rows)
            for x in range(4):
                part = (x, y % 2, slice(None), y // 2)
                copy = pltpu.make_async_copy(
                    tiles_ref.at[part], send_hbm.at[part], sent.at[y * 4 + x]
                )
                copy.start()
                copies.append(copy)
        for copy in copies:
            copy.wait()

    @pl.when(live <= LIGHT)
    def _():
        work(LIGHT)

    @pl.when(live > LIGHT)
    def _():
        work(every)


def half_tiles(core, y, both_ref, tiles_ref, rows):
    total = both_ref.shape[0] - 128
    left = lax.broadcasted_iota(jnp.int32, (16, 128), 1) < 64
    turned = jnp.concatenate(
        [
            both_ref[total:, pl.ds(pl.multiple_of((2 * core + k) * total, total), rows)]
            for k in range(2)
        ],
        0,
    )
    block = dot(turned, both_ref[:rows, y * 256 : (y + 1) * 256])
    for pair in range(2):
        part = block[:, pair * 128 : (pair + 1) * 128]
        swapped = pltpu.roll(part, 64, 1)
        for z in range(8):
            upper = slice(z * 32, z * 32 + 16)
            lower = slice(z * 32 + 16, z * 32 + 32)
            even = jnp.where(left, part[upper], swapped[lower])
            odd = jnp.where(left, swapped[upper], part[lower])
            for x, tile in ((2 * pair, even), (2 * pair + 1, odd)):
                tiles_ref[x, y % 2, z % 2, y // 2, z // 2] = tile.astype(BF16)


def keep_kernel(length_ref, both_ref, tiles_ref):
    live, _, _ = slot_order(length_ref, length_ref.shape[0])

    def work(rows):
        for y in range(8):
            half_tiles(lax.axis_index("core"), y, both_ref, tiles_ref, rows)

    @pl.when(live <= LIGHT)
    def _():
        work(LIGHT * 64)

    @pl.when(live > LIGHT)
    def _():
        work(both_ref.shape[0] - 128)


def history_kernel(
    length_ref,
    hist_hbm,
    cot_hbm,
    win_hbm,
    both_hbm,
    after_ref,
    out_ref,
    hist_ref,
    cot_ref,
    win_ref,
    dpre_ref,
    grad_ref,
    arrived,
):
    slots, positions, features = hist_ref.shape
    copies = []

    def fetch(source, target):
        copies.append(pltpu.make_async_copy(source, target, arrived.at[len(copies)]))
        copies[-1].start()

    parts = [slice(j * features, (j + 1) * features) for j in range(4)]
    for part in parts:
        fetch(both_hbm.at[: slots * positions, part], dpre_ref.at[:, part])
        fetch(win_hbm.at[:, part], win_ref.at[:, part])
    fetch(hist_hbm, hist_ref)
    fetch(cot_hbm, cot_ref)
    for j, part in enumerate(parts):
        copies[2 * j].wait()
        copies[2 * j + 1].wait()
        share = dot(dpre_ref[:, part], win_ref[:, part], ((1,), (1,)))
        grad_ref[...] = share if j == 0 else grad_ref[...] + share
    copies[-2].wait()
    copies[-1].wait()

    live, places, _ = slot_order(length_ref, slots)
    for i in range(slots):
        place = jnp.where(live <= LIGHT, jnp.minimum(places[i], LIGHT - 1), i)
        at = pl.ds(pl.multiple_of(place * positions, positions), positions)
        normed, scale = normalised(hist_ref[i].astype(F32))
        row = lax.broadcasted_iota(jnp.int32, (positions, features), 0)
        seed = jnp.where(row < length_ref[i], cot_ref[i].astype(F32), 0.0)
        total = seed + norm_backward(grad_ref[at, :], normed, scale)
        out_ref[i] = jnp.where(length_ref[i] > 0, total, 0.0).astype(BF16)


def pair_kernel(one_ref, other_ref, out_ref):
    step = 16

    def add(i, carry):
        at = pl.ds(i * step, step)
        out_ref[at] = (one_ref[at].astype(F32) + other_ref[at].astype(F32)).astype(BF16)
        return carry

    lax.fori_loop(0, out_ref.shape[0] // step, add, 0)


def sum_kernel(parts_ref, out_ref):
    parts, count = parts_ref.shape[:2]
    for i in range(count):
        total = parts_ref[0, i].astype(F32)
        for p in range(1, parts):
            total += parts_ref[p, i].astype(F32)
        out_ref[i] = total.astype(BF16)


def last_kernel(parts_ref, out_ref):
    total = parts_ref[0, 0].astype(F32)
    for p in range(1, parts_ref.shape[0]):
        total += parts_ref[p, 0].astype(F32)
    out_ref[:16, :] = total[:, :64]
    out_ref[16:, :] = total[:, 64:]


VMEM = pl.BlockSpec(memory_space=pltpu.VMEM)
SMEM = pl.BlockSpec(memory_space=pltpu.SMEM)
HBM = pl.BlockSpec(memory_space=pltpu.HBM)
TILES = (4, 2, 2, 4, 4, 16, 128)
ANY = pl.BlockSpec(memory_space=pl.ANY)


def weight_tiles(lengths, hist, cot, w_in, w_out):
    slots, positions, features = hist.shape
    rows = slots * positions
    return pl.pallas_call(
        weight_kernel,
        out_shape=(
            jax.ShapeDtypeStruct(TILES, BF16),
            jax.ShapeDtypeStruct((rows + 128, 4 * features), BF16),
        ),
        in_specs=[SMEM, HBM, HBM, HBM, HBM],
        out_specs=(HBM, HBM),
        scratch_shapes=[
            pltpu.VMEM(TILES, BF16),
            pltpu.VMEM((rows + 128, 4 * features), BF16),
            pltpu.VMEM(hist.shape, BF16),
            pltpu.VMEM(hist.shape, BF16),
            pltpu.VMEM(w_in.shape, BF16),
            pltpu.VMEM(w_out.shape, BF16),
            pltpu.VMEM((rows, features), BF16),
            pltpu.VMEM((rows, features), BF16),
            pltpu.VMEM((rows, 4 * features), BF16),
            pltpu.VMEM((rows, 4 * features), F32),
            pltpu.VMEM((rows, features), F32),
            pltpu.VMEM((rows, features), BF16),
            pltpu.VMEM((rows, features), F32),
            pltpu.VMEM((rows, features), BF16),
            pltpu.VMEM((rows, features), BF16),
            pltpu.VMEM((rows, features), BF16),
            pltpu.SMEM((hist.shape[0],), jnp.int32),
            pltpu.SemaphoreType.DMA((17,)),
            pltpu.SemaphoreType.DMA((36,)),
        ],
        compiler_params=pltpu.CompilerParams(vmem_limit_bytes=56 * 2**20),
        cost_estimate=pl.CostEstimate(
            flops=2 * rows * features * features * 9, bytes_accessed=8 * 2**20, transcendentals=10**6
        ),
    )(lengths, hist, cot, w_in, w_out)


def kept_tiles(lengths, both):
    return pl.pallas_call(
        keep_kernel,
        out_shape=jax.ShapeDtypeStruct(TILES, BF16),
        in_specs=[SMEM, VMEM],
        out_specs=VMEM,
        compiler_params=pltpu.CompilerParams(vmem_limit_bytes=12 * 2**20),
        cost_estimate=pl.CostEstimate(
            flops=both.shape[0] * both.shape[1] * 512,
            bytes_accessed=3 * 2**20,
            transcendentals=0,
        ),
    )(lengths, both)


def history_grads(lengths, hist, cot, w_in, both, after):
    rows = hist.shape[0] * hist.shape[1]
    return pl.pallas_call(
        history_kernel,
        out_shape=jax.ShapeDtypeStruct(hist.shape, BF16),
        in_specs=[SMEM, HBM, HBM, HBM, HBM, ANY],
        out_specs=VMEM,
        scratch_shapes=[
            pltpu.VMEM(hist.shape, BF16),
            pltpu.VMEM(hist.shape, BF16),
            pltpu.VMEM(w_in.shape, BF16),
            pltpu.VMEM((rows, w_in.shape[1]), BF16),
            pltpu.VMEM((rows, hist.shape[-1]), F32),
            pltpu.SemaphoreType.DMA((10,)),
        ],
        compiler_params=pltpu.CompilerParams(vmem_limit_bytes=56 * 2**20),
        cost_estimate=pl.CostEstimate(
            flops=2 * rows * w_in.shape[1] * hist.shape[-1],
            bytes_accessed=6 * 2**20,
            transcendentals=1000,
        ),
    )(lengths, hist, cot, w_in, both, after)


def pair_sum(one, other):
    return pl.pallas_call(
        pair_kernel,
        out_shape=jax.ShapeDtypeStruct(one.shape, BF16),
        in_specs=[VMEM, VMEM],
        out_specs=VMEM,
        compiler_params=pltpu.CompilerParams(vmem_limit_bytes=8 * 2**20),
    )(one, other)


def summed(parts):
    return pl.pallas_call(
        sum_kernel,
        out_shape=jax.ShapeDtypeStruct(parts.shape[1:], BF16),
        in_specs=[VMEM],
        out_specs=VMEM,
        compiler_params=pltpu.CompilerParams(vmem_limit_bytes=8 * 2**20),
    )(parts)


def last_sum(parts):
    return pl.pallas_call(
        last_kernel,
        out_shape=jax.ShapeDtypeStruct((32, 64), F32),
        in_specs=[VMEM],
        out_specs=VMEM,
        compiler_params=pltpu.CompilerParams(vmem_limit_bytes=2 * 2**20),
    )(parts)


def exchanged(tiles, axes):
    return lax.all_to_all(tiles, axes, 0, 0, tiled=True)


def shards(histories, cotangents, lengths, w_in, w_out):
    hist, cot, slot_lengths = histories[0, 0], cotangents[0, 0], lengths[0, 0]
    send, both = weight_tiles(slot_lengths, hist, cot, w_in, w_out)
    other = lax.ppermute(send.reshape(256, 16, 128), "core", [(0, 1), (1, 0)])
    keep = kept_tiles(slot_lengths, both)
    tiles = pair_sum(keep.reshape(256, 16, 128), other)
    tiles = summed(exchanged(tiles.reshape(16, 16, 16, 128), ("x", "yl", "zl")))
    grads = history_grads(slot_lengths, hist, cot, w_in, both, tiles)
    block = last_sum(exchanged(tiles.reshape(16, 1, 16, 128), ("yh", "zh")))
    return (grads[None, None], block)


def solution(mesh):
    torus = Mesh(mesh.devices.reshape(4, 2, 4, 4, 2, 2), AXES)
    seq, rep = ("yh", "yl", "x"), ("zh", "zl", "core")
    placed = (
        P(rep, seq, None, None, None),
        P(rep, seq, None, None, None),
        P(rep, seq, None),
        P(),
        P(),
    )
    return jax.shard_map(
        shards,
        mesh=torus,
        in_specs=placed,
        out_specs=(P(rep, seq, None, None, None), P(rep, seq)),
        check_vma=False,
    )
```

time: 64.5 us -> 64.5 us (level)
  starting transfers between devices: 14.5 us -> 16 us
    all_to_all x1, starting transfers between devices: 12.6 us -> 14.1 us  [exchanged(): return lax.all_to_all(tiles, axes, 0, 0, tiled=True)]
    pallas_call x1, Pallas kernels: 8.29 us -> 7.36 us  [weight_tiles(): pl.pallas_call(weight_kernel, out_shape=(jax.ShapeDtypeStruct(TILES, BF16...]
    unnamed x2 -> x4, local copies, waits for them, and re-layouts: 1.58 us -> 1.59 us
  transfers between devices with their start and end apart: 2 -> 2, of which waited for: 2 -> 2; matrix products, arithmetic and copies ran while one was open for 0% -> 0% of each run, Pallas kernels for 8% -> 9%
where the time goes in v8:
time: 64.5 us; the launch traced here: 64.8 us
  blocking collectives  23.8 us (37%)
  starting transfers between devices  16 us (25%)
  Pallas kernels  14.7 us (23%)
  waiting for transfers between devices  8.08 us (13%)
  local copies, waits for them, and re-layouts  1.59 us (2%)
  between operations  0.7 us (1%)
    all_to_all x1, blocking collectives, exchanged(): return lax.all_to_all(tiles, axes, 0, 0, tiled=True)  23.8 us
    all_to_all x1, starting transfers between devices, exchanged(): return lax.all_to_all(tiles, axes, 0, 0, tiled=True)  14.1 us
    all_to_all x1, waiting for transfers between devices, exchanged(): return lax.all_to_all(tiles, axes, 0, 0, tiled=True)  7.93 us
    pallas_call x1, Pallas kernels, weight_tiles(): pl.pallas_call(weight_kernel, out_shape=(jax.ShapeDtypeStruct(TILES, BF16...  7.36 us
    pallas_call x1, Pallas kernels, history_grads(): pl.pallas_call(history_kernel, out_shape=jax.ShapeDtypeStruct(hist.shape,...  4.49 us
    ppermute x1, starting transfers between devices, shards(): other = lax.ppermute(send.reshape(256, 16, 128), 'core', [(0, 1), (1, 0)])  1.92 us
    unnamed x4, local copies, waits for them, and re-layouts  1.59 us
  transfers between devices with their start and end apart: 2, of which 2 were waited for; matrix products, arithmetic and copies ran while one was open for 0% of the time, Pallas kernels for 9%

profile of v8, /device:TPU:8, one launch (start us, length us, event | category | flops | bytes accessed | tf_op | source)
XLA Modules:
  0.0 64.8 jit_solution(7094100167031828160)
XLA Ops:
  0.6 0.0 copy-start.1
  0.6 7.4 %shard_map.68 = (bf16[4,2,2,4,4,16,128]{6,5,4,3,2,1,0:T(8,128)(2,1)}, bf16[512,2048]{1,0:T(8,128)(2,1)}) custom-call(s32[6]{0:T(128)} %bitcast.10, bf16[6,64,512]{2,1,0:T(8,128)(2,1)} %bitcast.13, bf16[6,64,512]{2,1,0:T(8,128)(2,1)} %bitcast.15, bf16[512,2048]{1,0:T(8,128)(2,1)} %win_hbm.3, bf16[512,512]{1,0:T(8,128)(2,1)} %wout_hbm.1), custom_call_target="tpu_custom_call" | custom-call | flops 1811939328 | bytes 8388608 | tf_op jit(solution)/shard_map/pallas_call | solution.py:376
  8.0 1.9 %collective-permute-start = (bf16[256,16,128]{2,1,0:T(8,128)(2,1)}, bf16[256,16,128]{2,1,0:T(8,128)(2,1)S(1)}, u32[]{:S(2)}, u32[]{:S(2)}) collective-permute-start(bf16[256,16,128]{2,1,0:T(8,128)(2,1)} %bitcast.18), channel_id=1, source_target_pairs={{0,1},{1,0},{2,3},{3,2},{4,5},{5,4},{6,7},{7,6},{8,9},{9,8},{10,11... | collective-permute-start | bytes 3145736 | tf_op jit(solution)/shard_map/ppermute | solution.py:488
  9.9 0.0 copy-done.1
  9.9 0.0 copy-start
  10.0 1.6 %copy-done = bf16[512,2048]{1,0:T(8,128)(2,1)S(1)} copy-done((bf16[512,2048]{1,0:T(8,128)(2,1)S(1)}, bf16[512,2048]{1,0:T(8,128)(2,1)}, u32[]{:S(2)}) %copy-start) | copy-done | bytes 2097176
  11.5 1.1 %shard_map.69 = bf16[4,2,2,4,4,16,128]{6,5,4,3,2,1,0:T(8,128)(2,1)S(1)} custom-call(s32[6]{0:T(128)S(1)} %bitcast.12, bf16[512,2048]{1,0:T(8,128)(2,1)S(1)} %copy-done), custom_call_target="tpu_custom_call" | custom-call | flops 536870912 | bytes 3145728 | tf_op jit(solution)/shard_map/pallas_call | solution.py:413
  12.6 0.1 collective-permute-done.other_ref
  12.8 0.3 shard_map.70
  13.1 23.8 %all_to_all.10.parts_ref = bf16[16,16,16,128]{3,2,1,0:T(8,128)(2,1)S(1)} all-to-all(bf16[16,16,16,128]{3,2,1,0:T(8,128)(2,1)S(1)} %bitcast.9), channel_id=1, replica_groups=mesh['yh'=4,'yl'=2,'x'=4,'zh'=4,'zl'=2,'core'=2] {'x','yl','zl'}, dimensions={0} | all-to-all | bytes 2097152 | tf_op jit(solution)/shard_map/all_to_all | solution.py:482
  36.9 0.8 %shard_map.71.after_ref = bf16[16,16,128]{2,1,0:T(8,128)(2,1)} custom-call(bf16[16,16,16,128]{3,2,1,0:T(8,128)(2,1)S(1)} %all_to_all.10.parts_ref), custom_call_target="tpu_custom_call" | custom-call | tf_op jit(solution)/shard_map/pallas_call | solution.py:462
  37.6 14.1 %all-to-all-start.1 = ((bf16[16,1,16,128]{3,2,1,0:T(8,128)(2,1)}), bf16[16,1,16,128]{3,2,1,0:T(8,128)(2,1)S(1)}, u32[]{:S(2)}, u32[]{:S(2)}) async-start(bf16[16,1,16,128]{3,2,1,0:T(8,128)(2,1)} %bitcast.7), calls=%async_computation.1 | async-start | bytes 131072 | tf_op jit(solution)/shard_map/all_to_all | solution.py:482
  51.7 4.5 %shard_map.72 = bf16[6,64,512]{2,1,0:T(8,128)(2,1)} custom-call(s32[6]{0:T(128)} %bitcast.11, bf16[6,64,512]{2,1,0:T(8,128)(2,1)} %bitcast.14, bf16[6,64,512]{2,1,0:T(8,128)(2,1)} %bitcast.16, bf16[512,2048]{1,0:T(8,128)(2,1)} %win_hbm.3, bf16[512,2048]{1,0:T(8,128)(2,1)} %get-tuple-element.4.both_ref.both_hbm, bf16[16,16,128]{2,1,0:T(8,128)(2,1)} %shard_map.71.after_ref), custom_call_target="tpu_custom_call" | custom-call | flops 805306368 | bytes 6291456 | tf_op jit(solution)/shard_map/pallas_call | solution.py:429
  56.2 7.9 %all-to-all-done.1.parts_ref = bf16[16,1,16,128]{3,2,1,0:T(8,128)(2,1)S(1)} async-done(((bf16[16,1,16,128]{3,2,1,0:T(8,128)(2,1)}), bf16[16,1,16,128]{3,2,1,0:T(8,128)(2,1)S(1)}, u32[]{:S(2)}, u32[]{:S(2)}) %all-to-all-start.1) | async-done | bytes 65568 | tf_op jit(solution)/shard_map/all_to_all | solution.py:482
  64.1 0.7 %shard_map.73 = f32[32,64]{1,0:T(8,128)} custom-call(bf16[16,1,16,128]{3,2,1,0:T(8,128)(2,1)S(1)} %all-to-all-done.1.parts_ref), custom_call_target="tpu_custom_call" | custom-call | tf_op jit(solution)/shard_map/pallas_call | solution.py:472
Async XLA Ops:
  0.6 9.3 %copy-start.1 = (s32[1,1,6]{2,1,0:T(1,128)S(1)}, s32[1,1,6]{2,1,0:T(1,128)}, u32[]{:S(2)}) copy-start(s32[1,1,6]{2,1,0:T(1,128)} %param.7) | copy-start | bytes 76
  8.0 4.8 %collective-permute-start = (bf16[256,16,128]{2,1,0:T(8,128)(2,1)}, bf16[256,16,128]{2,1,0:T(8,128)(2,1)S(1)}, u32[]{:S(2)}, u32[]{:S(2)}) collective-permute-start(bf16[256,16,128]{2,1,0:T(8,128)(2,1)} %bitcast.18), channel_id=1, source_target_pairs={{0,1},{1,0},{2,3},{3,2},{4,5},{5,4},{6,7},{7,6},{8,9},{9,8},{10,11... | collective-permute-start | bytes 3145736 | tf_op jit(solution)/shard_map/ppermute | solution.py:488
  9.9 1.6 %copy-start = (bf16[512,2048]{1,0:T(8,128)(2,1)S(1)}, bf16[512,2048]{1,0:T(8,128)(2,1)}, u32[]{:S(2)}) copy-start(bf16[512,2048]{1,0:T(8,128)(2,1)} %get-tuple-element.4.both_ref.both_hbm) | copy-start | bytes 6291460
  37.6 26.5 %all-to-all-start.1 = ((bf16[16,1,16,128]{3,2,1,0:T(8,128)(2,1)}), bf16[16,1,16,128]{3,2,1,0:T(8,128)(2,1)S(1)}, u32[]{:S(2)}, u32[]{:S(2)}) async-start(bf16[16,1,16,128]{3,2,1,0:T(8,128)(2,1)} %bitcast.7), calls=%async_computation.1 | async-start | bytes 131072 | tf_op jit(solution)/shard_map/all_to_all | solution.py:482
